TPU v7x, 32 devices: a whole 2x2x4 slice. The times are simulated.
32 devices in a mesh: dp: 4 (over x, core), seq: 8 (over z, y).
Axes of the slice: x: 2, y: 2, z: 4, core: 2. Of those that a mesh axis runs over, the one named last changes fastest.
Arguments:
- tokens: float32 [8, 1024, 1024], P('dp', 'seq'), may hold values from -6 to 6
- encoder: float32 [8, 512, 1024], P('dp'), may hold values from -6 to 6
- cotangent: float32 [8, 1024, 1024], P('dp', 'seq'), may hold values from -6 to 6
- adapter_pick: int32 [8], P('dp'), may hold values from 0 to 7, as said below
- segment_order: int32 [8, 8], P('dp'), may hold values from 0 to 7, each once within a row
- parents: int32 [8, 8], P('dp'), may hold values from -1 to 3, as said below
- norm_gains: float32 [3, 1024], replicated, may hold values from 0.5 to 1.5
- w_qkv: float32 [1024, 3072], P(None, 'seq'), may hold values from -0.1875 to 0.1875
- w_self_out: float32 [1024, 1024], P('seq'), may hold values from -1.5 to 1.5
- w_cross_q: float32 [1024, 1024], P(None, 'seq'), may hold values from -0.1875 to 0.1875
- w_cross_kv: float32 [1024, 2048], P(None, 'seq'), may hold values from -0.1875 to 0.1875
- w_cross_out: float32 [1024, 1024], P('seq'), may hold values from -1.5 to 1.5
- w_fc_in: float32 [1024, 8192], P(None, 'seq'), may hold values from -0.1875 to 0.1875
- w_fc_out: float32 [8192, 1024], P('seq'), may hold values from -0.0625 to 0.0625
- attn_down: bfloat16 [8, 8, 1024, 16], replicated, may hold values from -0.1875 to 0.1875
- attn_up: bfloat16 [8, 8, 16, 1024], replicated, may hold values from -0.375 to 0.375
- fc_in_down: bfloat16 [8, 1024, 16], replicated, may hold values from -0.1875 to 0.1875
- fc_in_up: bfloat16 [8, 16, 8192], replicated, may hold values from -0.375 to 0.375
- fc_out_down: bfloat16 [8, 8192, 16], replicated, may hold values from -0.0625 to 0.0625
- fc_out_up: bfloat16 [8, 16, 1024], replicated, may hold values from -0.375 to 0.375
Outputs:
- layer_out: float32 [8, 1024, 1024], P('dp', 'seq')
- grad_tokens: float32 [8, 1024, 1024], P('dp', 'seq')
- grad_encoder: float32 [8, 512, 1024], P('dp', 'seq')
- grad_attn_down: float32 [8, 8, 1024, 16], replicated
- grad_attn_up: float32 [8, 8, 16, 1024], replicated
- grad_fc_in_down: float32 [8, 1024, 16], replicated
- grad_fc_in_up: float32 [8, 16, 8192], replicated
- grad_fc_out_down: float32 [8, 8192, 16], replicated
- grad_fc_out_up: float32 [8, 16, 1024], replicated
Inputs may be any that keep to these rules, and one draw needn't show every extreme that they name: `parents`: logical segments of the first quarter of the 8 form the trunk, each the child of the one before, segment 0 the root with parent -1; the second quarter are branch segments, the first four (all, if fewer) children of the trunk's last segment and each later one the child of the branch segment four before it; the other half are leaves, each the child of a branch segment, the last leaf that of the last branch segment. `adapter_pick`: every adapter is chosen by at least one tree.
All inputs are finite; a program needn't handle non-finite values.
Results may differ from a plain program's by a relative error of at most 0.0003.
Values sent between devices are 32-bit elements; how exact they have to be, the bound alone decides.
A program may use at most 512 MiB of HBM per device.

v0:
```python
import math

import jax
import jax.numpy as jnp
from jax import lax
from jax.sharding import PartitionSpec as P

HEADS = 16
HD = 64


PRECISE = lax.Precision.HIGHEST
ADAPT_SCALE = 2.0
NORM_EPS = 1e-05
MASK_FILL = -1e30


def matmul(left_side, right_side):
    return jnp.dot(left_side, right_side, precision=PRECISE, preferred_element_type=jnp.float32)


def product(formula, first_operand, second_operand):
    return jnp.einsum(
        formula,
        first_operand,
        second_operand,
        precision=PRECISE,
        preferred_element_type=jnp.float32,
    )


def reach_table(segment_order, parents):
    segment_count = parents.shape[-1]
    column = lax.broadcasted_iota(jnp.int32, (segment_count, segment_count), 1)
    identity = (
        lax.broadcasted_iota(jnp.int32, (segment_count, segment_count), 0) == column
    ).astype(jnp.int32)
    parent_hot = (parents[..., :, None] == column).astype(jnp.int32)

    def extend(sweep_index, reach_rows):
        return jnp.minimum(identity + jnp.einsum("gab,gbc->gac", parent_hot, reach_rows), 1)

    initial = jnp.broadcast_to(identity, parent_hot.shape)
    reach_rows = lax.fori_loop(0, segment_count, extend, initial)
    order_hot = (segment_order[..., :, None] == column).astype(jnp.int32)
    return jnp.einsum("gsa,gab,gtb->gst", order_hot, reach_rows, order_hot)


def layer_norm(values, gain_row):
    center = values - jnp.mean(values, -1, keepdims=True)
    inverse = lax.rsqrt(jnp.mean(center * center, -1, keepdims=True) + NORM_EPS)
    normal = center * inverse
    return (normal * gain_row, normal, inverse)


def norm_back(normal, inverse, gain_row, grads):
    scaled = grads * gain_row
    mean_one = jnp.mean(scaled, -1, keepdims=True)
    mean_two = jnp.mean(scaled * normal, -1, keepdims=True)
    return inverse * (scaled - mean_one - normal * mean_two)


def gelu_back(pre_act, d_hidden):

    def activate(values):
        return jax.nn.gelu(values, approximate=True)

    return jax.vjp(activate, pre_act)[1](d_hidden)[0]


def cols_forward(inputs, shard):
    flat_rows = inputs.reshape(-1, inputs.shape[-1])
    result = matmul(flat_rows, lax.all_gather(shard, "seq", axis=1, tiled=True))
    return result.reshape(inputs.shape[:-1] + (result.shape[-1],))


def cols_back(grads, shard):
    flat_grads = grads.reshape(-1, grads.shape[-1])
    result = matmul(flat_grads, lax.all_gather(shard, "seq", axis=1, tiled=True).T)
    return result.reshape(grads.shape[:-1] + (shard.shape[0],))


def rows_forward(inputs, shard):
    flat_rows = inputs.reshape(-1, inputs.shape[-1])
    result = matmul(flat_rows, lax.all_gather(shard, "seq", axis=0, tiled=True))
    return result.reshape(inputs.shape[:-1] + (shard.shape[1],))


def rows_back(grads, shard):
    flat_grads = grads.reshape(-1, grads.shape[-1])
    result = matmul(flat_grads, lax.all_gather(shard, "seq", axis=0, tiled=True).T)
    return result.reshape(grads.shape[:-1] + (result.shape[-1],))


def adapter_apply(inputs, down_map, up_map):
    inner = product("gsd,gdr->gsr", inputs, down_map)
    return (ADAPT_SCALE * product("gsr,gro->gso", inner, up_map), inner)


def adapter_back(inputs, inner, down_map, up_map, grads):
    d_inner = ADAPT_SCALE * product("gso,gro->gsr", grads, up_map)
    grad_up = ADAPT_SCALE * product("gsr,gso->gro", inner, grads)
    grad_down = product("gsd,gsr->gdr", inputs, d_inner)
    return (product("gsr,gdr->gsd", d_inner, down_map), grad_down, grad_up)


def key_mask(my_reach, my_slot, query_index, first_key, key_count, seg_len):
    slot_count = my_reach.shape[1]
    key_index = first_key + lax.broadcasted_iota(jnp.int32, (1, key_count), 1)
    key_slot = key_index // seg_len
    slot_hot = (key_slot[0][:, None] == lax.broadcasted_iota(jnp.int32, (1, slot_count), 1)).astype(
        jnp.int32
    )
    key_allowed = jnp.einsum("gc,nc->gn", my_reach, slot_hot)
    causal_ok = (key_slot != my_slot) | (key_index <= query_index)
    allowed = (key_allowed[:, None, :] > 0) & causal_ok[None]
    return (allowed, jnp.any(key_allowed > 0))


def self_forward(queries, key_rows, value_rows, my_reach, my_slot):
    groups, seg_len, width = queries.shape
    query_heads = queries.reshape(groups, seg_len, HEADS, HD) * HD ** (-0.5)
    query_index = my_slot * seg_len + lax.broadcasted_iota(jnp.int32, (seg_len, 1), 0)
    start_state = (
        jnp.full((groups, HEADS, seg_len), MASK_FILL, jnp.float32),
        jnp.zeros((groups, HEADS, seg_len), jnp.float32),
        jnp.zeros((groups, HEADS, seg_len, HD), jnp.float32),
    )
    key_part = lax.all_gather(key_rows, "seq", axis=1, tiled=True)
    value_part = lax.all_gather(value_rows, "seq", axis=1, tiled=True)
    key_count = key_part.shape[1]
    allowed, any_allowed = key_mask(
        my_reach, my_slot, query_index, jnp.int32(0), key_count, seg_len
    )

    def attend(state):
        peak, mass, accum = state
        key_heads = key_part.reshape(groups, key_count, HEADS, HD)
        value_heads = value_part.reshape(groups, key_count, HEADS, HD)
        scores = product("gshd,gnhd->ghsn", query_heads, key_heads)
        masked = jnp.where(allowed[:, None], scores, MASK_FILL)
        new_peak = jnp.maximum(peak, jnp.max(masked, -1))
        probs = jnp.where(allowed[:, None], jnp.exp(masked - new_peak[..., None]), 0.0)
        mass = jnp.sum(probs, -1)
        accum = product("ghsn,gnhd->ghsd", probs, value_heads)
        return (new_peak, mass, accum)

    peak, mass, accum = lax.cond(any_allowed, attend, lambda state: state, start_state)
    context = (accum / mass[..., None]).transpose(0, 2, 1, 3).reshape(groups, seg_len, width)
    return (context, peak + jnp.log(mass))


def self_backward(queries, key_all, value_all, log_mass, delta, d_context, my_reach, my_slot):
    groups, seg_len, width = queries.shape
    scale = HD ** (-0.5)
    query_heads = queries.reshape(groups, seg_len, HEADS, HD) * scale
    out_heads = d_context.reshape(groups, seg_len, HEADS, HD)
    query_index = my_slot * seg_len + lax.broadcasted_iota(jnp.int32, (seg_len, 1), 0)
    total_keys = key_all.shape[1]
    block_keys = seg_len * math.gcd(total_keys // seg_len, max(1, 512 // seg_len))
    firsts = jnp.arange(total_keys // block_keys, dtype=jnp.int32) * block_keys

    def block_step(state, first_key):
        allowed, any_allowed = key_mask(
            my_reach, my_slot, query_index, first_key, block_keys, seg_len
        )

        def gradients(inner_state):
            key_heads = lax.dynamic_slice_in_dim(key_all, first_key, block_keys, 1).reshape(
                groups, block_keys, HEADS, HD
            )
            value_heads = lax.dynamic_slice_in_dim(value_all, first_key, block_keys, 1).reshape(
                groups, block_keys, HEADS, HD
            )
            scores = product("gshd,gnhd->ghsn", query_heads, key_heads)
            masked = jnp.where(allowed[:, None], scores, MASK_FILL)
            probs = jnp.where(allowed[:, None], jnp.exp(masked - log_mass[..., None]), 0.0)
            d_probs = product("gshd,gnhd->ghsn", out_heads, value_heads)
            d_scores = probs * (d_probs - delta[..., None])
            d_query = inner_state[0] + product("ghsn,gnhd->gshd", d_scores, key_heads)
            d_value_part = product("ghsn,gshd->gnhd", probs, out_heads)
            d_key_part = product("ghsn,gshd->gnhd", d_scores, query_heads)
            d_key_all = lax.dynamic_update_slice_in_dim(
                inner_state[1], d_key_part.reshape(groups, block_keys, width), first_key, 1
            )
            d_value_all = lax.dynamic_update_slice_in_dim(
                inner_state[2], d_value_part.reshape(groups, block_keys, width), first_key, 1
            )
            return (d_query, d_key_all, d_value_all)

        return (lax.cond(any_allowed, gradients, lambda inner_state: inner_state, state), None)

    zero_query = jnp.zeros((groups, seg_len, HEADS, HD), jnp.float32)
    initial = (zero_query, jnp.zeros_like(key_all), jnp.zeros_like(value_all))
    final_state, unused = lax.scan(block_step, initial, firsts)
    d_query = final_state[0].reshape(groups, seg_len, width) * scale
    return (d_query, final_state[1], final_state[2])


def cross_forward(queries, key_rows, value_rows):
    groups, seg_len, width = queries.shape
    enc_rows = key_rows.shape[1]
    query_heads = queries.reshape(groups, seg_len, HEADS, HD) * HD ** (-0.5)
    scores = product("gshd,gehd->ghse", query_heads, key_rows.reshape(groups, enc_rows, HEADS, HD))
    probs = jax.nn.softmax(scores, axis=-1)
    context = product("ghse,gehd->gshd", probs, value_rows.reshape(groups, enc_rows, HEADS, HD))
    return (context.reshape(groups, seg_len, width), probs)


def cross_backward(queries, key_rows, value_rows, probs, d_context):
    groups, seg_len, width = queries.shape
    enc_rows = key_rows.shape[1]
    scale = HD ** (-0.5)
    query_heads = queries.reshape(groups, seg_len, HEADS, HD) * scale
    key_heads = key_rows.reshape(groups, enc_rows, HEADS, HD)
    value_heads = value_rows.reshape(groups, enc_rows, HEADS, HD)
    out_heads = d_context.reshape(groups, seg_len, HEADS, HD)
    d_values = product("ghse,gshd->gehd", probs, out_heads)
    d_probs = product("gshd,gehd->ghse", out_heads, value_heads)
    d_scores = probs * (d_probs - jnp.sum(probs * d_probs, -1, keepdims=True))
    d_queries = product("ghse,gehd->gshd", d_scores, key_heads) * scale
    d_keys = product("ghse,gshd->gehd", d_scores, query_heads)
    return (
        d_queries.reshape(groups, seg_len, width),
        d_keys.reshape(groups, enc_rows, width),
        d_values.reshape(groups, enc_rows, width),
    )


def shards(
    tokens,
    encoder,
    cotangent,
    adapter_pick,
    segment_order,
    parents,
    norm_gains,
    w_qkv,
    w_self_out,
    w_cross_q,
    w_cross_kv,
    w_cross_out,
    w_fc_in,
    w_fc_out,
    attn_down,
    attn_up,
    fc_in_down,
    fc_in_up,
    fc_out_down,
    fc_out_up,
):
    groups, seg_len, width = tokens.shape
    enc_rows = encoder.shape[1]
    my_slot = lax.axis_index("seq")
    reach_rows = reach_table(segment_order, parents)
    my_reach = lax.dynamic_index_in_dim(reach_rows, my_slot, 1, keepdims=False)
    adapter_count = attn_down.shape[0]
    chosen = (
        adapter_pick[:, None] == lax.broadcasted_iota(jnp.int32, (1, adapter_count), 1)
    ).astype(jnp.float32)
    chosen_low = chosen.astype(jnp.bfloat16)

    def select(adapter_table):
        return jnp.einsum(
            "ga,a...->g...", chosen_low, adapter_table, preferred_element_type=jnp.float32
        )

    sel_down = select(attn_down)
    sel_up = select(attn_up)
    in_down = select(fc_in_down)
    in_up = select(fc_in_up)
    out_down = select(fc_out_down)
    out_up = select(fc_out_up)
    normed_one, normal_one, inverse_one = layer_norm(tokens, norm_gains[0])
    inner_qkv = product("gsd,gpdr->gspr", normed_one, sel_down[:, 0:3])
    stacked = cols_forward(normed_one, w_qkv) + ADAPT_SCALE * product(
        "gspr,gpro->gspo", inner_qkv, sel_up[:, 0:3]
    ).reshape(groups, seg_len, 3 * width)
    queries = stacked[..., :width]
    key_rows = stacked[..., width : 2 * width]
    value_rows = stacked[..., 2 * width :]
    context, log_mass = self_forward(queries, key_rows, value_rows, my_reach, my_slot)
    self_term, inner_self = adapter_apply(context, sel_down[:, 3], sel_up[:, 3])
    middle = tokens + rows_forward(context, w_self_out) + self_term
    normed_two, normal_two, inverse_two = layer_norm(middle, norm_gains[1])
    query_term, inner_cross_q = adapter_apply(normed_two, sel_down[:, 4], sel_up[:, 4])
    cross_queries = cols_forward(normed_two, w_cross_q) + query_term
    inner_memory = product("ged,gpdr->gepr", encoder, sel_down[:, 5:7])
    memory = cols_forward(encoder, w_cross_kv) + ADAPT_SCALE * product(
        "gepr,gpro->gepo", inner_memory, sel_up[:, 5:7]
    ).reshape(groups, enc_rows, 2 * width)
    cross_keys = memory[..., :width]
    cross_values = memory[..., width:]
    cross_context, cross_probs = cross_forward(cross_queries, cross_keys, cross_values)
    cross_term, inner_cross_out = adapter_apply(cross_context, sel_down[:, 7], sel_up[:, 7])
    after_cross = middle + rows_forward(cross_context, w_cross_out) + cross_term
    normed_three, normal_three, inverse_three = layer_norm(after_cross, norm_gains[2])
    inner_in = product("gsd,gdr->gsr", normed_three, in_down)
    pre_act = cols_forward(normed_three, w_fc_in) + ADAPT_SCALE * product(
        "gsr,grf->gsf", inner_in, in_up
    )
    hidden = jax.nn.gelu(pre_act, approximate=True)
    inner_out = product("gsf,gfr->gsr", hidden, out_down)
    mlp_out = rows_forward(hidden, w_fc_out) + ADAPT_SCALE * product(
        "gsr,grd->gsd", inner_out, out_up
    )
    layer_out = after_cross + mlp_out
    d_inner_out = ADAPT_SCALE * product("gsd,grd->gsr", cotangent, out_up)
    grad_out_up_tree = ADAPT_SCALE * product("gsr,gsd->grd", inner_out, cotangent)
    d_hidden = rows_back(cotangent, w_fc_out) + product("gsr,gfr->gsf", d_inner_out, out_down)
    grad_out_down_tree = product("gsf,gsr->gfr", hidden, d_inner_out)
    d_pre = gelu_back(pre_act, d_hidden)
    d_inner_in = ADAPT_SCALE * product("gsf,grf->gsr", d_pre, in_up)
    grad_in_up_tree = ADAPT_SCALE * product("gsr,gsf->grf", inner_in, d_pre)
    d_normed_three = cols_back(d_pre, w_fc_in) + product("gsr,gdr->gsd", d_inner_in, in_down)
    grad_in_down_tree = product("gsd,gsr->gdr", normed_three, d_inner_in)
    d_after = cotangent + norm_back(normal_three, inverse_three, norm_gains[2], d_normed_three)
    d_cross_ctx, grad_down_seven, grad_up_seven = adapter_back(
        cross_context, inner_cross_out, sel_down[:, 7], sel_up[:, 7], d_after
    )
    d_cross_ctx = d_cross_ctx + rows_back(d_after, w_cross_out)
    d_cross_q, d_cross_k, d_cross_v = cross_backward(
        cross_queries, cross_keys, cross_values, cross_probs, d_cross_ctx
    )
    d_normed_two, grad_down_four, grad_up_four = adapter_back(
        normed_two, inner_cross_q, sel_down[:, 4], sel_up[:, 4], d_cross_q
    )
    d_normed_two = d_normed_two + cols_back(d_cross_q, w_cross_q)
    d_middle = d_after + norm_back(normal_two, inverse_two, norm_gains[1], d_normed_two)
    d_memory = jnp.concatenate([d_cross_k, d_cross_v], axis=-1)
    d_memory_split = d_memory.reshape(groups, enc_rows, 2, width)
    d_inner_memory = ADAPT_SCALE * product("gepo,gpro->gepr", d_memory_split, sel_up[:, 5:7])
    grad_up_memory = ADAPT_SCALE * product("gepr,gepo->gpro", inner_memory, d_memory_split)
    grad_down_memory = product("ged,gepr->gpdr", encoder, d_inner_memory)
    d_encoder_local = cols_back(d_memory, w_cross_kv) + product(
        "gepr,gpdr->ged", d_inner_memory, sel_down[:, 5:7]
    )
    grad_encoder = lax.psum_scatter(d_encoder_local, "seq", scatter_dimension=1, tiled=True)
    d_context, grad_down_three, grad_up_three = adapter_back(
        context, inner_self, sel_down[:, 3], sel_up[:, 3], d_middle
    )
    d_context = d_context + rows_back(d_middle, w_self_out)
    delta = jnp.sum(
        d_context.reshape(groups, seg_len, HEADS, HD) * context.reshape(groups, seg_len, HEADS, HD),
        -1,
    ).transpose(0, 2, 1)
    key_all, value_all = (
        lax.all_gather(key_rows, "seq", axis=1, tiled=True),
        lax.all_gather(value_rows, "seq", axis=1, tiled=True),
    )
    d_queries, d_key_all, d_value_all = self_backward(
        queries, key_all, value_all, log_mass, delta, d_context, my_reach, my_slot
    )
    d_keys, d_values = (
        lax.psum_scatter(d_key_all, "seq", scatter_dimension=1, tiled=True),
        lax.psum_scatter(d_value_all, "seq", scatter_dimension=1, tiled=True),
    )
    d_stacked = jnp.concatenate([d_queries, d_keys, d_values], axis=-1)
    d_split = d_stacked.reshape(groups, seg_len, 3, width)
    d_inner_qkv = ADAPT_SCALE * product("gspo,gpro->gspr", d_split, sel_up[:, 0:3])
    grad_up_qkv = ADAPT_SCALE * product("gspr,gspo->gpro", inner_qkv, d_split)
    grad_down_qkv = product("gsd,gspr->gpdr", normed_one, d_inner_qkv)
    d_normed_one = cols_back(d_stacked, w_qkv) + product(
        "gspr,gpdr->gsd", d_inner_qkv, sel_down[:, 0:3]
    )
    grad_tokens = d_middle + norm_back(normal_one, inverse_one, norm_gains[0], d_normed_one)
    down_stack = jnp.concatenate(
        [
            grad_down_qkv,
            grad_down_three[:, None],
            grad_down_four[:, None],
            grad_down_memory,
            grad_down_seven[:, None],
        ],
        axis=1,
    )
    up_stack = jnp.concatenate(
        [
            grad_up_qkv,
            grad_up_three[:, None],
            grad_up_four[:, None],
            grad_up_memory,
            grad_up_seven[:, None],
        ],
        axis=1,
    )
    tree_parts = (
        down_stack,
        up_stack,
        grad_in_down_tree,
        grad_in_up_tree,
        grad_out_down_tree,
        grad_out_up_tree,
    )
    shapes = (
        attn_down.shape,
        attn_up.shape,
        fc_in_down.shape,
        fc_in_up.shape,
        fc_out_down.shape,
        fc_out_up.shape,
    )
    local_sums = tuple(
        (product("ga,gx->ax", chosen, part.reshape(groups, -1)).reshape(-1) for part in tree_parts)
    )
    owned = lax.psum_scatter(local_sums, ("dp", "seq"), scatter_dimension=0, tiled=True)
    full_sums = lax.all_gather(owned, ("dp", "seq"), axis=0, tiled=True)
    results = [summed.reshape(shape) for summed, shape in zip(full_sums, shapes)]
    return (
        layer_out,
        grad_tokens,
        grad_encoder,
        results[0],
        results[1],
        results[2],
        results[3],
        results[4],
        results[5],
    )


def solution(mesh):
    return jax.shard_map(
        shards,
        mesh=mesh,
        in_specs=(
            P("dp", "seq", None),
            P("dp", None, None),
            P("dp", "seq", None),
            P("dp"),
            P("dp", None),
            P("dp", None),
            P(),
            P(None, "seq"),
            P("seq", None),
            P(None, "seq"),
            P(None, "seq"),
            P("seq", None),
            P(None, "seq"),
            P("seq", None),
            P(),
            P(),
            P(),
            P(),
            P(),
            P(),
        ),
        out_specs=(
            P("dp", "seq", None),
            P("dp", "seq", None),
            P("dp", "seq", None),
            P(),
            P(),
            P(),
            P(),
            P(),
            P(),
        ),
        check_vma=False,
    )
```

profile of v0, /device:TPU:0, one launch (start us, length us, event | category | flops | bytes accessed | tf_op | source)
XLA Modules:
  0.0 3491.0 jit_solution(12437756087125868278)
XLA Ops:
  28.1 161.1 %all-gather.14.cloned.1.call-done = f32[1024,3072]{1,0:T(8,128)} async-done(((f32[1024,384]{1,0:T(8,128)}), f32[1024,3072]{1,0:T(8,128)}) %all-gather.14.cloned.1.call-update) | async-done | bytes 12582928 | tf_op jit(solution)/shard_map/all_gather | solution.py:73
  255.4 59.5 %all-gather.22.cloned.1.call-done = f32[1024,2048]{1,0:T(8,128)} async-done(((f32[1024,256]{1,0:T(8,128)}), f32[1024,2048]{1,0:T(8,128)}) %all-gather.22.cloned.1.call-update) | async-done | bytes 8388624 | tf_op jit(solution)/shard_map/all_gather | solution.py:73
  314.9 30.7 fusion.85
  361.0 79.2 %all-gather.16.cloned.1.call-done = f32[2,1024,1024]{2,1,0:T(8,128)} async-done(((f32[2,128,1024]{2,1,0:T(8,128)}), f32[2,1024,1024]{2,1,0:T(8,128)}) %all-gather.16.cloned.1.call-update) | async-done | bytes 8388624 | tf_op jit(solution)/shard_map/all_gather | solution.py:129
  440.2 125.7 %all-gather.18.cloned.1.call-done = f32[2,1024,1024]{2,1,0:T(8,128)} async-done(((f32[2,128,1024]{2,1,0:T(8,128)}), f32[2,1024,1024]{2,1,0:T(8,128)}) %all-gather.18.cloned.1.call-update) | async-done | bytes 8388624 | tf_op jit(solution)/shard_map/all_gather | solution.py:130
  566.0 71.2 %conditional.2 = (f32[2,16,128]{2,1,0:T(8,128)}, f32[2,16,128]{2,1,0:T(8,128)}, f32[2,16,128,64]{2,3,1,0:T(8,128)S(1)}, f32[2,16,128]{2,1,0:T(8,128)}) conditional(s32[]{:T(128)} %convert_element_type.28, () %tuple.44, (pred[2,1024]{1,0:T(4,128)(4,1)S(1)}, s32[1,1024]{1,0:T(1,128)S(1)}, s32[]{:T(128)}, s32[]{:T(128)}, s32[1,128,1024]{2,1,0:T(8,128)S(1)}, ...), branch_computations={%region_5.6_spmd, %region_6.9_spmd} | conditional | flops 6480729088 | bytes 171845184 | solution.py:148
  610.4 26.4 fusion.10
  654.7 60.1 %all-gather.24.cloned.1.call-done = f32[1024,1024]{1,0:T(8,128)} async-done(((f32[1024,128]{1,0:T(8,128)}), f32[1024,1024]{1,0:T(8,128)}) %all-gather.24.cloned.1.call-update) | async-done | bytes 4194320 | tf_op jit(solution)/shard_map/all_gather | solution.py:73
  807.2 618.9 %all-gather.30.cloned.1.call-done = f32[8192,1024]{1,0:T(8,128)} async-done(((f32[1024,1024]{1,0:T(8,128)}), f32[8192,1024]{1,0:T(8,128)}) %all-gather.30.cloned.1.call-update) | async-done | bytes 33554448 | tf_op jit(solution)/shard_map/all_gather | solution.py:85
  1426.1 33.6 fusion.35
  1459.8 605.6 %all-gather.28.cloned.1.call-done = f32[1024,8192]{1,0:T(8,128)} async-done(((f32[1024,1024]{1,0:T(8,128)}), f32[1024,8192]{1,0:T(8,128)}) %all-gather.28.cloned.1.call-update) | async-done | bytes 33554448 | tf_op jit(solution)/shard_map/all_gather | solution.py:73
  2065.4 33.7 fusion.47
  2124.9 33.3 fusion.39
  2225.1 243.7 %while.29 = (s32[]{:T(128)}, f32[2,128,16,64]{1,3,2,0:T(8,128)S(1)}, f32[2,1024,1024]{1,2,0:T(8,128)}, f32[2,1024,1024]{1,2,0:T(8,128)}, s32[2]{0:T(128)S(1)}, /...) while((s32[]{:T(128)}, ...), condition=%wide.region_25.26_spmd.clone, body=%wide.region_21.25_spmd.clone.sunk | while | flops 8070404608 | bytes 145294864 | solution.py:195
  2228.4 109.4 %conditional.5 = ((f32[2,128,16,64]{1,3,2,0:T(8,128)S(1)}, f32[2,1024,1024]{1,2,0:T(8,128)}, f32[2,1024,1024]{1,2,0:T(8,128)})) conditional(s32[]{:T(128)} %convert_element_type.71, (f32[2,128,16,64]{1,3,2,0:T(8,128)S(1)}, f32[2,1024,1024]{1,2,0:T(8,128)}, f32[2,1024,1024]{1,2,0:T(8,128)}) %tuple.112, (s32[]{:T(128)}, ...), branch_computations={%region_23.23_spmd, %region_24.24_spmd.clone} | conditional | flops 8070373888 | bytes 145286784 | solution.py:191
  2349.4 107.0 %conditional.5 = ((f32[2,128,16,64]{1,3,2,0:T(8,128)S(1)}, f32[2,1024,1024]{1,2,0:T(8,128)}, f32[2,1024,1024]{1,2,0:T(8,128)})) conditional(s32[]{:T(128)} %convert_element_type.71, (f32[2,128,16,64]{1,3,2,0:T(8,128)S(1)}, f32[2,1024,1024]{1,2,0:T(8,128)}, f32[2,1024,1024]{1,2,0:T(8,128)}) %tuple.112, (s32[]{:T(128)}, ...), branch_computations={%region_23.23_spmd, %region_24.24_spmd.clone} | conditional | flops 8070373888 | bytes 145286784 | solution.py:191
  2589.0 37.7 %reduce-scatter.4.cloned.1.call-done = f32[2,128,1024]{2,1,0:T(8,128)} async-done(((f32[2,1024,1024]{2,1,0:T(8,128)}), f32[2,128,1024]{2,1,0:T(8,128)}) %reduce-scatter.4.cloned.1.call-update) | async-done | bytes 1048592 | tf_op jit(solution)/shard_map/reduce_scatter | solution.py:355
  2626.7 151.9 %reduce-scatter.6.cloned.1.call-done = f32[2,128,1024]{2,1,0:T(8,128)} async-done(((f32[2,1024,1024]{2,1,0:T(8,128)}), f32[2,128,1024]{2,1,0:T(8,128)}) %reduce-scatter.6.cloned.1.call-update) | async-done | bytes 1048592 | tf_op jit(solution)/shard_map/reduce_scatter | solution.py:356
  2839.8 294.0 %all-reduce.9.cloned.1.call-done = (f32[1048576]{0:T(1024)}, f32[1048576]{0:T(1024)}, f32[131072]{0:T(1024)}, f32[1048576]{0:T(1024)}, f32[1048576]{0:T(1024)}, /*index=5*/f32[131072]{0:T(1024)}) async-done(((f32[1048576]{0:T(1024)}, f32[1048576]{0:T(1024)}, f32[131072]{0:T(1024)}, f32[1048576]{0:T(1024)}, f32[1048576]{0:T(1024)}, /*index=5*/f32[131072]{0:T(1024)}), (f32[1048576]{0:T(1024)}, ...) | async-done | bytes 17825808
  3151.4 30.0 fusion.57
  3186.6 34.4 fusion.37
  3240.4 70.5 %all_gather.65 = f32[131072]{0:T(1024)S(1)} all-gather(f32[4096]{0:T(1024)S(1)} %dynamic-slice.2), channel_id=1, replica_groups=mesh['dp'=4,'seq'=8] {'dp','seq'}, dimensions={0}, use_global_device_ids=true | all-gather | bytes 540672 | tf_op jit(solution)/shard_map/all_gather | solution.py:407
  3318.1 68.1 %all_gather.68 = f32[131072]{0:T(1024)S(1)} all-gather(f32[4096]{0:T(1024)S(1)} %dynamic-slice.5), channel_id=1, replica_groups=mesh['dp'=4,'seq'=8] {'dp','seq'}, dimensions={0}, use_global_device_ids=true | all-gather | bytes 540672 | tf_op jit(solution)/shard_map/all_gather | solution.py:407
  3406.8 20.8 copy.255
  (537 shorter events, 872.0 us)
Async XLA Ops:
  7.2 182.0 %all-gather.14.cloned.1.call-start = ((), (), s32[]{:S(2)}) async-start(), calls=%async_computation.3 | async-start | bytes 14155776 | tf_op jit(solution)/shard_map/all_gather | solution.py:73
  7.9 306.9 %all-gather.22.cloned.1.call-start = ((), (), s32[]{:S(2)}) async-start(), calls=%async_computation.7 | async-start | bytes 9437184 | tf_op jit(solution)/shard_map/all_gather | solution.py:73
  8.7 431.5 %all-gather.16.cloned.1.call-start = ((), (), s32[]{:S(2)}) async-start(), calls=%async_computation.4 | async-start | bytes 9437184 | tf_op jit(solution)/shard_map/all_gather | solution.py:129
  16.2 2142.1 %copy-start.70 = (f32[1,1024]{1,0:T(1,128)}, f32[1,1024]{1,0:T(1,128)S(1)}, u32[]{:S(2)}) copy-start(f32[1,1024]{1,0:T(1,128)S(1)} %get-tuple-element.671) | copy-start | bytes 12292
  16.2 2182.3 %copy-start.98 = (f32[1,1024]{1,0:T(1,128)}, f32[1,1024]{1,0:T(1,128)S(1)}, u32[]{:S(2)}) copy-start(f32[1,1024]{1,0:T(1,128)S(1)} %get-tuple-element.673) | copy-start | bytes 12292
  205.0 361.0 %all-gather.18.cloned.1.call-start = ((), (), s32[]{:S(2)}) async-start(), calls=%async_computation.5 | async-start | bytes 9437184 | tf_op jit(solution)/shard_map/all_gather | solution.py:130
  205.6 439.3 %all-gather.20.cloned.1.call-start = ((), (), s32[]{:S(2)}) async-start(), calls=%async_computation.6 | async-start | bytes 4718592 | tf_op jit(solution)/shard_map/all_gather | solution.py:85
  206.1 508.7 %all-gather.24.cloned.1.call-start = ((), (), s32[]{:S(2)}) async-start(), calls=%async_computation.8 | async-start | bytes 4718592 | tf_op jit(solution)/shard_map/all_gather | solution.py:73
  206.7 581.8 %all-gather.26.cloned.1.call-start = ((), (), s32[]{:S(2)}) async-start(), calls=%async_computation.9 | async-start | bytes 4718592 | tf_op jit(solution)/shard_map/all_gather | solution.py:85
  207.5 1218.6 %all-gather.30.cloned.1.call-start = ((), (), s32[]{:S(2)}) async-start(), calls=%async_computation.11 | async-start | bytes 37748736 | tf_op jit(solution)/shard_map/all_gather | solution.py:85
  208.2 1857.2 %all-gather.28.cloned.1.call-start = ((), (), s32[]{:S(2)}) async-start(), calls=%async_computation.10 | async-start | bytes 37748736 | tf_op jit(solution)/shard_map/all_gather | solution.py:73
  209.0 2417.7 %reduce-scatter.4.cloned.1.call-start = ((), (), s32[]{:S(2)}) async-start(), calls=%async_computation.12 | async-start | bytes 9437184 | tf_op jit(solution)/shard_map/reduce_scatter | solution.py:355
  795.1 1364.6 %copy-start.4 = (f32[2,128,1024]{2,1,0:T(8,128)}, f32[2,128,1024]{2,1,0:T(8,128)S(1)}, u32[]{:S(2)}) copy-start(f32[2,128,1024]{2,1,0:T(8,128)S(1)} %get-tuple-element.681) | copy-start | bytes 3145732
  795.1 1364.6 %copy-start.77 = (f32[2,128]{1,0:T(2,128)}, f32[2,128]{1,0:T(2,128)S(1)}, u32[]{:S(2)}) copy-start(f32[2,128]{1,0:T(2,128)S(1)} %broadcast_multiply_fusion.8) | copy-start | bytes 3076
  795.4 1364.4 %copy-start.79 = (f32[2,128]{1,0:T(2,128)}, f32[2,128]{1,0:T(2,128)S(1)}, u32[]{:S(2)}) copy-start(f32[2,128]{1,0:T(2,128)S(1)} %add_rsqrt_fusion) | copy-start | bytes 3076
  2477.5 301.1 %reduce-scatter.6.cloned.1.call-start = ((), (), s32[]{:S(2)}) async-start(), calls=%async_computation.13 | async-start | bytes 9437184 | tf_op jit(solution)/shard_map/reduce_scatter | solution.py:356
  2486.4 647.4 %all-reduce.9.cloned.1.call-start = ((), (), s32[]{:S(2)}) async-start(), calls=%async_computation.19 | async-start | bytes 35651584
  2589.0 205.5 %copy-start.18 = (f32[2,128,1024]{2,1,0:T(8,128)S(1)}, f32[2,128,1024]{2,1,0:T(8,128)}, u32[]{:S(2)}) copy-start(f32[2,128,1024]{2,1,0:T(8,128)} %copy-done.17) | copy-start | bytes 3145732
  2589.0 205.5 %copy-start.84 = (f32[2,128,16]{1,2,0:T(8,128)S(1)}, f32[2,128,16]{1,2,0:T(8,128)}, u32[]{:S(2)}) copy-start(f32[2,128,16]{1,2,0:T(8,128)} %copy-done.83) | copy-start | bytes 49156
  2839.7 547.3 %all-gather.32.cloned.1.call-start = ((), (), s32[]{:S(2)}) async-start(), calls=%async_computation.15 | async-start | bytes 4325376 | tf_op jit(solution)/shard_map/all_gather | solution.py:407
  3135.4 292.1 %all-gather.38.cloned.1.call-start = ((), (), s32[]{:S(2)}) async-start(), calls=%async_computation.18 | async-start | bytes 4325376 | tf_op jit(solution)/shard_map/all_gather | solution.py:407
  3137.1 329.6 %all-gather.34.cloned.1.call-start = ((), (), s32[]{:S(2)}) async-start(), calls=%async_computation.16 | async-start | bytes 4325376 | tf_op jit(solution)/shard_map/all_gather | solution.py:407
  3138.7 332.9 %all-gather.36.cloned.1.call-start = ((), (), s32[]{:S(2)}) async-start(), calls=%async_computation.17 | async-start | bytes 4325376 | tf_op jit(solution)/shard_map/all_gather | solution.py:407
  3140.4 343.6 %reduce-scatter.8.cloned.1.call-start = ((), (), s32[]{:S(2)}) async-start(), calls=%async_computation.14 | async-start | bytes 4718592 | tf_op jit(solution)/shard_map/reduce_scatter | solution.py:338
  (126 other events, 3000.5 us)
Sparse Core Ops, SparseCore 0:
  10.3 178.8 all-gather.13
  191.2 123.6 all-gather.21
  317.1 123.0 all-gather.15
  442.8 123.0 all-gather.17
  567.9 71.6 all-gather.19
  641.5 73.2 all-gather.23
  716.9 71.5 all-gather.25
  790.1 635.9 all-gather.29
  1427.7 637.6 all-gather.27
  2477.7 148.9 reduce-scatter.3
  2630.8 147.8 reduce-scatter.5
  2839.8 293.9 all-reduce.8
  3137.5 61.8 all-gather.31
  3202.3 61.7 all-gather.37
  3267.0 62.1 all-gather.33
  3332.1 61.1 all-gather.35
  3397.3 86.5 reduce-scatter.7
where the time goes:
time: 3500 us; the launch traced here: 3490 us
  waiting for transfers between devices  2220 us (63%)
  matrix products  684 us (20%)
  local copies, waits for them, and re-layouts  372 us (11%)
  blocking collectives  139 us (4%)
    all_gather x4, waiting for transfers between devices, cols_forward(): result = matmul(flat_rows, lax.all_gather(shard, 'seq', axis=1, tiled=True))  886 us
    all_gather x3, waiting for transfers between devices, rows_forward(): result = matmul(flat_rows, lax.all_gather(shard, 'seq', axis=0, tiled=True))  633 us
    dot_general x65, matrix products, product(): jnp.einsum(formula, first_operand, second_operand, precision=PRECISE, pre...  399 us
    unnamed x18, waiting for transfers between devices  299 us
    dot_general x14, matrix products, matmul(): jnp.dot(left_side, right_side, precision=PRECISE, preferred_element_type=...  261 us
    reduce_scatter x1, waiting for transfers between devices, shards(): lax.psum_scatter(d_value_all, 'seq', scatter_dimension=1, tiled=True)  152 us
    all_gather x2, blocking collectives, shards(): full_sums = lax.all_gather(owned, ('dp', 'seq'), axis=0, tiled=True)  139 us
    all_gather x1, waiting for transfers between devices, self_forward(): value_part = lax.all_gather(value_rows, 'seq', axis=1, tiled=True)  126 us
  transfers between devices with their start and end apart: 17, of which 12 were waited for; matrix products, arithmetic and copies ran while one was open for 18% of the time, Pallas kernels for 0%

commit v1 on v0

--- a/solution.py
+++ b/solution.py
@@ -1,8 +1,11 @@
+import functools
 import math
 
 import jax
 import jax.numpy as jnp
 from jax import lax
+from jax.experimental import pallas as pl
+from jax.experimental.pallas import tpu as pltpu
 from jax.sharding import PartitionSpec as P
 
 HEADS = 16
@@ -419,42 +422,1331 @@
     )
 
 
+ROWS = ("z", "y")
+COPIES = ("x", "c")
+EVERY = ROWS + COPIES
+F32 = jnp.float32
+BF16 = jnp.bfloat16
+MIB = 1 << 20
+SWAP = [(0, 1), (1, 0)]
+NN = (((1,), (0,)), ((), ()))
+NT = (((1,), (1,)), ((), ()))
+TN = (((0,), (0,)), ((), ()))
+
+
+def split(values):
+    high = values.astype(BF16)
+    return high, (values - high.astype(F32)).astype(BF16)
+
+
+def dot(left, right, dims=NN):
+    return lax.dot_general(left, right, dims, preferred_element_type=F32)
+
+
+def dot3(left, right, dims=NN):
+    (left_high, left_low), (right_high, right_low) = left, right
+    return (
+        dot(left_high, right_high, dims)
+        + dot(left_high, right_low, dims)
+        + dot(left_low, right_high, dims)
+    )
+
+
+def dot2(left, right, dims=NN):
+    return dot(left[0], right, dims) + dot(left[1], right, dims)
+
+
+def adapted(rows, down, up):
+    inner = dot2(rows, down, NT)
+    return dot2(split(ADAPT_SCALE * inner), up), inner
+
+
+def adapted_back(rows, grads, down, up):
+    inner = split(ADAPT_SCALE * dot2(rows, down, NT))
+    d_inner = split(ADAPT_SCALE * dot2(grads, up, NT))
+    return dot2(d_inner, down), dot3(d_inner, rows, TN), dot3(inner, grads, TN)
+
+
+def both(parts, where):
+    return parts[0][where], parts[1][where]
+
+
+def vmem(limit):
+    return pltpu.CompilerParams(vmem_limit_bytes=limit * MIB)
+
+
+def shaped(*shape):
+    return jax.ShapeDtypeStruct(shape, F32)
+
+
+def whole_spec(shape):
+    return pl.BlockSpec(shape, lambda *_: (0,) * len(shape))
+
+
+def heads_kernel(
+    tokens_ref,
+    gains_ref,
+    weight_ref,
+    down_ref,
+    up_ref,
+    normed_ref,
+    inner_ref,
+    qkv_ref,
+    rows_ref,
+    w_high,
+    w_low,
+    out_sem,
+    up_sem,
+    down_sem,
+    across_sem,
+    here_sem,
+):
+    z, y = lax.axis_index("z"), lax.axis_index("y")
+    last = lax.axis_size("z") - 1
+    trees, seg_len, width = tokens_ref.shape
+    lanes = weight_ref.shape[2]
+    rank = up_ref.shape[2]
+
+    def place(level, side):
+        return level * 2 + side
+
+    def move(slot, sems, index, target):
+        return pltpu.make_async_remote_copy(
+            src_ref=rows_ref.at[slot],
+            dst_ref=rows_ref.at[slot],
+            send_sem=sems.at[index],
+            recv_sem=here_sem.at[slot],
+            device_id=target,
+            device_id_type=pl.DeviceIdType.MESH,
+        )
+
+    def upward(hop):
+        return move(place(z - hop, y), up_sem, hop, {"z": z + 1})
+
+    def downward(hop):
+        return move(place(z + hop, y), down_sem, hop, {"z": z - 1})
+
+    def across(level, index):
+        return move(place(level, y), across_sem, index, {"y": 1 - y})
+
+    def arrived(slot):
+        move(slot, across_sem, 0, {"y": 1 - y}).wait_recv()
+
+    barrier = pltpu.get_barrier_semaphore()
+    pl.semaphore_signal(barrier, 1, device_id={"y": 1 - y}, device_id_type=pl.DeviceIdType.MESH)
+
+    @pl.when(z > 0)
+    def _():
+        pl.semaphore_signal(
+            barrier, 1, device_id={"z": z - 1}, device_id_type=pl.DeviceIdType.MESH
+        )
+
+    @pl.when(z < last)
+    def _():
+        pl.semaphore_signal(
+            barrier, 1, device_id={"z": z + 1}, device_id_type=pl.DeviceIdType.MESH
+        )
+
+    own = place(z, y)
+    for tree in range(trees):
+        normed = layer_norm(tokens_ref[tree], gains_ref[0:1])[0]
+        rows_ref[own, tree * seg_len : (tree + 1) * seg_len] = normed
+    pl.semaphore_wait(
+        barrier, 1 + (z > 0).astype(jnp.int32) + (z < last).astype(jnp.int32)
+    )
+
+    @pl.when(z < last)
+    def _():
+        upward(0).start()
+
+    @pl.when(z > 0)
+    def _():
+        downward(0).start()
+
+    across(z, 0).start()
+    for kind in range(3):
+        high, low = split(weight_ref[kind])
+        w_high[:, kind * lanes : (kind + 1) * lanes] = high
+        w_low[:, kind * lanes : (kind + 1) * lanes] = low
+
+    def keep(slot):
+        return pltpu.make_async_copy(rows_ref.at[slot], normed_ref.at[slot], out_sem.at[slot])
+
+    def work(slot):
+        keep(slot).start()
+        parts = split(rows_ref[slot])
+        product = dot3(parts, (w_high[...], w_low[...]))
+        for tree in range(trees):
+            rows = slice(tree * seg_len, (tree + 1) * seg_len)
+            inner = dot2(both(parts, rows), down_ref[tree], NT)
+            inner_ref[slot, tree] = inner
+            inner_parts = split(ADAPT_SCALE * inner)
+            for kind in range(3):
+                term = dot2(
+                    both(inner_parts, (slice(None), slice(kind * rank, (kind + 1) * rank))),
+                    up_ref[tree, kind],
+                )
+                qkv_ref[slot, kind, tree] = (
+                    product[rows, kind * lanes : (kind + 1) * lanes] + term
+                )
+
+    work(own)
+    for hop in range(1, last + 1):
+
+        @pl.when(z - hop >= 0)
+        def _(hop=hop):
+            arrived(place(z - hop, y))
+
+            @pl.when(z < last)
+            def _():
+                upward(hop).start()
+
+            across(z - hop, hop).start()
+
+        @pl.when(z + hop <= last)
+        def _(hop=hop):
+            arrived(place(z + hop, y))
+
+            @pl.when(z > 0)
+            def _():
+                downward(hop).start()
+
+            across(z + hop, last + hop).start()
+
+        for step in (-1, 1):
+            level = z + step * hop
+            before = level - step
+
+            @pl.when(jnp.logical_and(level >= 0, level <= last))
+            def _(level=level):
+                work(place(level, y))
+
+            if hop == 1 and step == 1:
+                continue
+
+            @pl.when(jnp.logical_and(before >= 0, before <= last))
+            def _(before=before):
+                arrived(place(before, 1 - y))
+                work(place(before, 1 - y))
+
+    for level in (z - last, z + last):
+
+        @pl.when(jnp.logical_and(level >= 0, level <= last))
+        def _(level=level):
+            arrived(place(level, 1 - y))
+            work(place(level, 1 - y))
+
+    across(z, 0).wait_send()
+    for hop in range(0, last + 1):
+
+        @pl.when(jnp.logical_and(z - hop >= 0, z < last))
+        def _(hop=hop):
+            upward(hop).wait_send()
+
+        @pl.when(jnp.logical_and(z + hop <= last, z > 0))
+        def _(hop=hop):
+            downward(hop).wait_send()
+
+        if hop:
+
+            @pl.when(z - hop >= 0)
+            def _(hop=hop):
+                across(z - hop, hop).wait_send()
+
+            @pl.when(z + hop <= last)
+            def _(hop=hop):
+                across(z + hop, last + hop).wait_send()
+
+    for slot in range(normed_ref.shape[0]):
+        keep(slot).wait()
+
+
+def heads_call(tokens, gains, weight, down, up):
+    trees, seg_len, width = tokens.shape
+    slots = lax.axis_size(ROWS)
+    levels = lax.axis_size("z")
+    lanes = weight.shape[2]
+    inner = down.shape[1]
+    dma = pltpu.SemaphoreType.DMA
+    here = pl.BlockSpec(memory_space=pltpu.VMEM)
+    return pl.pallas_call(
+        heads_kernel,
+        out_shape=[
+            shaped(slots, trees * seg_len, width),
+            shaped(slots, trees, seg_len, inner),
+            shaped(slots, 3, trees, seg_len, lanes),
+        ],
+        in_specs=[here] * 5,
+        out_specs=[pl.BlockSpec(memory_space=pl.ANY), here, here],
+        scratch_shapes=[
+            pltpu.VMEM((slots, trees * seg_len, width), F32),
+            pltpu.VMEM((width, 3 * lanes), BF16),
+            pltpu.VMEM((width, 3 * lanes), BF16),
+            dma((slots,)),
+            dma((levels,)),
+            dma((levels,)),
+            dma((2 * levels - 1,)),
+            dma((slots,)),
+        ],
+        compiler_params=pltpu.CompilerParams(
+            vmem_limit_bytes=48 * MIB, collective_id=0, has_side_effects=True
+        ),
+    )(tokens, gains, weight, down, up)
+
+
+def ancestor_slots(order_ref, parents_ref, slot_of, tree, slot, depth):
+    segment = order_ref[tree, slot]
+    chain = [(slot, None)]
+    there = None
+    for _ in range(depth - 1):
+        parent = parents_ref[tree, segment]
+        there = parent >= 0 if there is None else jnp.logical_and(there, parent >= 0)
+        segment = jnp.maximum(parent, 0)
+        chain.append((slot_of[segment], there))
+    return chain
+
+
+def fill_slot_of(order_ref, slot_of, tree, slots):
+    for slot in range(slots):
+        slot_of[order_ref[tree, slot]] = slot
+
+
+def chain_mask(chain, seg_len):
+    row = lax.broadcasted_iota(jnp.int32, (seg_len, seg_len), 0)
+    column = lax.broadcasted_iota(jnp.int32, (seg_len, seg_len), 1)
+    masks = [(column <= row).astype(jnp.int32)]
+    for _, there in chain[1:]:
+        masks.append(jnp.full((seg_len, seg_len), there.astype(jnp.int32)))
+    return jnp.concatenate(masks, axis=1) > 0
+
+
+def attend(queries, keys, values, mask):
+    scores = dot3(split(queries), split(keys), NT)
+    if mask is not None:
+        scores = jnp.where(mask, scores, MASK_FILL)
+    weights = jnp.exp(scores - jnp.max(scores, -1, keepdims=True))
+    mass = jnp.sum(weights, -1, keepdims=True)
+    return dot3(split(weights), split(values)) / mass
+
+
+def attend_back(queries, keys, values, d_context, mask):
+    query_parts, key_parts = split(queries), split(keys)
+    value_parts, out_parts = split(values), split(d_context)
+    scores = dot3(query_parts, key_parts, NT)
+    if mask is not None:
+        scores = jnp.where(mask, scores, MASK_FILL)
+    weights = jnp.exp(scores - jnp.max(scores, -1, keepdims=True))
+    weights = weights / jnp.sum(weights, -1, keepdims=True)
+    d_weights = dot3(out_parts, value_parts, NT)
+    shared = jnp.sum(weights * d_weights, -1, keepdims=True)
+    score_parts = split(weights * (d_weights - shared))
+    return (
+        dot3(score_parts, key_parts) * HD ** (-0.5),
+        dot3(score_parts, query_parts, TN),
+        dot3(split(weights), out_parts, TN),
+    )
+
+
+def by_head(formula, *arrays, mask=None):
+    results = []
+    for head in range(arrays[0].shape[1] // HD):
+        lanes = slice(head * HD, (head + 1) * HD)
+        results.append(formula(*[array[:, lanes] for array in arrays], mask))
+    if isinstance(results[0], tuple):
+        return [jnp.concatenate(parts, axis=1) for parts in zip(*results)]
+    return jnp.concatenate(results, axis=1)
+
+
+def self_forward_kernel(depth, order_ref, parents_ref, qkv_ref, context_ref, slot_of):
+    tree = pl.program_id(0)
+    slots, seg_len = qkv_ref.shape[0], qkv_ref.shape[3]
+    fill_slot_of(order_ref, slot_of, tree, slots)
+
+    def one_slot(slot, carry):
+        chain = ancestor_slots(order_ref, parents_ref, slot_of, tree, slot, depth)
+        keys = jnp.concatenate([qkv_ref[where, 1, 0] for where, _ in chain], axis=0)
+        values = jnp.concatenate([qkv_ref[where, 2, 0] for where, _ in chain], axis=0)
+        context_ref[slot, 0] = by_head(
+            attend,
+            qkv_ref[slot, 0, 0] * HD ** (-0.5),
+            keys,
+            values,
+            mask=chain_mask(chain, seg_len),
+        )
+        return carry
+
+    lax.fori_loop(0, slots, one_slot, 0)
+
+
+def self_backward_kernel(
+    depth,
+    order_ref,
+    parents_ref,
+    qkv_ref,
+    d_context_ref,
+    normed_ref,
+    inner_ref,
+    up_ref,
+    d_qkv_ref,
+    g_down_ref,
+    g_up_ref,
+    slot_of,
+):
+    tree = pl.program_id(0)
+    slots, seg_len, pair = qkv_ref.shape[0], qkv_ref.shape[3], qkv_ref.shape[4]
+    rank = up_ref.shape[2]
+    fill_slot_of(order_ref, slot_of, tree, slots)
+    d_qkv_ref[...] = jnp.zeros_like(d_qkv_ref)
+
+    def one_slot(slot, carry):
+        chain = ancestor_slots(order_ref, parents_ref, slot_of, tree, slot, depth)
+        keys = jnp.concatenate([qkv_ref[where, 1, 0] for where, _ in chain], axis=0)
+        values = jnp.concatenate([qkv_ref[where, 2, 0] for where, _ in chain], axis=0)
+        d_queries, d_keys, d_values = by_head(
+            attend_back,
+            qkv_ref[slot, 0, 0] * HD ** (-0.5),
+            keys,
+            values,
+            d_context_ref[slot, 0],
+            mask=chain_mask(chain, seg_len),
+        )
+        d_qkv_ref[slot, 0, 0] += d_queries
+        for entry, (where, _) in enumerate(chain):
+            rows = slice(entry * seg_len, (entry + 1) * seg_len)
+            d_qkv_ref[where, 1, 0] += d_keys[rows]
+            d_qkv_ref[where, 2, 0] += d_values[rows]
+        return carry
+
+    lax.fori_loop(0, slots, one_slot, 0)
+
+    normed = split(normed_ref[...].reshape(slots * seg_len, -1))
+    inner = split(ADAPT_SCALE * inner_ref[...].reshape(slots * seg_len, 3 * rank))
+    for kind in range(3):
+        grads = split(d_qkv_ref[:, kind, 0].reshape(slots * seg_len, pair))
+        ranks = slice(kind * rank, (kind + 1) * rank)
+        d_inner = split(ADAPT_SCALE * dot2(grads, up_ref[0, kind], NT))
+        g_down_ref[0, kind] = dot3(d_inner, normed, TN)
+        g_up_ref[0, kind] = dot3(both(inner, (slice(None), ranks)), grads, TN)
+
+
+def slots_spec(shape):
+    lead = len(shape) - 3
+    return pl.BlockSpec(
+        shape[:lead] + (1,) + shape[lead + 1 :],
+        lambda tree, *_: (0,) * lead + (tree, 0, 0),
+    )
+
+
+def tree_spec(shape):
+    return pl.BlockSpec((1,) + shape[1:], lambda tree, *_: (tree,) + (0,) * (len(shape) - 1))
+
+
+def self_call(kernel, depth, order, parents, operands, in_specs, out_shape, out_specs):
+    trees, slots = order.shape
+    return pl.pallas_call(
+        functools.partial(kernel, depth),
+        out_shape=out_shape,
+        grid_spec=pltpu.PrefetchScalarGridSpec(
+            num_scalar_prefetch=2,
+            grid=(trees,),
+            in_specs=in_specs,
+            out_specs=out_specs,
+            scratch_shapes=[pltpu.SMEM((slots,), jnp.int32)],
+        ),
+        compiler_params=vmem(56),
+    )(order, parents, *operands)
+
+
+def cross_forward_kernel(query_ref, key_ref, value_ref, context_ref):
+    context_ref[0] = by_head(
+        attend, query_ref[0] * HD ** (-0.5), key_ref[0], value_ref[0]
+    )
+
+
+def cross_backward_kernel(
+    query_ref, key_ref, value_ref, d_context_ref, d_query_ref, d_key_ref, d_value_ref
+):
+    d_query_ref[0], d_key_ref[0], d_value_ref[0] = by_head(
+        attend_back,
+        query_ref[0] * HD ** (-0.5),
+        key_ref[0],
+        value_ref[0],
+        d_context_ref[0],
+    )
+
+
+def cross_call(kernel, queries, memory, rest, long_outs):
+    trees, seg_len, width = queries.shape
+    enc_rows = memory.shape[1]
+    lanes = 2 * HD
+    steps = width // lanes
+    short = pl.BlockSpec((1, seg_len, lanes), lambda tree, step: (tree, 0, step))
+    keys = pl.BlockSpec((1, enc_rows, lanes), lambda tree, step: (tree, 0, step))
+    values = pl.BlockSpec((1, enc_rows, lanes), lambda tree, step: (tree, 0, steps + step))
+    return pl.pallas_call(
+        kernel,
+        out_shape=[shaped(trees, seg_len, width)] + [shaped(trees, enc_rows, width)] * long_outs,
+        grid=(trees, steps),
+        in_specs=[short, keys, values] + [short] * len(rest),
+        out_specs=[short] + [keys] * long_outs,
+        compiler_params=vmem(48),
+    )(queries, memory, memory, *rest)
+
+
+def square(ref):
+    return ref[...].reshape(-1, ref.shape[-1])
+
+
+def joined(ref):
+    slots, trees = ref.shape[:2]
+    return jnp.concatenate(
+        [
+            jnp.concatenate([ref[slot, tree] for slot in range(slots)], axis=1)
+            for tree in range(trees)
+        ],
+        axis=0,
+    )
+
+
+def rows_of(ref):
+    return ref[...].reshape(-1, ref.shape[-1])
+
+
+def tree_rows(trees, count):
+    return [slice(tree * count, (tree + 1) * count) for tree in range(trees)]
+
+
+def with_adapters(parts, down_ref, up_ref, entry, trees):
+    count = parts[0].shape[0] // trees
+    return jnp.concatenate(
+        [
+            adapted(both(parts, rows), down_ref[tree, entry], up_ref[tree, entry])[0]
+            for tree, rows in enumerate(tree_rows(trees, count))
+        ],
+        axis=0,
+    )
+
+
+def with_adapters_back(parts, grads, down_ref, up_ref, entry, trees, g_down_ref, g_up_ref, place):
+    count = parts[0].shape[0] // trees
+    terms = []
+    for tree, rows in enumerate(tree_rows(trees, count)):
+        term, g_down_ref[tree, place], g_up_ref[tree, place] = adapted_back(
+            both(parts, rows), both(grads, rows), down_ref[tree, entry], up_ref[tree, entry]
+        )
+        terms.append(term)
+    return jnp.concatenate(terms, axis=0)
+
+
+def after_self_kernel(
+    context_ref, tokens_ref, gains_ref, out_ref, query_ref, down_ref, up_ref, middle_ref, cross_ref
+):
+    trees = tokens_ref.shape[0]
+    context = split(joined(context_ref))
+    middle = rows_of(tokens_ref) + dot3(context, split(square(out_ref)))
+    middle = middle + with_adapters(context, down_ref, up_ref, 3, trees)
+    middle_ref[...] = middle.reshape(middle_ref.shape)
+    normed = split(layer_norm(middle, gains_ref[1:2])[0])
+    queries = dot3(normed, split(square(query_ref)), NT)
+    queries = queries + with_adapters(normed, down_ref, up_ref, 4, trees)
+    cross_ref[...] = queries.reshape(cross_ref.shape)
+
+
+def after_cross_kernel(
+    context_ref, middle_ref, gains_ref, out_ref, down_ref, up_ref, after_ref, normed_ref
+):
+    trees = context_ref.shape[0]
+    context = split(rows_of(context_ref))
+    after = rows_of(middle_ref) + dot3(context, split(square(out_ref)))
+    after = after + with_adapters(context, down_ref, up_ref, 7, trees)
+    after_ref[...] = after.reshape(after_ref.shape)
+    normed = layer_norm(after, gains_ref[2:3])[0]
+    normed_ref[...] = normed.reshape(normed_ref.shape)
+
+
+def into_cross_kernel(
+    own_ref,
+    other_ref,
+    after_ref,
+    cotangent_ref,
+    context_ref,
+    gains_ref,
+    out_ref,
+    down_ref,
+    up_ref,
+    d_after_ref,
+    d_context_ref,
+    g_down_ref,
+    g_up_ref,
+):
+    trees = after_ref.shape[0]
+    _, normal, inverse = layer_norm(rows_of(after_ref), gains_ref[2:3])
+    d_normed = rows_of(own_ref) + rows_of(other_ref)
+    d_after = rows_of(cotangent_ref) + norm_back(normal, inverse, gains_ref[2:3], d_normed)
+    d_after_ref[...] = d_after.reshape(d_after_ref.shape)
+    grads = split(d_after)
+    context = split(rows_of(context_ref))
+    d_context = dot3(grads, split(square(out_ref)), NT)
+    d_context = d_context + with_adapters_back(
+        context, grads, down_ref, up_ref, 7, trees, g_down_ref, g_up_ref, 0
+    )
+    d_context_ref[...] = d_context.reshape(d_context_ref.shape)
+
+
+def into_self_kernel(
+    d_query_ref,
+    d_after_ref,
+    middle_ref,
+    context_ref,
+    gains_ref,
+    query_ref,
+    out_ref,
+    down_ref,
+    up_ref,
+    d_middle_ref,
+    d_context_ref,
+    g_down_ref,
+    g_up_ref,
+):
+    slots, trees, seg_len, lanes = context_ref.shape
+    rows, normal, inverse = layer_norm(rows_of(middle_ref), gains_ref[1:2])
+    grads = split(rows_of(d_query_ref))
+    d_normed = dot3(grads, split(square(query_ref)))
+    d_normed = d_normed + with_adapters_back(
+        split(rows), grads, down_ref, up_ref, 4, trees, g_down_ref, g_up_ref, 1
+    )
+    d_middle = rows_of(d_after_ref) + norm_back(normal, inverse, gains_ref[1:2], d_normed)
+    d_middle_ref[...] = d_middle.reshape(d_middle_ref.shape)
+    grads = split(d_middle)
+    context = split(joined(context_ref))
+    d_context = dot3(grads, split(square(out_ref)), NT)
+    d_context = d_context + with_adapters_back(
+        context, grads, down_ref, up_ref, 3, trees, g_down_ref, g_up_ref, 0
+    )
+    for slot in range(slots):
+        for tree in range(trees):
+            d_context_ref[slot, tree] = d_context[
+                tree * seg_len : (tree + 1) * seg_len, slot * lanes : (slot + 1) * lanes
+            ]
+
+
+def packed_spec(packed, first, count):
+    return pl.BlockSpec(
+        packed.shape[:2] + (count, packed.shape[3]), lambda *_: (0, 0, first // count, 0)
+    )
+
+
+def rows_call(kernel, operands, specs, out_shape):
+    return pl.pallas_call(
+        kernel,
+        out_shape=out_shape,
+        grid=(1,),
+        in_specs=[
+            whole_spec(operand.shape) if spec is None else spec
+            for operand, spec in zip(operands, specs)
+        ],
+        out_specs=[whole_spec(out.shape) for out in out_shape],
+        compiler_params=vmem(56),
+    )(*operands)
+
+
+def memory_kernel(encoder_ref, weight_ref, down_ref, up_ref, memory_ref, row_high, row_low, inner):
+    trees, rank = down_ref.shape[0], down_ref.shape[2]
+    step = pl.program_id(0)
+    half = pl.num_programs(0) // 2
+    lanes = memory_ref.shape[2]
+    count = encoder_ref.shape[1]
+
+    @pl.when(step == 0)
+    def _():
+        row_high[...], row_low[...] = split(rows_of(encoder_ref))
+        for tree, rows in enumerate(tree_rows(trees, count)):
+            for kind in range(2):
+                parts = (row_high[rows], row_low[rows])
+                inner[kind, rows] = jnp.concatenate(
+                    split(ADAPT_SCALE * dot2(parts, down_ref[tree, 5 + kind], NT)), axis=1
+                )
+
+    result = dot3((row_high[...], row_low[...]), split(square(weight_ref)), NT)
+    kind = step // half
+    for tree, rows in enumerate(tree_rows(trees, count)):
+        up = up_ref[tree, 0]
+        term = dot(inner[kind, rows], jnp.concatenate([up, up], axis=0))
+        memory_ref[tree] = result[rows] + term
+
+
+def memory_call(encoder, packed, down, up):
+    trees, count, width = encoder.shape
+    rank = down.shape[2]
+    slots, copies = packed.shape[:2]
+    lanes = 2 * width // slots
+    half = slots // 2
+    return pl.pallas_call(
+        memory_kernel,
+        out_shape=shaped(trees, count, 2 * width),
+        grid=(slots,),
+        in_specs=[
+            whole_spec(encoder.shape),
+            pl.BlockSpec((1, copies, lanes // copies, width), lambda step: (step, 0, 0, 0)),
+            whole_spec(down.shape),
+            pl.BlockSpec((trees, 1, rank, lanes), lambda step: (0, 5 + step // half, 0, step % half)),
+        ],
+        out_specs=pl.BlockSpec((trees, count, lanes), lambda step: (0, 0, step)),
+        scratch_shapes=[
+            pltpu.VMEM((trees * count, width), BF16),
+            pltpu.VMEM((trees * count, width), BF16),
+            pltpu.VMEM((2, trees * count, 2 * rank), BF16),
+        ],
+        compiler_params=vmem(56),
+    )(encoder, packed, down, up)
+
+
+def memory_back_kernel(
+    encoder_ref,
+    d_key_ref,
+    d_value_ref,
+    weight_ref,
+    down_ref,
+    up_ref,
+    d_encoder_ref,
+    g_down_ref,
+    g_up_ref,
+    row_high,
+    row_low,
+    inner,
+    d_inner,
+):
+    trees, rank = down_ref.shape[0], down_ref.shape[2]
+    step = pl.program_id(0)
+    half = pl.num_programs(0) // 2
+    count = encoder_ref.shape[1]
+    spans = tree_rows(trees, count)
+
+    @pl.when(step == 0)
+    def _():
+        row_high[...], row_low[...] = split(rows_of(encoder_ref))
+        d_encoder_ref[...] = jnp.zeros_like(d_encoder_ref)
+        d_inner[...] = jnp.zeros_like(d_inner)
+        for tree, rows in enumerate(spans):
+            for kind in range(2):
+                parts = (row_high[rows], row_low[rows])
+                inner[kind, rows] = jnp.concatenate(
+                    split(ADAPT_SCALE * dot2(parts, down_ref[tree, 5 + kind], NT)), axis=1
+                )
+
+    kind = step // half
+    grads = split(jnp.where(kind == 0, rows_of(d_key_ref), rows_of(d_value_ref)))
+    d_encoder_ref[...] += dot3(grads, split(square(weight_ref))).reshape(d_encoder_ref.shape)
+    for tree, rows in enumerate(spans):
+        own = both(grads, rows)
+        d_inner[kind, rows] += dot2(own, up_ref[tree, 0], NT)
+        high, low = inner[kind, rows, :rank], inner[kind, rows, rank:]
+        g_up_ref[tree, 0] = dot3((high, low), own, TN)
+
+    @pl.when(step == 2 * half - 1)
+    def _():
+        for tree, rows in enumerate(spans):
+            parts = (row_high[rows], row_low[rows])
+            for kind in range(2):
+                own = split(ADAPT_SCALE * d_inner[kind, rows])
+                d_encoder_ref[tree] += dot2(own, down_ref[tree, 5 + kind])
+                g_down_ref[tree, kind] = dot3(own, parts, TN)
+
+
+def memory_back_call(encoder, d_keys, d_values, packed, down, up):
+    trees, count, width = encoder.shape
+    rank = down.shape[2]
+    slots, copies = packed.shape[:2]
+    lanes = 2 * width // slots
+    half = slots // 2
+    kind_spec = pl.BlockSpec((trees, 1, rank, lanes), lambda step: (0, step // half, 0, step % half))
+    return pl.pallas_call(
+        memory_back_kernel,
+        out_shape=[
+            shaped(trees, count, width),
+            shaped(trees, 2, rank, width),
+            shaped(trees, 2, rank, width),
+        ],
+        grid=(slots,),
+        in_specs=[
+            whole_spec(encoder.shape),
+            pl.BlockSpec((trees, count, lanes), lambda step: (0, 0, jnp.minimum(step, half - 1))),
+            pl.BlockSpec((trees, count, lanes), lambda step: (0, 0, jnp.maximum(step - half, 0))),
+            pl.BlockSpec((1, copies, lanes // copies, width), lambda step: (step, 0, 0, 0)),
+            whole_spec(down.shape),
+            pl.BlockSpec((trees, 1, rank, lanes), lambda step: (0, 5 + step // half, 0, step % half)),
+        ],
+        out_specs=[
+            whole_spec((trees, count, width)),
+            whole_spec((trees, 2, rank, width)),
+            kind_spec,
+        ],
+        scratch_shapes=[
+            pltpu.VMEM((trees * count, width), BF16),
+            pltpu.VMEM((trees * count, width), BF16),
+            pltpu.VMEM((2, trees * count, 2 * rank), BF16),
+            pltpu.VMEM((2, trees * count, rank), F32),
+        ],
+        compiler_params=vmem(56),
+    )(encoder, d_keys, d_values, packed, down, up)
+
+
+def feed_forward_kernel(
+    rows_ref,
+    cot_ref,
+    w_in_ref,
+    w_out_ref,
+    in_up_ref,
+    out_down_ref,
+    in_down_ref,
+    out_up_ref,
+    out_ref,
+    d_rows_ref,
+    g_in_up_ref,
+    g_out_down_ref,
+    g_in_down_ref,
+    g_out_up_ref,
+    row_high,
+    row_low,
+    cot_high,
+    cot_low,
+    inner_in,
+    d_inner_out,
+    inner_in_t,
+    d_inner_out_t,
+    inner_out,
+    d_inner_in,
+):
+    trees, rank = in_up_ref.shape[0], in_up_ref.shape[1]
+    step = pl.program_id(0) * pl.num_programs(1) + pl.program_id(1)
+    last = pl.num_programs(0) * pl.num_programs(1) - 1
+    spans = tree_rows(trees, rows_ref.shape[0] // trees)
+
+    @pl.when(step == 0)
+    def _():
+        row_high[...], row_low[...] = split(rows_ref[...])
+        cot_high[...], cot_low[...] = split(cot_ref[...])
+        out_ref[...] = jnp.zeros_like(out_ref)
+        d_rows_ref[...] = jnp.zeros_like(d_rows_ref)
+        inner_out[...] = jnp.zeros_like(inner_out)
+        d_inner_in[...] = jnp.zeros_like(d_inner_in)
+        for tree, own in enumerate(spans):
+            rows = (row_high[own], row_low[own])
+            cots = (cot_high[own], cot_low[own])
+            down, up = in_down_ref[tree], out_up_ref[tree]
+            inner_in[own] = jnp.concatenate(
+                split(ADAPT_SCALE * dot2(rows, down, NT)), axis=1
+            )
+            d_inner_out[own] = jnp.concatenate(
+                split(ADAPT_SCALE * dot2(cots, up, NT)), axis=1
+            )
+            inner_in_t[tree] = jnp.concatenate(
+                split(ADAPT_SCALE * (dot(down, rows[0], NT) + dot(down, rows[1], NT))), axis=0
+            )
+            d_inner_out_t[tree] = jnp.concatenate(
+                split(ADAPT_SCALE * (dot(up, cots[0], NT) + dot(up, cots[1], NT))), axis=0
+            )
+
+    rows = (row_high[...], row_low[...])
+    cots = (cot_high[...], cot_low[...])
+    w_in = split(w_in_ref[0])
+    w_out = split(w_out_ref[0])
+
+    def per_tree(inner, maps):
+        return jnp.concatenate(
+            [
+                dot(inner[own], jnp.concatenate([maps[tree], maps[tree]], axis=0))
+                for tree, own in enumerate(spans)
+            ],
+            axis=0,
+        )
+
+    pre_act = dot3(rows, w_in) + per_tree(inner_in, in_up_ref)
+    root = math.sqrt(2.0 / math.pi)
+    squared = pre_act * pre_act
+    bend = jnp.tanh(root * (pre_act + 0.044715 * (squared * pre_act)))
+    hidden = 0.5 * pre_act * (1.0 + bend)
+    slope = 0.5 * (1.0 + bend) + 0.5 * pre_act * (1.0 - bend * bend) * (
+        root * (1.0 + 3 * 0.044715 * squared)
+    )
+    hidden_parts = split(hidden)
+    out_ref[...] += dot3(hidden_parts, w_out)
+    d_hidden = dot3(cots, w_out, NT) + per_tree(d_inner_out, out_down_ref)
+    pre_parts = split(d_hidden * slope)
+    d_rows_ref[...] += dot3(pre_parts, w_in, NT)
+
+    for tree, own in enumerate(spans):
+        hidden_own = both(hidden_parts, own)
+        pre_own = both(pre_parts, own)
+        inner_out[own] += dot2(hidden_own, out_down_ref[tree], NT)
+        d_inner_in[own] += dot2(pre_own, in_up_ref[tree], NT)
+        pair = dot(inner_in_t[tree], pre_own[0])
+        g_in_up_ref[tree] = (
+            pair[:rank] + pair[rank:] + dot(inner_in_t[tree, :rank], pre_own[1])
+        )
+        pair = dot(d_inner_out_t[tree], hidden_own[0])
+        g_out_down_ref[tree] = (
+            pair[:rank] + pair[rank:] + dot(d_inner_out_t[tree, :rank], hidden_own[1])
+        )
+
+    @pl.when(step == last)
+    def _():
+        for tree, own in enumerate(spans):
+            inner = split(ADAPT_SCALE * inner_out[own])
+            d_inner = split(ADAPT_SCALE * d_inner_in[own])
+            out_ref[own] += dot2(inner, out_up_ref[tree])
+            d_rows_ref[own] += dot2(d_inner, in_down_ref[tree])
+            g_in_down_ref[tree] = dot3(d_inner, (row_high[own], row_low[own]), TN)
+            g_out_up_ref[tree] = dot3(inner, (cot_high[own], cot_low[own]), TN)
+
+
+def feed_forward(rows, cots, weights, in_up, out_down, in_down, out_up):
+    count, width = rows.shape
+    w_in, w_out = weights
+    shards, units = w_in.shape[0], w_in.shape[2]
+    trees, rank = in_up.shape[0], in_up.shape[1]
+    block = min(units, 512)
+    steps = units // block
+    columns = pl.BlockSpec(
+        (trees, rank, block), lambda shard, step: (0, 0, shard * steps + step)
+    )
+    maps = [whole_spec(in_down.shape), whole_spec(out_up.shape)]
+    rows_spec = whole_spec((count, width))
+    return pl.pallas_call(
+        feed_forward_kernel,
+        out_shape=[shaped(count, width)] * 2
+        + [shaped(*in_up.shape), shaped(*out_down.shape)]
+        + [shaped(*in_down.shape), shaped(*out_up.shape)],
+        grid=(shards, steps),
+        in_specs=[
+            rows_spec,
+            rows_spec,
+            pl.BlockSpec((1, width, block), lambda shard, step: (shard, 0, step)),
+            pl.BlockSpec((1, block, width), lambda shard, step: (shard, step, 0)),
+            columns,
+            columns,
+        ]
+        + maps,
+        out_specs=[rows_spec, rows_spec, columns, columns] + maps,
+        scratch_shapes=[pltpu.VMEM((count, width), BF16)] * 4
+        + [pltpu.VMEM((count, 2 * rank), BF16)] * 2
+        + [pltpu.VMEM((trees, 2 * rank, count // trees), BF16)] * 2
+        + [pltpu.VMEM((count, rank), F32)] * 2,
+        compiler_params=vmem(56),
+    )(rows, cots, w_in, w_out, in_up, out_down, in_down, out_up)
+
+
+def into_tokens_kernel(
+    d_qkv_ref, weight_ref, tokens_ref, d_middle_ref, gains_ref, down_ref, up_ref, out_ref, total
+):
+    slots, trees, seg_len = d_qkv_ref.shape[0], d_qkv_ref.shape[2], d_qkv_ref.shape[3]
+    kind = pl.program_id(0)
+    spans = tree_rows(trees, seg_len)
+
+    @pl.when(kind == 0)
+    def _():
+        total[...] = jnp.zeros_like(total)
+
+    grads = split(joined(d_qkv_ref.at[:, 0]))
+    total[...] += dot3(grads, split(weight_ref[...]))
+    for tree, rows in enumerate(spans):
+        inner = split(ADAPT_SCALE * dot2(both(grads, rows), up_ref[tree, 0], NT))
+        total[rows] += dot2(inner, down_ref[tree, 0])
+
+    @pl.when(kind == pl.num_programs(0) - 1)
+    def _():
+        _, normal, inverse = layer_norm(rows_of(tokens_ref), gains_ref[0:1])
+        grad = rows_of(d_middle_ref) + norm_back(normal, inverse, gains_ref[0:1], total[...])
+        out_ref[...] = grad.reshape(out_ref.shape)
+
+
+def into_tokens_call(d_qkv, weight, tokens, d_middle, gains, down, up):
+    slots, kinds, trees, seg_len, lanes = d_qkv.shape
+    width = tokens.shape[2]
+    rank = up.shape[2]
+    one = pl.BlockSpec((trees, 1, rank, width), lambda kind: (0, kind, 0, 0))
+    return pl.pallas_call(
+        into_tokens_kernel,
+        out_shape=shaped(*tokens.shape),
+        grid=(kinds,),
+        in_specs=[
+            pl.BlockSpec((slots, 1, trees, seg_len, lanes), lambda kind: (0, kind, 0, 0, 0)),
+            pl.BlockSpec((width, width), lambda kind: (kind, 0)),
+            whole_spec(tokens.shape),
+            whole_spec(tokens.shape),
+            whole_spec(gains.shape),
+            one,
+            one,
+        ],
+        out_specs=whole_spec(tokens.shape),
+        scratch_shapes=[pltpu.VMEM((trees * seg_len, width), F32)],
+        compiler_params=vmem(56),
+    )(d_qkv, weight, tokens, d_middle, gains, down, up)
+
+
+def place_kernel(source_ref, early_ref, late_ref, down_ref, up_ref, in_down_ref, out_up_ref):
+    owners = early_ref.shape[1]
+    late_count = late_ref.shape[3] // 2
+    early_count = early_ref.shape[3] // 2 - 1
+    for owner in range(owners):
+        lanes = slice(owner * late_ref.shape[5], (owner + 1) * late_ref.shape[5])
+        for entry in range(late_count):
+            down_ref[0, entry, :, lanes] = late_ref[0, owner, 0, entry]
+            up_ref[0, entry, :, lanes] = late_ref[0, owner, 0, late_count + entry]
+        for entry in range(early_count):
+            down_ref[0, late_count + entry, :, lanes] = early_ref[0, owner, 0, entry]
+            up_ref[0, late_count + entry, :, lanes] = early_ref[0, owner, 0, early_count + entry]
+        in_down_ref[0, :, lanes] = early_ref[0, owner, 0, 2 * early_count]
+        out_up_ref[0, :, lanes] = early_ref[0, owner, 0, 2 * early_count + 1]
+
+
+def place_hidden_kernel(source_ref, parts_ref, in_up_ref, out_down_ref):
+    for owner in range(parts_ref.shape[1]):
+        units = parts_ref.shape[5]
+        lanes = slice(owner * units, (owner + 1) * units)
+        in_up_ref[0, :, lanes] = parts_ref[0, owner, 0, 0]
+        out_down_ref[0, :, lanes] = parts_ref[0, owner, 0, 1]
+
+
+def place_call(kernel, source, arrays, out_shape):
+    def chosen(array):
+        groups = array.shape[2]
+        return pl.BlockSpec(
+            (1, array.shape[1], 1) + array.shape[3:],
+            lambda entry, tree: (tree[entry] // groups, 0, tree[entry] % groups, 0, 0, 0),
+        )
+
+    return pl.pallas_call(
+        kernel,
+        out_shape=out_shape,
+        grid_spec=pltpu.PrefetchScalarGridSpec(
+            num_scalar_prefetch=1,
+            grid=(out_shape[0].shape[0],),
+            in_specs=[chosen(array) for array in arrays],
+            out_specs=[tree_spec(out.shape) for out in out_shape],
+        ),
+        compiler_params=vmem(48),
+    )(source, *arrays)
+
+
+def my_quarter(shard):
+    part = shard.shape[0] // lax.axis_size(COPIES)
+    return lax.dynamic_slice_in_dim(shard, lax.axis_index(COPIES) * part, part, 0)
+
+
+def gather_pair_half(shard):
+    whole = lax.all_gather(my_quarter(shard), ("z",) + COPIES, axis=0, tiled=True)
+    return whole.reshape((-1,) + shard.shape)
+
+
+def pick(table, adapter_pick):
+    return jnp.stack(
+        [
+            lax.dynamic_index_in_dim(table, adapter_pick[tree], 0, keepdims=False)
+            for tree in range(adapter_pick.shape[0])
+        ]
+    )
+
+
+def own_heads(w_qkv):
+    slots = lax.axis_size(ROWS)
+    lanes = w_qkv.shape[1] // 3
+    me = lax.axis_index(ROWS)
+    blocks = [
+        lax.ppermute(
+            w_qkv[:, i * lanes : (i + 1) * lanes],
+            ROWS,
+            [(s, (3 * s + i) % slots) for s in range(slots)],
+        )
+        for i in range(3)
+    ]
+    kinds = [0] * (3 * slots)
+    for s in range(slots):
+        for i in range(3):
+            kinds[(3 * s + i) % slots * 3 + (3 * s + i) // slots] = i
+    stacked = jnp.stack(blocks)
+    table = jnp.array(kinds, jnp.int32)
+    return jnp.stack(
+        [
+            lax.dynamic_index_in_dim(stacked, table[me * 3 + kind], 0, keepdims=False)
+            for kind in range(3)
+        ]
+    )
+
+
+def swap(array):
+    return lax.ppermute(array, "y", SWAP)
+
+
+def summed_to_owner(parts, axes):
+    return jnp.sum(lax.all_to_all(parts, axes, split_axis=0, concat_axis=0, tiled=True), axis=0)
+
+
+def to_everyone(array):
+    everyone = lax.all_gather(array, COPIES + ROWS, axis=0, tiled=False)
+    return everyone.reshape((-1, lax.axis_size(ROWS)) + array.shape)
+
+
+def by_heads(
+    tokens,
+    encoder,
+    cotangent,
+    adapter_pick,
+    segment_order,
+    parents,
+    norm_gains,
+    w_qkv,
+    w_self_out,
+    w_cross_q,
+    w_cross_kv,
+    w_cross_out,
+    w_fc_in,
+    w_fc_out,
+    attn_down,
+    attn_up,
+    fc_in_down,
+    fc_in_up,
+    fc_out_down,
+    fc_out_up,
+):
+    trees, seg_len, width = tokens.shape
+    slots = lax.axis_size(ROWS)
+    copies = lax.axis_size(COPIES)
+    adapters, projections, rank = attn_up.shape[:3]
+    hidden_units = fc_in_up.shape[2]
+    pairs = lax.axis_size("y")
+    me, my_y = lax.axis_index(ROWS), lax.axis_index("y")
+    lanes = width // slots
+    depth = 4
+
+    down = pick(attn_down.swapaxes(2, 3), adapter_pick)
+    up = pick(attn_up, adapter_pick)
+    in_down = pick(fc_in_down.swapaxes(1, 2), adapter_pick)
+    out_up = pick(fc_out_up, adapter_pick)
+
+    def half_columns(table):
+        picked = pick(table, adapter_pick).reshape(
+            trees, rank, slots // pairs, pairs, hidden_units // slots
+        )
+        return lax.dynamic_index_in_dim(picked, my_y, 3, keepdims=False).reshape(
+            trees, rank, hidden_units // pairs
+        )
+
+    in_up = half_columns(fc_in_up)
+    out_down = half_columns(fc_out_down.swapaxes(1, 2))
+    down_qkv = down[:, 0:3].reshape(trees, 3 * rank, width)
+    up_own = lax.dynamic_slice_in_dim(up[:, 0:3], me * lanes, lanes, 3)
+
+    parts = [my_quarter(w) for w in (w_cross_kv.T, w_self_out, w_cross_out, w_cross_q.T)]
+    packed = lax.all_gather(jnp.concatenate(parts, axis=0), EVERY, axis=0, tiled=False)
+    packed = packed.reshape((slots, copies) + packed.shape[1:])
+    row = width // (slots * copies)
+    self_out_spec = packed_spec(packed, 2 * row, row)
+    cross_out_spec = packed_spec(packed, 3 * row, row)
+    cross_q_spec = packed_spec(packed, 4 * row, row)
+    fc_in_half = gather_pair_half(w_fc_in)
+    fc_out_half = gather_pair_half(w_fc_out)
+    qkv_rows = lax.all_gather(my_quarter(w_qkv.T), EVERY, axis=0, tiled=True)
+
+    normed_all, inner_all, qkv = heads_call(
+        tokens, norm_gains, own_heads(w_qkv), down_qkv, up_own
+    )
+    own_context = self_call(
+        self_forward_kernel,
+        depth,
+        segment_order,
+        parents,
+        (qkv,),
+        [slots_spec(qkv.shape)],
+        shaped(slots, trees, seg_len, lanes),
+        slots_spec((slots, trees, seg_len, lanes)),
+    )
+    context = lax.all_to_all(own_context, ROWS, split_axis=0, concat_axis=0, tiled=True)
+
+    memory = memory_call(encoder, packed, down, up)
+    middle, cross_queries = rows_call(
+        after_self_kernel,
+        (context, tokens, norm_gains, packed, packed, down, up),
+        (None, None, None, self_out_spec, cross_q_spec, None, None),
+        [shaped(*tokens.shape)] * 2,
+    )
+    (cross_context,) = cross_call(cross_forward_kernel, cross_queries, memory, (), 0)
+    after_cross, normed_three = rows_call(
+        after_cross_kernel,
+        (cross_context, middle, norm_gains, packed, down, up),
+        (None, None, None, cross_out_spec, None, None),
+        [shaped(*tokens.shape)] * 2,
+    )
+
+    def with_partner(rows):
+        return jnp.stack([rows, swap(rows)], axis=1).reshape(-1, width)
+
+    out_part, d_rows_part, g_in_up, g_out_down, g_in_down, g_out_up = feed_forward(
+        with_partner(normed_three),
+        with_partner(cotangent),
+        (fc_in_half, fc_out_half),
+        in_up,
+        out_down,
+        in_down,
+        out_up,
+    )
+    d_rows_part = d_rows_part.reshape(trees, 2, seg_len, width)
+    out_part = out_part.reshape(trees, 2, seg_len, width)
+    d_rows_other = swap(d_rows_part[:, 1])
+    layer_out = after_cross + out_part[:, 0] + swap(out_part[:, 1])
+
+    pair_maps = [shaped(trees, 1, rank, width)] * 2
+    d_after, d_cross_ctx, g_down_seven, g_up_seven = rows_call(
+        into_cross_kernel,
+        (
+            d_rows_part[:, 0],
+            d_rows_other,
+            after_cross,
+            cotangent,
+            cross_context,
+            norm_gains,
+            packed,
+            down,
+            up,
+        ),
+        (None,) * 6 + (cross_out_spec, None, None),
+        [shaped(*tokens.shape)] * 2 + pair_maps,
+    )
+    d_cross_q, d_cross_k, d_cross_v = cross_call(
+        cross_backward_kernel, cross_queries, memory, (d_cross_ctx,), 2
+    )
+    d_middle, d_context, g_down_mid, g_up_mid = rows_call(
+        into_self_kernel,
+        (d_cross_q, d_after, middle, context, norm_gains, packed, packed, down, up),
+        (None,) * 5 + (cross_q_spec, self_out_spec, None, None),
+        [shaped(*tokens.shape), shaped(slots, trees, seg_len, lanes)]
+        + [shaped(trees, 2, rank, width)] * 2,
+    )
+    d_own_context = lax.all_to_all(d_context, ROWS, split_axis=0, concat_axis=0, tiled=True)
+    d_encoder, g_down_memory, g_up_memory = memory_back_call(
+        encoder, d_cross_k, d_cross_v, packed, down, up
+    )
+    grad_encoder = lax.psum_scatter(d_encoder, ROWS, scatter_dimension=1, tiled=True)
+
+    def columns(parts):
+        stack = jnp.concatenate(parts, axis=1)
+        return stack.reshape(stack.shape[:3] + (slots, lanes)).transpose(3, 0, 1, 2, 4)
+
+    hidden_parts = jnp.stack([g_in_up, g_out_down], axis=1).reshape(
+        trees, 2, rank, slots // pairs, hidden_units // slots
+    )
+    hidden_all = to_everyone(summed_to_owner(hidden_parts.transpose(3, 0, 1, 2, 4), "z"))
+    early = columns(
+        [
+            g_down_mid,
+            g_down_memory,
+            g_down_seven,
+            g_up_mid,
+            g_up_memory,
+            g_up_seven,
+            g_in_down[:, None],
+            g_out_up[:, None],
+        ]
+    )
+    early_all = to_everyone(summed_to_owner(early, ROWS))
+
+    normed_shape = (slots, trees, seg_len, width)
+    d_qkv, g_down_part, g_up_qkv = self_call(
+        self_backward_kernel,
+        depth,
+        segment_order,
+        parents,
+        (qkv, d_own_context, normed_all.reshape(normed_shape), inner_all, up_own),
+        [
+            slots_spec(qkv.shape),
+            slots_spec(d_own_context.shape),
+            slots_spec(normed_shape),
+            slots_spec(inner_all.shape),
+            tree_spec(up_own.shape),
+        ],
+        [
+            shaped(*qkv.shape),
+            shaped(trees, 3, rank, width),
+            shaped(trees, 3, rank, lanes),
+        ],
+        [
+            slots_spec(qkv.shape),
+            tree_spec((trees, 3, rank, width)),
+            tree_spec((trees, 3, rank, lanes)),
+        ],
+    )
+    g_down_qkv = summed_to_owner(columns([g_down_part]), ROWS)
+    late_all = to_everyone(jnp.concatenate([g_down_qkv, g_up_qkv], axis=1))
+    d_split = lax.all_to_all(d_qkv, ROWS, split_axis=0, concat_axis=0, tiled=True)
+    grad_tokens = into_tokens_call(
+        d_split, qkv_rows, tokens, d_middle, norm_gains, down, up
+    )
+
+    all_picks = lax.all_gather(adapter_pick, COPIES, axis=0, tiled=True)
+    entry = lax.broadcasted_iota(jnp.int32, (adapters, 1), 0)
+    tree_index = lax.broadcasted_iota(jnp.int32, (1, all_picks.shape[0]), 1)
+    source = jnp.sum(jnp.where(entry == all_picks[None, :], tree_index, 0), axis=1)
+    wide = shaped(adapters, projections, rank, width)
+    narrow = shaped(adapters, rank, width)
+    grad_down, grad_up, grad_in_down, grad_out_up = place_call(
+        place_kernel, source, (early_all, late_all), [wide, wide, narrow, narrow]
+    )
+    grad_in_up, grad_out_down = place_call(
+        place_hidden_kernel, source, (hidden_all,), [shaped(adapters, rank, hidden_units)] * 2
+    )
+    return (
+        layer_out,
+        grad_tokens,
+        grad_encoder,
+        grad_down.swapaxes(2, 3),
+        grad_up,
+        grad_in_down.swapaxes(1, 2),
+        grad_in_up,
+        grad_out_down.swapaxes(1, 2),
+        grad_out_up,
+    )
+
+
+def placements(rows, copies):
+    spread = P(copies, rows, None)
+    ins = (
+        spread,
+        P(copies, None, None),
+        spread,
+        P(copies),
+        P(copies, None),
+        P(copies, None),
+        P(),
+        P(None, rows),
+        P(rows, None),
+        P(None, rows),
+        P(None, rows),
+        P(rows, None),
+        P(None, rows),
+        P(rows, None),
+    ) + (P(),) * 6
+    return ins, (spread,) * 3 + (P(),) * 6
+
+
 def solution(mesh):
-    return jax.shard_map(
+    copies, rows = mesh.shape["dp"], mesh.shape["seq"]
+    general = jax.shard_map(
         shards,
         mesh=mesh,
-        in_specs=(
-            P("dp", "seq", None),
-            P("dp", None, None),
-            P("dp", "seq", None),
-            P("dp"),
-            P("dp", None),
-            P("dp", None),
-            P(),
-            P(None, "seq"),
-            P("seq", None),
-            P(None, "seq"),
-            P(None, "seq"),
-            P("seq", None),
-            P(None, "seq"),
-            P("seq", None),
-            P(),
-            P(),
-            P(),
-            P(),
-            P(),
-            P(),
-        ),
-        out_specs=(
-            P("dp", "seq", None),
-            P("dp", "seq", None),
-            P("dp", "seq", None),
-            P(),
-            P(),
-            P(),
-            P(),
-            P(),
-            P(),
-        ),
+        in_specs=placements("seq", "dp")[0],
+        out_specs=placements("seq", "dp")[1],
         check_vma=False,
     )
+    if rows != 8 or copies % 2:
+        return general
+    fine = jax.sharding.Mesh(
+        mesh.devices.reshape(copies // 2, 2, rows // 2, 2), ("x", "c", "z", "y")
+    )
+    ins, outs = placements(ROWS, COPIES)
+    special = jax.shard_map(by_heads, mesh=fine, in_specs=ins, out_specs=outs, check_vma=False)
+
+    def step(*arrays):
+        one_each = arrays[0].shape[0] == arrays[14].shape[0]
+        return (special if one_each else general)(*arrays)
+
+    return step

time: 3500 us -> 1140 us (0.33)
  waiting for transfers between devices: 2220 us -> 386 us
  matrix products: 684 us -> 0 us
  Pallas kernels: 0 us -> 503 us
  local copies, waits for them, and re-layouts: 372 us -> 47.8 us
    all_gather x13 -> x7, waiting for transfers between devices: 1720 us -> 163 us  [the longest x2 134 us: gather_pair_half(): lax.all_gather(my_quarter(shard), ('z',) + COPIES, axis=0, tiled=True)]
    dot_general x97 -> x0, matrix products: 682 us -> none  [the longest x65 399 us: product(): jnp.einsum(formula, first_operand, second_operand, precision=PRECISE, pre...]
    pallas_call x0 -> x15, Pallas kernels: none -> 503 us  [the longest x1 184 us: heads_call(): pl.pallas_call(heads_kernel, out_shape=[shaped(slots, trees * seg_len, wi...]
    unnamed x18 -> x8, waiting for transfers between devices: 299 us -> 0.81 us
    all_gather x2 -> x0, blocking collectives: 139 us -> none  [shards(): full_sums = lax.all_gather(owned, ('dp', 'seq'), axis=0, tiled=True)]
    all_to_all x0 -> x4, blocking collectives: none -> 130 us  [the longest x3 99.9 us: summed_to_owner(): lax.all_to_all(parts, axes, split_axis=0, concat_axis=0, tiled=True)]
    reduce_scatter x3 -> x1, waiting for transfers between devices: 197 us -> 81.3 us  [by_heads(): lax.psum_scatter(d_encoder, ROWS, scatter_dimension=1, tiled=True)]
    ppermute x0 -> x7, waiting for transfers between devices: none -> 105 us  [the longest x4 95.7 us: swap(): return lax.ppermute(array, 'y', SWAP)]
  transfers between devices with their start and end apart: 17 -> 17, of which waited for: 12 -> 10; matrix products, arithmetic and copies ran while one was open for 18% -> 4% of each run, Pallas kernels for 0% -> 44%
where the time goes in v1:
time: 1140 us; the launch traced here: 1130 us
  Pallas kernels  503 us (44%)
  waiting for transfers between devices  386 us (34%)
  blocking collectives  134 us (12%)
  local copies, waits for them, and re-layouts  47.8 us (4%)
  starting transfers between devices  26.3 us (2%)
  between operations  25.2 us (2%)
  other arithmetic  11.8 us (1%)
    pallas_call x1, Pallas kernels, heads_call(): pl.pallas_call(heads_kernel, out_shape=[shaped(slots, trees * seg_len, wi...  184 us
    all_gather x2, waiting for transfers between devices, gather_pair_half(): lax.all_gather(my_quarter(shard), ('z',) + COPIES, axis=0, tiled=True)  134 us
    all_to_all x3, blocking collectives, summed_to_owner(): lax.all_to_all(parts, axes, split_axis=0, concat_axis=0, tiled=True)  99.9 us
    ppermute x4, waiting for transfers between devices, swap(): return lax.ppermute(array, 'y', SWAP)  95.7 us
    reduce_scatter x1, waiting for transfers between devices, by_heads(): lax.psum_scatter(d_encoder, ROWS, scatter_dimension=1, tiled=True)  81.3 us
    pallas_call x1, Pallas kernels, feed_forward(): pl.pallas_call(feed_forward_kernel, out_shape=[shaped(count, width)] * 2...  75.9 us
    pallas_call x2, Pallas kernels, self_call(): pl.pallas_call(functools.partial(kernel, depth), out_shape=out_shape, gri...  63.7 us
    pallas_call x2, Pallas kernels, cross_call(): pl.pallas_call(kernel, out_shape=[shaped(trees, seg_len, width)] + [shape...  51.8 us
  transfers between devices with their start and end apart: 17, of which 10 were waited for; matrix products, arithmetic and copies ran while one was open for 4% of the time, Pallas kernels for 44%

profile of v1, /device:TPU:0, one launch (start us, length us, event | category | flops | bytes accessed | tf_op | source)
XLA Modules:
  0.0 1134.0 jit_solution(6438593616248209242)
XLA Ops:
  55.8 183.6 %shard_map.268 = (f32[8,256,1024]{2,1,0:T(8,128)}, f32[8,2,128,48]{3,2,1,0:T(8,128)S(1)}, f32[8,3,2,128,128]{4,3,2,1,0:T(8,128)}) custom-call(f32[2,128,1024]{2,1,0:T(8,128)S(1)} %copy-done.3, f32[3,1024]{1,0:T(4,128)S(1)} %copy-done.10, f32[3,1024,128]{2,1,0:T(8,128)S(1)} %pad_maximum_fusion.3.weight_ref, bf16[2,48,1024]{2,1,0:T(8,128)(2,1)S(1)} %bitcast.116, ...), custom_call_target="tpu_custom_call" | custom-call | tf_op jit(solution)/shard_map/pallas_call | solution.py:672
  240.5 20.3 %shard_map.269 = f32[8,2,128,128]{3,2,1,0:T(8,128)} custom-call(s32[2,8]{1,0:T(2,128)} %order_ref.3, s32[2,8]{1,0:T(2,128)} %parents_ref.3, f32[8,3,2,128,128]{4,3,2,1,0:T(8,128)} %get-tuple-element.45.qkv_ref), custom_call_target="tpu_custom_call" | custom-call | tf_op jit(solution)/shard_map/pallas_call | solution.py:846
  269.0 22.3 %shard_map.271.key_ref.value_ref = f32[2,512,2048]{2,1,0:T(8,128)} custom-call(f32[2,512,1024]{2,1,0:T(8,128)} %encoder_ref.3, f32[8,4,160,1024]{3,2,1,0:T(8,128)} %bitcast.117, bf16[2,8,16,1024]{3,2,1,0:T(8,128)(2,1)} %get-tuple-element.110.down_ref, bf16[2,8,16,1024]{3,2,1,0:T(8,128)(2,1)} %get-tuple-element.111.up_ref), custom_call_target="tpu_custom_call" | custom-call | tf_op jit(solution)/shard_map/pallas_call | solution.py:1084
  291.3 15.2 %all-to-all-done.context_ref = f32[8,2,128,128]{3,2,1,0:T(8,128)S(1)} async-done(((f32[8,2,128,128]{3,2,1,0:T(8,128)}), f32[8,2,128,128]{3,2,1,0:T(8,128)S(1)}, u32[]{:S(2)}, u32[]{:S(2)}) %all-to-all-start) | async-done | bytes 1048608 | tf_op jit(solution)/shard_map/all_to_all | solution.py:1564
  307.5 12.7 %shard_map.270 = (f32[2,128,1024]{2,1,0:T(8,128)}, f32[2,128,1024]{2,1,0:T(8,128)}) custom-call(f32[8,2,128,128]{3,2,1,0:T(8,128)} %copy-done.12, f32[2,128,1024]{2,1,0:T(8,128)} %tokens_ref.5, f32[3,1024]{1,0:T(4,128)} %gains_ref.11, f32[8,4,160,1024]{3,2,1,0:T(8,128)} %bitcast.118, f32[8,4,160,1024]{3,2,1,0:T(8,128)} %bitcast.119, ...), custom_call_target="tpu_custom_call" | custom-call | tf_op jit(solution)/shard_map/pallas_call | solution.py:1040
  321.4 19.2 %shard_map.272.context_ref = f32[2,128,1024]{2,1,0:T(8,128)S(1)} custom-call(f32[2,128,1024]{2,1,0:T(8,128)S(1)} %copy-done.4, f32[2,512,2048]{2,1,0:T(8,128)} %shard_map.271.key_ref.value_ref, f32[2,512,2048]{2,1,0:T(8,128)} %shard_map.271.key_ref.value_ref), custom_call_target="tpu_custom_call" | custom-call | tf_op jit(solution)/shard_map/pallas_call | solution.py:886
  361.7 12.8 %collective-permute-done.3 = f32[2,128,1024]{2,1,0:T(8,128)} collective-permute-done((f32[2,128,1024]{2,1,0:T(8,128)}, f32[2,128,1024]{2,1,0:T(8,128)}, u32[]{:S(2)}, u32[]{:S(2)}) %collective-permute-start.3) | collective-permute-done | bytes 1048608 | tf_op jit(solution)/shard_map/ppermute | solution.py:1478
  383.5 127.8 %all-gather.14.cloned.1.call-done = f32[4096,1024]{1,0:T(8,128)} async-done(((f32[256,1024]{1,0:T(8,128)}), f32[4096,1024]{1,0:T(8,128)}) %all-gather.14.cloned.1.call-update) | async-done | bytes 16777232 | tf_op jit(solution)/shard_map/all_gather | solution.py:1438
  511.4 75.9 %shard_map.274 = (f32[512,1024]{1,0:T(8,128)}, f32[512,1024]{1,0:T(8,128)}, f32[2,16,4096]{2,1,0:T(8,128)}, f32[2,16,4096]{2,1,0:T(8,128)}, f32[2,16,1024]{2,1,0:T(8,128)}, /*index=5*/f32[2,16,1024]{2,1,0:T(8,128)}) custom-call(f32[512,1024]{1,0:T(8,128)} %bitcast.129, f32[512,1024]{1,0:T(8,128)} %bitcast.128, f32[4,1024,1024]{2,1,0:T(8,128)} %bitcast.125, ...), custom_call_target="tpu_custom_call" | custom-call | tf_op jit(solution)/shard_map/pallas_call | solution.py:1315
  591.6 23.8 %collective-permute-done.6.other_ref = f32[2,128,1024]{2,1,0:T(8,128)S(1)} collective-permute-done((f32[2,128,1024]{2,1,0:T(8,128)S(1)}, f32[2,128,1024]{2,1,0:T(8,128)S(1)}, u32[]{:S(2)}, u32[]{:S(2)}) %collective-permute-start.6) | collective-permute-done | bytes 1048608 | tf_op jit(solution)/shard_map/ppermute | solution.py:1478
  626.5 32.6 %shard_map.276 = (f32[2,128,1024]{2,1,0:T(8,128)S(1)}, f32[2,512,1024]{2,1,0:T(8,128)}, f32[2,512,1024]{2,1,0:T(8,128)}) custom-call(f32[2,128,1024]{2,1,0:T(8,128)S(1)} %copy-done.5, f32[2,512,2048]{2,1,0:T(8,128)} %shard_map.271.key_ref.value_ref, f32[2,512,2048]{2,1,0:T(8,128)} %shard_map.271.key_ref.value_ref, f32[2,128,1024]{2,1,0:T(8,128)S(1)} %copy-done.9), custom_call_target="tpu_custom_call" | custom-call | tf_op jit(solution)/shard_map/pallas_call | solution.py:886
  660.2 12.6 %shard_map.277 = (f32[2,128,1024]{2,1,0:T(8,128)}, f32[8,2,128,128]{3,2,1,0:T(8,128)}, f32[2,2,16,1024]{3,2,1,0:T(8,128)}, f32[2,2,16,1024]{3,2,1,0:T(8,128)}) custom-call(f32[2,128,1024]{2,1,0:T(8,128)} %copy-done.8, f32[2,128,1024]{2,1,0:T(8,128)} %get-tuple-element.54.d_after_ref, f32[2,128,1024]{2,1,0:T(8,128)} %get-tuple-element.47.middle_ref, ...), custom_call_target="tpu_custom_call" | custom-call | tf_op jit(solution)/shard_map/pallas_call | solution.py:1040
  672.8 29.9 %all_to_all.30.d_context_ref = f32[8,2,128,128]{3,2,1,0:T(8,128)} all-to-all(f32[8,2,128,128]{3,2,1,0:T(8,128)} %get-tuple-element.55), channel_id=1, replica_groups=mesh['x'=2,'c'=2,'z'=4,'y'=2] {'z','y'}, dimensions={0} | all-to-all | bytes 2097152 | tf_op jit(solution)/shard_map/all_to_all | solution.py:1625
  702.7 43.4 %shard_map.278 = (f32[8,3,2,128,128]{4,3,2,1,0:T(8,128)}, f32[2,3,16,1024]{3,2,1,0:T(8,128)}, f32[2,3,16,128]{3,2,1,0:T(8,128)}) custom-call(s32[2,8]{1,0:T(2,128)} %order_ref.3, s32[2,8]{1,0:T(2,128)} %parents_ref.3, f32[8,3,2,128,128]{4,3,2,1,0:T(8,128)} %get-tuple-element.45.qkv_ref, f32[8,2,128,128]{3,2,1,0:T(8,128)} %all_to_all.30.d_context_ref, ...), custom_call_target="tpu_custom_call" | custom-call | tf_op jit(solution)/shard_map/pallas_call | solution.py:846
  747.2 15.2 %all_to_all.31 = f32[8,2,3,16,128]{4,3,2,1,0:T(8,128)S(1)} all-to-all(f32[8,2,3,16,128]{4,3,2,1,0:T(8,128)S(1)} %bitcast_bitcast_fusion), channel_id=1, replica_groups=mesh['x'=2,'c'=2,'z'=4,'y'=2] {'z','y'}, dimensions={0} | all-to-all | bytes 786432 | tf_op jit(solution)/shard_map/all_to_all | solution.py:1482
  764.1 31.2 %shard_map.280 = (f32[2,512,1024]{2,1,0:T(8,128)}, f32[2,2,16,1024]{3,2,1,0:T(8,128)}, f32[2,2,16,1024]{3,2,1,0:T(8,128)}) custom-call(f32[2,512,1024]{2,1,0:T(8,128)} %encoder_ref.3, f32[2,512,1024]{2,1,0:T(8,128)} %get-tuple-element.60.d_key_ref, f32[2,512,1024]{2,1,0:T(8,128)} %get-tuple-element.61.d_value_ref, f32[8,4,160,1024]{3,2,1,0:T(8,128)} %bitcast.124, ...), custom_call_target="tpu_custom_call" | custom-call | tf_op jit(solution)/shard_map/pallas_call | solution.py:1163
  797.4 48.1 %all_to_all.32 = f32[8,2,12,16,128]{4,3,2,1,0:T(8,128)S(1)} all-to-all(f32[8,2,12,16,128]{4,3,2,1,0:T(8,128)S(1)} %bitcast.133), channel_id=1, replica_groups=mesh['x'=2,'c'=2,'z'=4,'y'=2] {'z','y'}, dimensions={0} | all-to-all | bytes 3145728 | tf_op jit(solution)/shard_map/all_to_all | solution.py:1482
  847.9 36.6 %all_to_all.33 = f32[4,2,2,16,1024]{4,3,1,2,0:T(8,128)S(1)} all-to-all(f32[4,2,2,16,1024]{4,3,1,2,0:T(8,128)S(1)} %maximum_bitcast_fusion), channel_id=1, replica_groups=mesh['x'=2,'c'=2,'z'=4,'y'=2] {'z'}, dimensions={0} | all-to-all | bytes 2097152 | tf_op jit(solution)/shard_map/all_to_all | solution.py:1482
  899.5 59.1 %collective-permute-done.5 = f32[2,128,1024]{2,1,0:T(8,128)} collective-permute-done((f32[2,128,1024]{2,1,0:T(8,128)}, f32[2,128,1024]{2,1,0:T(8,128)}, u32[]{:S(2)}, u32[]{:S(2)}) %collective-permute-start.5) | collective-permute-done | bytes 1048608 | tf_op jit(solution)/shard_map/ppermute | solution.py:1478
  961.2 20.9 %all-to-all-done.2.d_qkv_ref = f32[8,3,2,128,128]{4,3,2,1,0:T(8,128)} async-done(((f32[8,3,2,128,128]{4,3,2,1,0:T(8,128)}), f32[8,3,2,128,128]{4,3,2,1,0:T(8,128)}, u32[]{:S(2)}, u32[]{:S(2)}) %all-to-all-start.2) | async-done | bytes 3145760 | tf_op jit(solution)/shard_map/all_to_all | solution.py:1680
  982.1 13.7 %shard_map.279 = f32[2,128,1024]{2,1,0:T(8,128)} custom-call(f32[8,3,2,128,128]{4,3,2,1,0:T(8,128)} %all-to-all-done.2.d_qkv_ref, f32[3072,1024]{1,0:T(8,128)} %all-gather.16.cloned.1.call-done.weight_ref, f32[2,128,1024]{2,1,0:T(8,128)} %tokens_ref.5, f32[2,128,1024]{2,1,0:T(8,128)} %get-tuple-element.59.d_middle_ref, f32[3,1024]{1,0:T(4,128)} %gains_ref.11, ...), custom_call_target="tpu_custom_call" | custom-call | tf_op jit(solution)/shard_map/pallas_call | solution.py:1368
  1006.9 29.2 %all-gather.24.cloned.1.call-done = f32[64,2,16,1024]{3,2,1,0:T(8,128)} async-done(((f32[2,2,16,1024]{3,2,1,0:T(8,128)}), f32[64,2,16,1024]{3,2,1,0:T(8,128)}) %all-gather.24.cloned.1.call-update) | async-done | bytes 8388624 | tf_op jit(solution)/shard_map/all_gather | solution.py:1486
  1036.1 9.5 shard_map.282
  1045.6 81.3 %reduce-scatter.2.cloned.1.call-done = f32[2,64,1024]{2,1,0:T(8,128)} async-done(((f32[2,512,1024]{2,1,0:T(8,128)}), f32[2,64,1024]{2,1,0:T(8,128)}) %reduce-scatter.2.cloned.1.call-update) | async-done | bytes 524304 | tf_op jit(solution)/shard_map/reduce_scatter | solution.py:1629
  (172 shorter events, 131.7 us)
Async XLA Ops:
  7.2 261.8 %all-gather.18.cloned.1.call-start = ((), (), s32[]{:S(2)}) async-start(), calls=%async_computation.11 | async-start | bytes 21626880 | tf_op jit(solution)/shard_map/all_gather | solution.py:1541
  11.1 372.5 %all-gather.12.cloned.1.call-start = ((), (), s32[]{:S(2)}) async-start(), calls=%async_computation.7 | async-start | bytes 17825792 | tf_op jit(solution)/shard_map/all_gather | solution.py:1438
  13.5 497.9 %all-gather.14.cloned.1.call-start = ((), (), s32[]{:S(2)}) async-start(), calls=%async_computation.8 | async-start | bytes 17825792 | tf_op jit(solution)/shard_map/all_gather | solution.py:1438
  15.9 945.2 %all-gather.16.cloned.1.call-start = ((), (), s32[]{:S(2)}) async-start(), calls=%async_computation.9 | async-start | bytes 12976128 | tf_op jit(solution)/shard_map/all_gather | solution.py:1549
  18.4 25.9 %collective-permute-start = (f32[1024,128]{1,0:T(8,128)}, f32[1024,128]{1,0:T(8,128)S(1)}, u32[]{:S(2)}, u32[]{:S(2)}) collective-permute-start(f32[1024,128]{1,0:T(8,128)} %get-tuple-element.94), channel_id=1, source_target_pairs={{0,0},{1,3},{2,6},{3,1},{4,4},{5,7},{6,2},{7,5},{8,8},{9,11},{10,1... | collective-permute-start | bytes 1572872 | tf_op jit(solution)/shard_map/ppermute | solution.py:1456
  20.1 33.3 %collective-permute-start.1 = (f32[1024,128]{1,0:T(8,128)}, f32[1024,128]{1,0:T(8,128)S(1)}, u32[]{:S(2)}, u32[]{:S(2)}) collective-permute-start(f32[1024,128]{1,0:T(8,128)} %get-tuple-element.95), channel_id=1, source_target_pairs={{0,1},{1,4},{2,7},{3,2},{4,5},{5,0},{6,3},{7,6},{8,9},{9,12},{10,1... | collective-permute-start | bytes 1572872 | tf_op jit(solution)/shard_map/ppermute | solution.py:1456
  24.9 28.5 %collective-permute-start.2 = (f32[1024,128]{1,0:T(8,128)}, f32[1024,128]{1,0:T(8,128)}, u32[]{:S(2)}, u32[]{:S(2)}) collective-permute-start(f32[1024,128]{1,0:T(8,128)} %get-tuple-element.96), channel_id=1, source_target_pairs={{0,2},{1,5},{2,0},{3,3},{4,6},{5,1},{6,4},{7,7},{8,10},{9,13},{10,... | collective-permute-start | bytes 1572872 | tf_op jit(solution)/shard_map/ppermute | solution.py:1456
  29.3 329.6 %collective-permute-start.4 = (f32[2,128,1024]{2,1,0:T(8,128)S(1)}, f32[2,128,1024]{2,1,0:T(8,128)}, u32[]{:S(2)}, u32[]{:S(2)}) collective-permute-start(f32[2,128,1024]{2,1,0:T(8,128)S(1)} %copy-done.13), channel_id=1, source_target_pairs={{0,1},{1,0},{2,3},{3,2},{4,5},{5,4},{6,7},{7,6},{8,9},{9,8},{10,11... | collective-permute-start | bytes 3145736 | tf_op jit(solution)/shard_map/ppermute | solution.py:1478
  260.9 45.7 %all-to-all-start = ((f32[8,2,128,128]{3,2,1,0:T(8,128)}), f32[8,2,128,128]{3,2,1,0:T(8,128)S(1)}, u32[]{:S(2)}, u32[]{:S(2)}) async-start(f32[8,2,128,128]{3,2,1,0:T(8,128)} %shard_map.269), calls=%async_computation | async-start | bytes 2097152 | tf_op jit(solution)/shard_map/all_to_all | solution.py:1564
  265.7 730.0 %all-gather.22.cloned.1.call-start = ((), (), s32[]{:S(2)}) async-start(), calls=%async_computation.13 | async-start | bytes 3244032 | tf_op jit(solution)/shard_map/all_gather | solution.py:1486
  348.9 25.6 %collective-permute-start.3 = (f32[2,128,1024]{2,1,0:T(8,128)}, f32[2,128,1024]{2,1,0:T(8,128)}, u32[]{:S(2)}, u32[]{:S(2)}) collective-permute-start(f32[2,128,1024]{2,1,0:T(8,128)} %get-tuple-element.49), channel_id=1, source_target_pairs={{0,1},{1,0},{2,3},{3,2},{4,5},{5,4},{6,7},{7,6},{8,9},{9,8},{10,11... | collective-permute-start | bytes 3145736 | tf_op jit(solution)/shard_map/ppermute | solution.py:1478
  590.1 25.3 %collective-permute-start.6 = (f32[2,128,1024]{2,1,0:T(8,128)S(1)}, f32[2,128,1024]{2,1,0:T(8,128)S(1)}, u32[]{:S(2)}, u32[]{:S(2)}) collective-permute-start(f32[2,128,1024]{2,1,0:T(8,128)S(1)} %get-tuple-element.81), channel_id=1, source_target_pairs={{0,1},{1,0},{2,3},{3,2},{4,5},{5,4},{6,7},{7,6},{8,9},{9,8},{10,11... | collective-permute-start | bytes 3145736 | tf_op jit(solution)/shard_map/ppermute | solution.py:1478
  746.0 17.9 %copy-start.29 = (f32[2,1,16,1024]{3,2,1,0:T(8,128)S(1)}, f32[2,1,16,1024]{3,2,1,0:T(8,128)}, u32[]{:S(2)}) copy-start(f32[2,1,16,1024]{3,2,1,0:T(8,128)} %get-tuple-element.65) | copy-start | bytes 393220
  746.1 17.9 %copy-start.28 = (f32[2,1,16,1024]{3,2,1,0:T(8,128)S(1)}, f32[2,1,16,1024]{3,2,1,0:T(8,128)}, u32[]{:S(2)}) copy-start(f32[2,1,16,1024]{3,2,1,0:T(8,128)} %get-tuple-element.68) | copy-start | bytes 393220
  763.8 232.0 %all-gather.20.cloned.1.call-start = ((), (), s32[]{:S(2)}) async-start(), calls=%async_computation.12 | async-start | bytes 6488064 | tf_op jit(solution)/shard_map/all_gather | solution.py:1486
  764.0 31.2 %copy-start.25 = (f32[2,2,16,1024]{3,2,1,0:T(8,128)S(1)}, f32[2,2,16,1024]{3,2,1,0:T(8,128)}, u32[]{:S(2)}) copy-start(f32[2,2,16,1024]{3,2,1,0:T(8,128)} %get-tuple-element.63) | copy-start | bytes 786436
  764.0 32.3 %copy-start.24 = (f32[2,2,16,1024]{3,2,1,0:T(8,128)S(1)}, f32[2,2,16,1024]{3,2,1,0:T(8,128)}, u32[]{:S(2)}) copy-start(f32[2,2,16,1024]{3,2,1,0:T(8,128)} %get-tuple-element.66) | copy-start | bytes 786436
  797.4 49.0 %copy-start.23 = (f32[2,16,4096]{2,1,0:T(8,128)S(1)}, f32[2,16,4096]{2,1,0:T(8,128)}, u32[]{:S(2)}) copy-start(f32[2,16,4096]{2,1,0:T(8,128)} %get-tuple-element.76) | copy-start | bytes 1572868
  846.4 189.7 %all-gather.24.cloned.1.call-start = ((), (), s32[]{:S(2)}) async-start(), calls=%async_computation.14 | async-start | bytes 8650752 | tf_op jit(solution)/shard_map/all_gather | solution.py:1486
  885.3 241.6 %reduce-scatter.2.cloned.1.call-start = ((), (), s32[]{:S(2)}) async-start(), calls=%async_computation.10 | async-start | bytes 4718592 | tf_op jit(solution)/shard_map/reduce_scatter | solution.py:1629
  886.1 96.0 %all-to-all-start.2 = ((f32[8,3,2,128,128]{4,3,2,1,0:T(8,128)}), f32[8,3,2,128,128]{4,3,2,1,0:T(8,128)}, u32[]{:S(2)}, u32[]{:S(2)}) async-start(f32[8,3,2,128,128]{4,3,2,1,0:T(8,128)} %get-tuple-element.58), calls=%async_computation.2 | async-start | bytes 6291456 | tf_op jit(solution)/shard_map/all_to_all | solution.py:1680
  890.7 68.0 %copy-start.14 = (f32[2,128,1024]{2,1,0:T(8,128)S(1)}, f32[2,128,1024]{2,1,0:T(8,128)}, u32[]{:S(2)}) copy-start(f32[2,128,1024]{2,1,0:T(8,128)} %get-tuple-element.48.after_ref) | copy-start | bytes 3145732
  891.8 66.9 %collective-permute-start.5 = (f32[2,128,1024]{2,1,0:T(8,128)}, f32[2,128,1024]{2,1,0:T(8,128)}, u32[]{:S(2)}, u32[]{:S(2)}) collective-permute-start(f32[2,128,1024]{2,1,0:T(8,128)} %slice_bitcast_fusion.2), channel_id=1, source_target_pairs={{0,1},{1,0},{2,3},{3,2},{4,5},{5,4},{6,7},{7,6},{8,9},{9,8},{10,11... | collective-permute-start | bytes 3145736 | tf_op jit(solution)/shard_map/ppermute | solution.py:1478
  1036.1 90.9 %copy-start.1 = (f32[1024,256]{1,0:T(8,128)S(1)}, f32[1024,256]{1,0:T(8,128)}, u32[]{:S(2)}) copy-start(f32[1024,256]{1,0:T(8,128)} %param.31) | copy-start | bytes 3145732
  (26 other events, 162.5 us)
Sparse Core Ops, SparseCore 0:
  11.5 224.0 all-gather.17
  238.3 145.2 all-gather.11
  386.3 125.0 all-gather.13
  514.1 94.0 all-gather.15
  763.9 65.8 all-gather.21
  846.5 105.7 all-gather.19
  955.8 80.1 all-gather.23
  1040.3 86.6 reduce-scatter.1

commit v2 on v1

--- a/solution.py
+++ b/solution.py
@@ -475,12 +475,43 @@
     return pltpu.CompilerParams(vmem_limit_bytes=limit * MIB)
 
 
+def lasting(micros):
+    return pl.CostEstimate(
+        flops=int(micros * 1e9), bytes_accessed=int(micros * 3e6), transcendentals=0
+    )
+
+
 def shaped(*shape):
     return jax.ShapeDtypeStruct(shape, F32)
 
 
 def whole_spec(shape):
     return pl.BlockSpec(shape, lambda *_: (0,) * len(shape))
+
+
+def signal(target):
+    pl.semaphore_signal(
+        pltpu.get_barrier_semaphore(), 1, device_id=target, device_id_type=pl.DeviceIdType.MESH
+    )
+
+
+def greet(z, last, partners, more=0):
+    for partner in partners:
+        signal(partner)
+
+    @pl.when(z > 0)
+    def _():
+        signal({"z": z - 1})
+
+    @pl.when(z < last)
+    def _():
+        signal({"z": z + 1})
+
+    def met():
+        lines = (z > 0).astype(jnp.int32) + (z < last).astype(jnp.int32)
+        pl.semaphore_wait(pltpu.get_barrier_semaphore(), len(partners) + lines + more)
+
+    return met
 
 
 def heads_kernel(
@@ -492,7 +523,9 @@
     normed_ref,
     inner_ref,
     qkv_ref,
+    own_weight_ref,
     rows_ref,
+    blocks_ref,
     w_high,
     w_low,
     out_sem,
@@ -500,12 +533,16 @@
     down_sem,
     across_sem,
     here_sem,
+    block_sem,
+    block_here_sem,
+    keep_sem,
 ):
     z, y = lax.axis_index("z"), lax.axis_index("y")
     last = lax.axis_size("z") - 1
     trees, seg_len, width = tokens_ref.shape
-    lanes = weight_ref.shape[2]
+    lanes = weight_ref.shape[1] // 3
     rank = up_ref.shape[2]
+    slots = rows_ref.shape[0]
 
     def place(level, side):
         return level * 2 + side
@@ -532,28 +569,42 @@
     def arrived(slot):
         move(slot, across_sem, 0, {"y": 1 - y}).wait_recv()
 
-    barrier = pltpu.get_barrier_semaphore()
-    pl.semaphore_signal(barrier, 1, device_id={"y": 1 - y}, device_id_type=pl.DeviceIdType.MESH)
-
-    @pl.when(z > 0)
-    def _():
-        pl.semaphore_signal(
-            barrier, 1, device_id={"z": z - 1}, device_id_type=pl.DeviceIdType.MESH
-        )
-
-    @pl.when(z < last)
-    def _():
-        pl.semaphore_signal(
-            barrier, 1, device_id={"z": z + 1}, device_id_type=pl.DeviceIdType.MESH
-        )
-
     own = place(z, y)
+
+    def block_move(i):
+        block = 3 * own + i
+        target, kind = block % slots, block // slots
+        source = weight_ref.at[:, i * lanes : (i + 1) * lanes]
+
+        def sent():
+            return pltpu.make_async_remote_copy(
+                src_ref=source,
+                dst_ref=blocks_ref.at[kind],
+                send_sem=block_sem.at[i],
+                recv_sem=block_here_sem.at[kind],
+                device_id={"z": target // 2, "y": target % 2},
+                device_id_type=pl.DeviceIdType.MESH,
+            )
+
+        def kept():
+            return pltpu.make_async_copy(source, blocks_ref.at[kind], block_here_sem.at[kind])
+
+        return target, sent, kept
+
+    away = jnp.int32(0)
+    for i in range(3):
+        giver = (slots * i + own) // 3
+        away = away + ((3 * own + i) % slots != own).astype(jnp.int32)
+
+        @pl.when(giver != own)
+        def _(giver=giver):
+            signal({"z": giver // 2, "y": giver % 2})
+
+    met = greet(z, last, [{"y": 1 - y}], away)
     for tree in range(trees):
         normed = layer_norm(tokens_ref[tree], gains_ref[0:1])[0]
         rows_ref[own, tree * seg_len : (tree + 1) * seg_len] = normed
-    pl.semaphore_wait(
-        barrier, 1 + (z > 0).astype(jnp.int32) + (z < last).astype(jnp.int32)
-    )
+    met()
 
     @pl.when(z < last)
     def _():
@@ -564,10 +615,16 @@
         downward(0).start()
 
     across(z, 0).start()
-    for kind in range(3):
-        high, low = split(weight_ref[kind])
-        w_high[:, kind * lanes : (kind + 1) * lanes] = high
-        w_low[:, kind * lanes : (kind + 1) * lanes] = low
+    for i in range(3):
+        target, sent, kept = block_move(i)
+
+        @pl.when(target != own)
+        def _(sent=sent):
+            sent().start()
+
+        @pl.when(target == own)
+        def _(kept=kept):
+            kept().start()
 
     def keep(slot):
         return pltpu.make_async_copy(rows_ref.at[slot], normed_ref.at[slot], out_sem.at[slot])
@@ -590,7 +647,17 @@
                     product[rows, kind * lanes : (kind + 1) * lanes] + term
                 )
 
-    work(own)
+    def keep_blocks():
+        return pltpu.make_async_copy(blocks_ref, own_weight_ref, keep_sem)
+
+    def take_blocks():
+        for kind in range(3):
+            block = blocks_ref.at[kind]
+            pltpu.make_async_copy(block, block, block_here_sem.at[kind]).wait()
+            where = slice(kind * lanes, (kind + 1) * lanes)
+            w_high[:, where], w_low[:, where] = split(block[...])
+        keep_blocks().start()
+
     for hop in range(1, last + 1):
 
         @pl.when(z - hop >= 0)
@@ -613,6 +680,9 @@
 
             across(z + hop, last + hop).start()
 
+        if hop == 1:
+            take_blocks()
+            work(own)
         for step in (-1, 1):
             level = z + step * hop
             before = level - step
@@ -636,6 +706,14 @@
             arrived(place(level, 1 - y))
             work(place(level, 1 - y))
 
+    keep_blocks().wait()
+    for i in range(3):
+        target, sent, _ = block_move(i)
+
+        @pl.when(target != own)
+        def _(sent=sent):
+            sent().wait_send()
+
     across(z, 0).wait_send()
     for hop in range(0, last + 1):
 
@@ -665,21 +743,24 @@
     trees, seg_len, width = tokens.shape
     slots = lax.axis_size(ROWS)
     levels = lax.axis_size("z")
-    lanes = weight.shape[2]
+    lanes = weight.shape[1] // 3
     inner = down.shape[1]
     dma = pltpu.SemaphoreType.DMA
     here = pl.BlockSpec(memory_space=pltpu.VMEM)
+    there = pl.BlockSpec(memory_space=pl.ANY)
     return pl.pallas_call(
         heads_kernel,
         out_shape=[
             shaped(slots, trees * seg_len, width),
             shaped(slots, trees, seg_len, inner),
             shaped(slots, 3, trees, seg_len, lanes),
+            shaped(3, width, lanes),
         ],
-        in_specs=[here] * 5,
-        out_specs=[pl.BlockSpec(memory_space=pl.ANY), here, here],
+        in_specs=[here, here, there, here, here],
+        out_specs=[there, here, here, there],
         scratch_shapes=[
             pltpu.VMEM((slots, trees * seg_len, width), F32),
+            pltpu.VMEM((3, width, lanes), F32),
             pltpu.VMEM((width, 3 * lanes), BF16),
             pltpu.VMEM((width, 3 * lanes), BF16),
             dma((slots,)),
@@ -687,10 +768,14 @@
             dma((levels,)),
             dma((2 * levels - 1,)),
             dma((slots,)),
+            dma((3,)),
+            dma((3,)),
+            dma,
         ],
         compiler_params=pltpu.CompilerParams(
             vmem_limit_bytes=48 * MIB, collective_id=0, has_side_effects=True
         ),
+        cost_estimate=lasting(110),
     )(tokens, gains, weight, down, up)
 
 
@@ -841,7 +926,7 @@
     return pl.BlockSpec((1,) + shape[1:], lambda tree, *_: (tree,) + (0,) * (len(shape) - 1))
 
 
-def self_call(kernel, depth, order, parents, operands, in_specs, out_shape, out_specs):
+def self_call(kernel, depth, order, parents, operands, in_specs, out_shape, out_specs, micros):
     trees, slots = order.shape
     return pl.pallas_call(
         functools.partial(kernel, depth),
@@ -854,6 +939,7 @@
             scratch_shapes=[pltpu.SMEM((slots,), jnp.int32)],
         ),
         compiler_params=vmem(56),
+        cost_estimate=lasting(micros),
     )(order, parents, *operands)
 
 
@@ -890,6 +976,7 @@
         in_specs=[short, keys, values] + [short] * len(rest),
         out_specs=[short] + [keys] * long_outs,
         compiler_params=vmem(48),
+        cost_estimate=lasting(32 if long_outs else 19),
     )(queries, memory, memory, *rest)
 
 
@@ -1047,6 +1134,7 @@
         ],
         out_specs=[whole_spec(out.shape) for out in out_shape],
         compiler_params=vmem(56),
+        cost_estimate=lasting(10),
     )(*operands)
 
 
@@ -1098,6 +1186,7 @@
             pltpu.VMEM((2, trees * count, 2 * rank), BF16),
         ],
         compiler_params=vmem(56),
+        cost_estimate=lasting(22),
     )(encoder, packed, down, up)
 
 
@@ -1188,7 +1277,19 @@
             pltpu.VMEM((2, trees * count, rank), F32),
         ],
         compiler_params=vmem(56),
+        cost_estimate=lasting(31),
     )(encoder, d_keys, d_values, packed, down, up)
+
+
+def nearest(z, last, turn):
+    orders = [
+        sorted((level for level in range(last + 1) if level != own), key=lambda level: abs(level - own))
+        for own in range(last + 1)
+    ]
+    level = orders[0][turn]
+    for own in range(1, last + 1):
+        level = jnp.where(z == own, orders[own][turn], level)
+    return level
 
 
 def feed_forward_kernel(
@@ -1206,6 +1307,8 @@
     g_out_down_ref,
     g_in_down_ref,
     g_out_up_ref,
+    shards_ref,
+    w_in_buf,
     row_high,
     row_low,
     cot_high,
@@ -1216,188 +1319,453 @@
     d_inner_out_t,
     inner_out,
     d_inner_in,
+    own_sem,
+    w_in_sem,
+    line_sem,
+    line_here_sem,
+    plane_sem,
+    plane_here_sem,
+    core_sem,
+    core_here_sem,
 ):
-    trees, rank = in_up_ref.shape[0], in_up_ref.shape[1]
-    step = pl.program_id(0) * pl.num_programs(1) + pl.program_id(1)
-    last = pl.num_programs(0) * pl.num_programs(1) - 1
+    trees, rank = in_up_ref.shape[0], in_up_ref.shape[2]
     spans = tree_rows(trees, rows_ref.shape[0] // trees)
-
-    @pl.when(step == 0)
+    x, c, z = lax.axis_index("x"), lax.axis_index("c"), lax.axis_index("z")
+    last = lax.axis_size("z") - 1
+    block = shards_ref.shape[2]
+    part = block // 2
+    levels = [nearest(z, last, turn) for turn in range(last)]
+
+    def piece(level, plane, core):
+        return shards_ref.at[level, plane, pl.ds(pl.multiple_of(core * part, part), part)]
+
+    def move(source, target, sem, arrival, device):
+        return pltpu.make_async_remote_copy(
+            src_ref=source,
+            dst_ref=target,
+            send_sem=sem,
+            recv_sem=arrival,
+            device_id=device,
+            device_id_type=pl.DeviceIdType.MESH,
+        )
+
+    mine = w_out_ref.at[pl.ds(pl.multiple_of(x * block + c * part, part), part)]
+
+    def own_move(index, target):
+        return move(
+            mine, piece(z, x, c), line_sem.at[index], line_here_sem.at[z], {"z": target}
+        )
+
+    def line_move(turn, target):
+        level = levels[turn]
+        here = piece(level, x, c)
+        return move(here, here, line_sem.at[2 + turn], line_here_sem.at[level], {"z": target})
+
+    def plane_move(turn):
+        here = piece(levels[turn], x, c)
+        return move(here, here, plane_sem.at[turn], plane_here_sem.at[turn], {"x": 1 - x})
+
+    def core_move(turn, kind):
+        here = piece(levels[turn], x if kind == 0 else 1 - x, c)
+        index = 2 * turn + kind
+        return move(here, here, core_sem.at[index], core_here_sem.at[index], {"c": 1 - c})
+
+    def wait_line(turn):
+        line_move(turn, z).wait_recv()
+
+    def passing(turn, action):
+        level = levels[turn]
+
+        @pl.when(jnp.logical_and(level < z, z < last))
+        def _():
+            action(line_move(turn, z + 1))
+
+        @pl.when(jnp.logical_and(level > z, z > 0))
+        def _():
+            action(line_move(turn, z - 1))
+
+    def relay(turn):
+        wait_line(turn)
+        passing(turn, lambda copy: copy.start())
+        plane_move(turn).start()
+        core_move(turn, 0).start()
+
+    def relay_plane(turn):
+        plane_move(turn).wait_recv()
+        core_move(turn, 1).start()
+
+    order = [(-1, 0), (-1, 1), (0, 0), (1, 0), (0, 1), (2, 0), (1, 1), (2, 1)]
+
+    def chosen(step):
+        level, plane = z, x
+        for index, (turn, other) in enumerate(order):
+            hit = step == index
+            level = jnp.where(hit, z if turn < 0 else levels[turn], level)
+            plane = jnp.where(hit, 1 - x if other else x, plane)
+        return level, plane
+
+    def w_in_copy(step):
+        level, plane = chosen(step)
+        columns = pl.ds(pl.multiple_of(plane * block, block), block)
+        slot = lax.rem(step, 2)
+        return pltpu.make_async_copy(
+            w_in_ref.at[level, :, columns], w_in_buf.at[slot], w_in_sem.at[slot]
+        )
+
+    def own_copy(plane):
+        return pltpu.make_async_copy(
+            w_out_ref.at[pl.ds(plane * block, block)], shards_ref.at[z, plane], own_sem.at[plane]
+        )
+
+    met = greet(z, last, [{"x": 1 - x}, {"c": 1 - c}])
+    for plane in range(2):
+        own_copy(plane).start()
+    w_in_copy(0).start()
+    met()
+
+    @pl.when(z < last)
     def _():
-        row_high[...], row_low[...] = split(rows_ref[...])
-        cot_high[...], cot_low[...] = split(cot_ref[...])
-        out_ref[...] = jnp.zeros_like(out_ref)
-        d_rows_ref[...] = jnp.zeros_like(d_rows_ref)
-        inner_out[...] = jnp.zeros_like(inner_out)
-        d_inner_in[...] = jnp.zeros_like(d_inner_in)
+        own_move(0, z + 1).start()
+
+    @pl.when(z > 0)
+    def _():
+        own_move(1, z - 1).start()
+
+    row_high[...], row_low[...] = split(rows_ref[...])
+    cot_high[...], cot_low[...] = split(cot_ref[...])
+    out_ref[...] = jnp.zeros_like(out_ref)
+    d_rows_ref[...] = jnp.zeros_like(d_rows_ref)
+    inner_out[...] = jnp.zeros_like(inner_out)
+    d_inner_in[...] = jnp.zeros_like(d_inner_in)
+    for tree, own in enumerate(spans):
+        rows = (row_high[own], row_low[own])
+        cots = (cot_high[own], cot_low[own])
+        down, up = in_down_ref[tree], out_up_ref[tree]
+        inner_in[own] = jnp.concatenate(split(ADAPT_SCALE * dot2(rows, down, NT)), axis=1)
+        d_inner_out[own] = jnp.concatenate(split(ADAPT_SCALE * dot2(cots, up, NT)), axis=1)
+        inner_in_t[tree] = jnp.concatenate(
+            split(ADAPT_SCALE * (dot(down, rows[0], NT) + dot(down, rows[1], NT))), axis=0
+        )
+        d_inner_out_t[tree] = jnp.concatenate(
+            split(ADAPT_SCALE * (dot(up, cots[0], NT) + dot(up, cots[1], NT))), axis=0
+        )
+    for plane in range(2):
+        own_copy(plane).wait()
+
+    def work(step, carry):
+        level, plane = chosen(step)
+        entry = level * 2 + plane
+
+        @pl.when(step + 1 < len(order))
+        def _():
+            w_in_copy(step + 1).start()
+
+        @pl.when(step == 2)
+        def _():
+            relay(0)
+            core_move(0, 0).wait_recv()
+
+        @pl.when(step == 3)
+        def _():
+            relay(1)
+            relay_plane(0)
+            core_move(1, 0).wait_recv()
+
+        @pl.when(step == 4)
+        def _():
+            core_move(0, 1).wait_recv()
+
+        @pl.when(step == 5)
+        def _():
+            relay(2)
+            relay_plane(1)
+            core_move(2, 0).wait_recv()
+
+        @pl.when(step == 6)
+        def _():
+            core_move(1, 1).wait_recv()
+
+        @pl.when(step == 7)
+        def _():
+            relay_plane(2)
+            core_move(2, 1).wait_recv()
+
+        w_in_copy(step).wait()
+        rows = (row_high[...], row_low[...])
+        cots = (cot_high[...], cot_low[...])
+        w_in = split(w_in_buf[lax.rem(step, 2)])
+        w_out = split(shards_ref[level, plane])
+        in_up = [in_up_ref[tree, entry] for tree in range(trees)]
+        out_down = [out_down_ref[tree, entry] for tree in range(trees)]
+
+        def per_tree(inner, maps):
+            return jnp.concatenate(
+                [
+                    dot(inner[own], jnp.concatenate([maps[tree], maps[tree]], axis=0))
+                    for tree, own in enumerate(spans)
+                ],
+                axis=0,
+            )
+
+        pre_act = dot3(rows, w_in) + per_tree(inner_in, in_up)
+        root = math.sqrt(2.0 / math.pi)
+        squared = pre_act * pre_act
+        bend = jnp.tanh(root * (pre_act + 0.044715 * (squared * pre_act)))
+        hidden = 0.5 * pre_act * (1.0 + bend)
+        slope = 0.5 * (1.0 + bend) + 0.5 * pre_act * (1.0 - bend * bend) * (
+            root * (1.0 + 3 * 0.044715 * squared)
+        )
+        hidden_parts = split(hidden)
+        out_ref[...] += dot3(hidden_parts, w_out)
+        d_hidden = dot3(cots, w_out, NT) + per_tree(d_inner_out, out_down)
+        pre_parts = split(d_hidden * slope)
+        d_rows_ref[...] += dot3(pre_parts, w_in, NT)
+
         for tree, own in enumerate(spans):
-            rows = (row_high[own], row_low[own])
-            cots = (cot_high[own], cot_low[own])
-            down, up = in_down_ref[tree], out_up_ref[tree]
-            inner_in[own] = jnp.concatenate(
-                split(ADAPT_SCALE * dot2(rows, down, NT)), axis=1
+            hidden_own = both(hidden_parts, own)
+            pre_own = both(pre_parts, own)
+            inner_out[own] += dot2(hidden_own, out_down[tree], NT)
+            d_inner_in[own] += dot2(pre_own, in_up[tree], NT)
+            pair = dot(inner_in_t[tree], pre_own[0])
+            g_in_up_ref[tree, entry] = (
+                pair[:rank] + pair[rank:] + dot(inner_in_t[tree, :rank], pre_own[1])
             )
-            d_inner_out[own] = jnp.concatenate(
-                split(ADAPT_SCALE * dot2(cots, up, NT)), axis=1
+            pair = dot(d_inner_out_t[tree], hidden_own[0])
+            g_out_down_ref[tree, entry] = (
+                pair[:rank] + pair[rank:] + dot(d_inner_out_t[tree, :rank], hidden_own[1])
             )
-            inner_in_t[tree] = jnp.concatenate(
-                split(ADAPT_SCALE * (dot(down, rows[0], NT) + dot(down, rows[1], NT))), axis=0
-            )
-            d_inner_out_t[tree] = jnp.concatenate(
-                split(ADAPT_SCALE * (dot(up, cots[0], NT) + dot(up, cots[1], NT))), axis=0
-            )
-
-    rows = (row_high[...], row_low[...])
-    cots = (cot_high[...], cot_low[...])
-    w_in = split(w_in_ref[0])
-    w_out = split(w_out_ref[0])
-
-    def per_tree(inner, maps):
-        return jnp.concatenate(
-            [
-                dot(inner[own], jnp.concatenate([maps[tree], maps[tree]], axis=0))
-                for tree, own in enumerate(spans)
-            ],
-            axis=0,
-        )
-
-    pre_act = dot3(rows, w_in) + per_tree(inner_in, in_up_ref)
-    root = math.sqrt(2.0 / math.pi)
-    squared = pre_act * pre_act
-    bend = jnp.tanh(root * (pre_act + 0.044715 * (squared * pre_act)))
-    hidden = 0.5 * pre_act * (1.0 + bend)
-    slope = 0.5 * (1.0 + bend) + 0.5 * pre_act * (1.0 - bend * bend) * (
-        root * (1.0 + 3 * 0.044715 * squared)
-    )
-    hidden_parts = split(hidden)
-    out_ref[...] += dot3(hidden_parts, w_out)
-    d_hidden = dot3(cots, w_out, NT) + per_tree(d_inner_out, out_down_ref)
-    pre_parts = split(d_hidden * slope)
-    d_rows_ref[...] += dot3(pre_parts, w_in, NT)
+        return carry
+
+    lax.fori_loop(0, len(order), work, 0)
 
     for tree, own in enumerate(spans):
-        hidden_own = both(hidden_parts, own)
-        pre_own = both(pre_parts, own)
-        inner_out[own] += dot2(hidden_own, out_down_ref[tree], NT)
-        d_inner_in[own] += dot2(pre_own, in_up_ref[tree], NT)
-        pair = dot(inner_in_t[tree], pre_own[0])
-        g_in_up_ref[tree] = (
-            pair[:rank] + pair[rank:] + dot(inner_in_t[tree, :rank], pre_own[1])
-        )
-        pair = dot(d_inner_out_t[tree], hidden_own[0])
-        g_out_down_ref[tree] = (
-            pair[:rank] + pair[rank:] + dot(d_inner_out_t[tree, :rank], hidden_own[1])
-        )
-
-    @pl.when(step == last)
+        inner = split(ADAPT_SCALE * inner_out[own])
+        d_inner = split(ADAPT_SCALE * d_inner_in[own])
+        out_ref[own] += dot2(inner, out_up_ref[tree])
+        d_rows_ref[own] += dot2(d_inner, in_down_ref[tree])
+        g_in_down_ref[tree] = dot3(d_inner, (row_high[own], row_low[own]), TN)
+        g_out_up_ref[tree] = dot3(inner, (cot_high[own], cot_low[own]), TN)
+
+    @pl.when(z < last)
     def _():
-        for tree, own in enumerate(spans):
-            inner = split(ADAPT_SCALE * inner_out[own])
-            d_inner = split(ADAPT_SCALE * d_inner_in[own])
-            out_ref[own] += dot2(inner, out_up_ref[tree])
-            d_rows_ref[own] += dot2(d_inner, in_down_ref[tree])
-            g_in_down_ref[tree] = dot3(d_inner, (row_high[own], row_low[own]), TN)
-            g_out_up_ref[tree] = dot3(inner, (cot_high[own], cot_low[own]), TN)
-
-
-def feed_forward(rows, cots, weights, in_up, out_down, in_down, out_up):
+        own_move(0, z + 1).wait_send()
+
+    @pl.when(z > 0)
+    def _():
+        own_move(1, z - 1).wait_send()
+
+    for turn in range(last):
+        passing(turn, lambda copy: copy.wait_send())
+        plane_move(turn).wait_send()
+        core_move(turn, 0).wait_send()
+        core_move(turn, 1).wait_send()
+
+
+def feed_forward(rows, cots, w_in, w_out, in_up, out_down, in_down, out_up):
     count, width = rows.shape
-    w_in, w_out = weights
-    shards, units = w_in.shape[0], w_in.shape[2]
-    trees, rank = in_up.shape[0], in_up.shape[1]
-    block = min(units, 512)
-    steps = units // block
-    columns = pl.BlockSpec(
-        (trees, rank, block), lambda shard, step: (0, 0, shard * steps + step)
-    )
-    maps = [whole_spec(in_down.shape), whole_spec(out_up.shape)]
-    rows_spec = whole_spec((count, width))
+    levels, _, units = w_in.shape
+    block = units // 2
+    trees, entries, rank = in_up.shape[:3]
+    dma = pltpu.SemaphoreType.DMA
+    here = pl.BlockSpec(memory_space=pltpu.VMEM)
+    there = pl.BlockSpec(memory_space=pl.ANY)
     return pl.pallas_call(
         feed_forward_kernel,
         out_shape=[shaped(count, width)] * 2
         + [shaped(*in_up.shape), shaped(*out_down.shape)]
         + [shaped(*in_down.shape), shaped(*out_up.shape)],
-        grid=(shards, steps),
-        in_specs=[
-            rows_spec,
-            rows_spec,
-            pl.BlockSpec((1, width, block), lambda shard, step: (shard, 0, step)),
-            pl.BlockSpec((1, block, width), lambda shard, step: (shard, step, 0)),
-            columns,
-            columns,
+        in_specs=[here, here, there, there] + [here] * 4,
+        out_specs=[here] * 6,
+        scratch_shapes=[
+            pltpu.VMEM((levels, 2, block, width), F32),
+            pltpu.VMEM((2, width, block), F32),
         ]
-        + maps,
-        out_specs=[rows_spec, rows_spec, columns, columns] + maps,
-        scratch_shapes=[pltpu.VMEM((count, width), BF16)] * 4
+        + [pltpu.VMEM((count, width), BF16)] * 4
         + [pltpu.VMEM((count, 2 * rank), BF16)] * 2
         + [pltpu.VMEM((trees, 2 * rank, count // trees), BF16)] * 2
-        + [pltpu.VMEM((count, rank), F32)] * 2,
-        compiler_params=vmem(56),
+        + [pltpu.VMEM((count, rank), F32)] * 2
+        + [
+            dma((2,)),
+            dma((2,)),
+            dma((levels + 1,)),
+            dma((levels,)),
+            dma((levels - 1,)),
+            dma((levels - 1,)),
+            dma((2 * levels - 2,)),
+            dma((2 * levels - 2,)),
+        ],
+        compiler_params=pltpu.CompilerParams(
+            vmem_limit_bytes=60 * MIB, collective_id=2, has_side_effects=True
+        ),
+        cost_estimate=lasting(110),
     )(rows, cots, w_in, w_out, in_up, out_down, in_down, out_up)
 
 
+def by_distance(z, last, turn):
+    orders = [sorted(range(last + 1), key=lambda level: -abs(level - own)) for own in range(last + 1)]
+    level = orders[0][turn]
+    for own in range(1, last + 1):
+        level = jnp.where(z == own, orders[own][turn], level)
+    return level
+
+
 def into_tokens_kernel(
-    d_qkv_ref, weight_ref, tokens_ref, d_middle_ref, gains_ref, down_ref, up_ref, out_ref, total
+    d_qkv_ref,
+    weight_ref,
+    tokens_ref,
+    d_middle_ref,
+    gains_ref,
+    down_ref,
+    up_ref,
+    out_ref,
+    own_ref,
+    sent_ref,
+    across_ref,
+    rising_ref,
+    falling_ref,
+    w_high,
+    w_low,
+    sent_sem,
+    line_sem,
+    across_sem,
+    rising_sem,
+    falling_sem,
 ):
-    slots, trees, seg_len = d_qkv_ref.shape[0], d_qkv_ref.shape[2], d_qkv_ref.shape[3]
-    kind = pl.program_id(0)
-    spans = tree_rows(trees, seg_len)
-
-    @pl.when(kind == 0)
-    def _():
-        total[...] = jnp.zeros_like(total)
-
-    grads = split(joined(d_qkv_ref.at[:, 0]))
-    total[...] += dot3(grads, split(weight_ref[...]))
-    for tree, rows in enumerate(spans):
-        inner = split(ADAPT_SCALE * dot2(both(grads, rows), up_ref[tree, 0], NT))
-        total[rows] += dot2(inner, down_ref[tree, 0])
-
-    @pl.when(kind == pl.num_programs(0) - 1)
-    def _():
-        _, normal, inverse = layer_norm(rows_of(tokens_ref), gains_ref[0:1])
-        grad = rows_of(d_middle_ref) + norm_back(normal, inverse, gains_ref[0:1], total[...])
-        out_ref[...] = grad.reshape(out_ref.shape)
+    z, y = lax.axis_index("z"), lax.axis_index("y")
+    last = lax.axis_size("z") - 1
+    trees, rank = up_ref.shape[0], up_ref.shape[2]
+    seg_len, lanes = d_qkv_ref.shape[3], d_qkv_ref.shape[4]
+    met = greet(z, last, [{"y": 1 - y}])
+    for kind in range(3):
+        where = slice(kind * lanes, (kind + 1) * lanes)
+        w_high[:, where], w_low[:, where] = split(weight_ref[kind])
+    met()
+
+    def partial(level, side, ref):
+        slot = level * 2 + side
+        grads = split(
+            jnp.concatenate(
+                [
+                    jnp.concatenate([d_qkv_ref[slot, kind, tree] for kind in range(3)], axis=1)
+                    for tree in range(trees)
+                ],
+                axis=0,
+            )
+        )
+        total = dot3(grads, (w_high[...], w_low[...]), NT)
+        for tree, rows in enumerate(tree_rows(trees, seg_len)):
+            inner = jnp.concatenate(
+                [
+                    dot2(
+                        both(grads, (rows, slice(kind * lanes, (kind + 1) * lanes))),
+                        up_ref[tree, kind],
+                        NT,
+                    )
+                    for kind in range(3)
+                ],
+                axis=1,
+            )
+            ref[level, rows] = total[rows] + dot2(split(ADAPT_SCALE * inner), down_ref[tree])
+
+    def move(source, target, level, sem, arrival, device):
+        return pltpu.make_async_remote_copy(
+            src_ref=source.at[level],
+            dst_ref=target.at[level],
+            send_sem=sem,
+            recv_sem=arrival.at[level],
+            device_id=device,
+            device_id_type=pl.DeviceIdType.MESH,
+        )
+
+    def across(turn, level):
+        return move(sent_ref, across_ref, level, sent_sem.at[turn], across_sem, {"y": 1 - y})
+
+    def rising(turn, level):
+        return move(own_ref, rising_ref, level, line_sem.at[turn], rising_sem, {"z": z + 1})
+
+    def falling(turn, level):
+        return move(own_ref, falling_ref, level, line_sem.at[turn], falling_sem, {"z": z - 1})
+
+    levels = [by_distance(z, last, turn) for turn in range(last + 1)]
+    for turn, level in enumerate(levels):
+        partial(level, 1 - y, sent_ref)
+        across(turn, level).start()
+    for level in levels:
+        partial(level, y, own_ref)
+    for turn, level in enumerate(levels):
+        across(turn, level).wait_recv()
+        own_ref[level] += across_ref[level]
+
+        @pl.when(jnp.logical_and(level >= z, z > 0))
+        def _(level=level):
+            rising(0, level).wait_recv()
+            own_ref[level] += rising_ref[level]
+
+        @pl.when(jnp.logical_and(level <= z, z < last))
+        def _(level=level):
+            falling(0, level).wait_recv()
+            own_ref[level] += falling_ref[level]
+
+        @pl.when(level > z)
+        def _(turn=turn, level=level):
+            rising(turn, level).start()
+
+        @pl.when(level < z)
+        def _(turn=turn, level=level):
+            falling(turn, level).start()
+
+    _, normal, inverse = layer_norm(rows_of(tokens_ref), gains_ref[0:1])
+    grad = rows_of(d_middle_ref) + norm_back(normal, inverse, gains_ref[0:1], own_ref[z])
+    out_ref[...] = grad.reshape(out_ref.shape)
+    for turn, level in enumerate(levels):
+        across(turn, level).wait_send()
+
+        @pl.when(level > z)
+        def _(turn=turn, level=level):
+            rising(turn, level).wait_send()
+
+        @pl.when(level < z)
+        def _(turn=turn, level=level):
+            falling(turn, level).wait_send()
 
 
 def into_tokens_call(d_qkv, weight, tokens, d_middle, gains, down, up):
-    slots, kinds, trees, seg_len, lanes = d_qkv.shape
-    width = tokens.shape[2]
-    rank = up.shape[2]
-    one = pl.BlockSpec((trees, 1, rank, width), lambda kind: (0, kind, 0, 0))
+    trees, seg_len, width = tokens.shape
+    levels = lax.axis_size("z")
+    lanes = weight.shape[2]
+    dma = pltpu.SemaphoreType.DMA((levels,))
+    here = pl.BlockSpec(memory_space=pltpu.VMEM)
     return pl.pallas_call(
         into_tokens_kernel,
         out_shape=shaped(*tokens.shape),
-        grid=(kinds,),
-        in_specs=[
-            pl.BlockSpec((slots, 1, trees, seg_len, lanes), lambda kind: (0, kind, 0, 0, 0)),
-            pl.BlockSpec((width, width), lambda kind: (kind, 0)),
-            whole_spec(tokens.shape),
-            whole_spec(tokens.shape),
-            whole_spec(gains.shape),
-            one,
-            one,
-        ],
-        out_specs=whole_spec(tokens.shape),
-        scratch_shapes=[pltpu.VMEM((trees * seg_len, width), F32)],
-        compiler_params=vmem(56),
+        in_specs=[here] * 7,
+        out_specs=here,
+        scratch_shapes=[pltpu.VMEM((levels, trees * seg_len, width), F32)] * 5
+        + [pltpu.VMEM((width, 3 * lanes), BF16)] * 2
+        + [dma] * 5,
+        compiler_params=pltpu.CompilerParams(
+            vmem_limit_bytes=56 * MIB, collective_id=1, has_side_effects=True
+        ),
+        cost_estimate=lasting(110),
     )(d_qkv, weight, tokens, d_middle, gains, down, up)
 
 
-def place_kernel(source_ref, early_ref, late_ref, down_ref, up_ref, in_down_ref, out_up_ref):
-    owners = early_ref.shape[1]
-    late_count = late_ref.shape[3] // 2
-    early_count = early_ref.shape[3] // 2 - 1
-    for owner in range(owners):
-        lanes = slice(owner * late_ref.shape[5], (owner + 1) * late_ref.shape[5])
-        for entry in range(late_count):
-            down_ref[0, entry, :, lanes] = late_ref[0, owner, 0, entry]
-            up_ref[0, entry, :, lanes] = late_ref[0, owner, 0, late_count + entry]
-        for entry in range(early_count):
-            down_ref[0, late_count + entry, :, lanes] = early_ref[0, owner, 0, entry]
-            up_ref[0, late_count + entry, :, lanes] = early_ref[0, owner, 0, early_count + entry]
-        in_down_ref[0, :, lanes] = early_ref[0, owner, 0, 2 * early_count]
-        out_up_ref[0, :, lanes] = early_ref[0, owner, 0, 2 * early_count + 1]
+LATE_DOWN, LATE_UP = (0, 1, 2, 5, 6), (5, 6)
+OWN_UP = (0, 1, 2)
+EARLY = (3, 4, 7)
+
+
+def place_kernel(source_ref, parts_ref, down_ref, up_ref, in_down_ref, out_up_ref):
+    places = [(down_ref, entry) for entry in LATE_DOWN] + [(up_ref, entry) for entry in LATE_UP]
+    places += [(up_ref, entry) for entry in OWN_UP]
+    places += [(down_ref, entry) for entry in EARLY] + [(up_ref, entry) for entry in EARLY]
+    span = parts_ref.shape[5]
+    for owner in range(parts_ref.shape[1]):
+        lanes = slice(owner * span, (owner + 1) * span)
+        for part, (ref, entry) in enumerate(places):
+            ref[0, entry, :, lanes] = parts_ref[0, owner, 0, part]
+        in_down_ref[0, :, lanes] = parts_ref[0, owner, 0, len(places)]
+        out_up_ref[0, :, lanes] = parts_ref[0, owner, 0, len(places) + 1]
 
 
 def place_hidden_kernel(source_ref, parts_ref, in_up_ref, out_down_ref):
@@ -1426,6 +1794,7 @@
             out_specs=[tree_spec(out.shape) for out in out_shape],
         ),
         compiler_params=vmem(48),
+        cost_estimate=lasting(9),
     )(source, *arrays)
 
 
@@ -1444,32 +1813,6 @@
         [
             lax.dynamic_index_in_dim(table, adapter_pick[tree], 0, keepdims=False)
             for tree in range(adapter_pick.shape[0])
-        ]
-    )
-
-
-def own_heads(w_qkv):
-    slots = lax.axis_size(ROWS)
-    lanes = w_qkv.shape[1] // 3
-    me = lax.axis_index(ROWS)
-    blocks = [
-        lax.ppermute(
-            w_qkv[:, i * lanes : (i + 1) * lanes],
-            ROWS,
-            [(s, (3 * s + i) % slots) for s in range(slots)],
-        )
-        for i in range(3)
-    ]
-    kinds = [0] * (3 * slots)
-    for s in range(slots):
-        for i in range(3):
-            kinds[(3 * s + i) % slots * 3 + (3 * s + i) // slots] = i
-    stacked = jnp.stack(blocks)
-    table = jnp.array(kinds, jnp.int32)
-    return jnp.stack(
-        [
-            lax.dynamic_index_in_dim(stacked, table[me * 3 + kind], 0, keepdims=False)
-            for kind in range(3)
         ]
     )
 
@@ -1528,9 +1871,8 @@
         picked = pick(table, adapter_pick).reshape(
             trees, rank, slots // pairs, pairs, hidden_units // slots
         )
-        return lax.dynamic_index_in_dim(picked, my_y, 3, keepdims=False).reshape(
-            trees, rank, hidden_units // pairs
-        )
+        half = lax.dynamic_index_in_dim(picked, my_y, 3, keepdims=False)
+        return half.reshape(trees, rank, slots, -1).swapaxes(1, 2)
 
     in_up = half_columns(fc_in_up)
     out_down = half_columns(fc_out_down.swapaxes(1, 2))
@@ -1545,11 +1887,9 @@
     cross_out_spec = packed_spec(packed, 3 * row, row)
     cross_q_spec = packed_spec(packed, 4 * row, row)
     fc_in_half = gather_pair_half(w_fc_in)
-    fc_out_half = gather_pair_half(w_fc_out)
-    qkv_rows = lax.all_gather(my_quarter(w_qkv.T), EVERY, axis=0, tiled=True)
-
-    normed_all, inner_all, qkv = heads_call(
-        tokens, norm_gains, own_heads(w_qkv), down_qkv, up_own
+
+    normed_all, inner_all, qkv, qkv_own = heads_call(
+        tokens, norm_gains, w_qkv, down_qkv, up_own
     )
     own_context = self_call(
         self_forward_kernel,
@@ -1560,6 +1900,7 @@
         [slots_spec(qkv.shape)],
         shaped(slots, trees, seg_len, lanes),
         slots_spec((slots, trees, seg_len, lanes)),
+        20,
     )
     context = lax.all_to_all(own_context, ROWS, split_axis=0, concat_axis=0, tiled=True)
 
@@ -1584,7 +1925,8 @@
     out_part, d_rows_part, g_in_up, g_out_down, g_in_down, g_out_up = feed_forward(
         with_partner(normed_three),
         with_partner(cotangent),
-        (fc_in_half, fc_out_half),
+        fc_in_half,
+        w_fc_out,
         in_up,
         out_down,
         in_down,
@@ -1593,7 +1935,8 @@
     d_rows_part = d_rows_part.reshape(trees, 2, seg_len, width)
     out_part = out_part.reshape(trees, 2, seg_len, width)
     d_rows_other = swap(d_rows_part[:, 1])
-    layer_out = after_cross + out_part[:, 0] + swap(out_part[:, 1])
+    out_other, d_rows_other = lax.optimization_barrier((out_part[:, 1], d_rows_other))
+    out_other = swap(out_other)
 
     pair_maps = [shaped(trees, 1, rank, width)] * 2
     d_after, d_cross_ctx, g_down_seven, g_up_seven = rows_call(
@@ -1615,6 +1958,8 @@
     d_cross_q, d_cross_k, d_cross_v = cross_call(
         cross_backward_kernel, cross_queries, memory, (d_cross_ctx,), 2
     )
+    out_other, d_cross_q = lax.optimization_barrier((out_other, d_cross_q))
+    layer_out = after_cross + out_part[:, 0] + out_other
     d_middle, d_context, g_down_mid, g_up_mid = rows_call(
         into_self_kernel,
         (d_cross_q, d_after, middle, context, norm_gains, packed, packed, down, up),
@@ -1623,32 +1968,40 @@
         + [shaped(trees, 2, rank, width)] * 2,
     )
     d_own_context = lax.all_to_all(d_context, ROWS, split_axis=0, concat_axis=0, tiled=True)
+    d_context, d_cross_k = lax.optimization_barrier((d_context, d_cross_k))
     d_encoder, g_down_memory, g_up_memory = memory_back_call(
         encoder, d_cross_k, d_cross_v, packed, down, up
     )
-    grad_encoder = lax.psum_scatter(d_encoder, ROWS, scatter_dimension=1, tiled=True)
+    enc_rows = encoder.shape[1] // slots
+    sides = d_encoder.reshape(trees, slots // pairs, pairs, enc_rows, width).transpose(2, 1, 0, 3, 4)
+    other_side = lax.dynamic_index_in_dim(sides, 1 - my_y, 0, keepdims=False)
+    own_side = lax.dynamic_index_in_dim(sides, my_y, 0, keepdims=False)
+    enc_side = own_side + swap(other_side)
 
     def columns(parts):
         stack = jnp.concatenate(parts, axis=1)
         return stack.reshape(stack.shape[:3] + (slots, lanes)).transpose(3, 0, 1, 2, 4)
 
     hidden_parts = jnp.stack([g_in_up, g_out_down], axis=1).reshape(
-        trees, 2, rank, slots // pairs, hidden_units // slots
-    )
-    hidden_all = to_everyone(summed_to_owner(hidden_parts.transpose(3, 0, 1, 2, 4), "z"))
-    early = columns(
-        [
-            g_down_mid,
-            g_down_memory,
-            g_down_seven,
-            g_up_mid,
-            g_up_memory,
-            g_up_seven,
-            g_in_down[:, None],
-            g_out_up[:, None],
-        ]
-    )
-    early_all = to_everyone(summed_to_owner(early, ROWS))
+        trees, 2, slots // pairs, 2, rank, -1
+    )
+    hidden_parts = hidden_parts.transpose(2, 0, 1, 4, 3, 5).reshape(
+        slots // pairs, trees, 2, rank, hidden_units // slots
+    )
+    hidden_all = to_everyone(summed_to_owner(hidden_parts, "z"))
+    early = summed_to_owner(
+        columns(
+            [
+                g_down_mid,
+                g_down_seven,
+                g_up_mid,
+                g_up_seven,
+                g_in_down[:, None],
+                g_out_up[:, None],
+            ]
+        ),
+        ROWS,
+    )
 
     normed_shape = (slots, trees, seg_len, width)
     d_qkv, g_down_part, g_up_qkv = self_call(
@@ -1674,12 +2027,14 @@
             tree_spec((trees, 3, rank, width)),
             tree_spec((trees, 3, rank, lanes)),
         ],
-    )
-    g_down_qkv = summed_to_owner(columns([g_down_part]), ROWS)
-    late_all = to_everyone(jnp.concatenate([g_down_qkv, g_up_qkv], axis=1))
-    d_split = lax.all_to_all(d_qkv, ROWS, split_axis=0, concat_axis=0, tiled=True)
+        43,
+    )
+    enc_side, g_down_part = lax.optimization_barrier((enc_side, g_down_part))
+    late = summed_to_owner(columns([g_down_part, g_down_memory, g_up_memory]), ROWS)
+    grad_encoder = summed_to_owner(enc_side, "z")
+    attention_all = to_everyone(jnp.concatenate([late, g_up_qkv, early], axis=1))
     grad_tokens = into_tokens_call(
-        d_split, qkv_rows, tokens, d_middle, norm_gains, down, up
+        d_qkv, qkv_own, tokens, d_middle, norm_gains, down_qkv, up_own
     )
 
     all_picks = lax.all_gather(adapter_pick, COPIES, axis=0, tiled=True)
@@ -1689,7 +2044,7 @@
     wide = shaped(adapters, projections, rank, width)
     narrow = shaped(adapters, rank, width)
     grad_down, grad_up, grad_in_down, grad_out_up = place_call(
-        place_kernel, source, (early_all, late_all), [wide, wide, narrow, narrow]
+        place_kernel, source, (attention_all,), [wide, wide, narrow, narrow]
     )
     grad_in_up, grad_out_down = place_call(
         place_hidden_kernel, source, (hidden_all,), [shaped(adapters, rank, hidden_units)] * 2

time: 1140 us -> 975 us (0.86)
  waiting for transfers between devices: 386 us -> 111 us
  Pallas kernels: 503 us -> 731 us
  blocking collectives: 134 us -> 7.64 us
    all_gather x2 -> x1, waiting for transfers between devices: 134 us -> 0.01 us  [gather_pair_half(): lax.all_gather(my_quarter(shard), ('z',) + COPIES, axis=0, tiled=True)]
    pallas_call x1, Pallas kernels: 13.7 us -> 146 us  [into_tokens_call(): pl.pallas_call(into_tokens_kernel, out_shape=shaped(*tokens.shape), in_sp...]
    all_to_all x4 -> x0, blocking collectives: 130 us -> none  [the longest x3 99.9 us: summed_to_owner(): lax.all_to_all(parts, axes, split_axis=0, concat_axis=0, tiled=True)]
    reduce_scatter x1 -> x0, waiting for transfers between devices: 81.3 us -> none  [by_heads(): lax.psum_scatter(d_encoder, ROWS, scatter_dimension=1, tiled=True)]
    ppermute x4 -> x5, waiting for transfers between devices: 95.7 us -> 16.8 us  [swap(): return lax.ppermute(array, 'y', SWAP)]
    pallas_call x1, Pallas kernels: 75.9 us -> 124 us  [feed_forward(): pl.pallas_call(feed_forward_kernel, out_shape=[shaped(count, width)] * 2...]
    pallas_call x1, Pallas kernels: 184 us -> 231 us  [heads_call(): pl.pallas_call(heads_kernel, out_shape=[shaped(slots, trees * seg_len, wi...]
    all_to_all x1, waiting for transfers between devices: 15.2 us -> 52.5 us  [by_heads(): lax.all_to_all(own_context, ROWS, split_axis=0, concat_axis=0, tiled=True)]
  transfers between devices with their start and end apart: 17 -> 15, of which waited for: 10 -> 5; matrix products, arithmetic and copies ran while one was open for 4% -> 4% of each run, Pallas kernels for 44% -> 62%
where the time goes in v2:
time: 975 us; the launch traced here: 964 us
  Pallas kernels  731 us (75%)
  waiting for transfers between devices  111 us (11%)
  local copies, waits for them, and re-layouts  44 us (5%)
  starting transfers between devices  36 us (4%)
  between operations  19.4 us (2%)
  other arithmetic  15.8 us (2%)
    pallas_call x1, Pallas kernels, heads_call(): pl.pallas_call(heads_kernel, out_shape=[shaped(slots, trees * seg_len, wi...  231 us
    pallas_call x1, Pallas kernels, into_tokens_call(): pl.pallas_call(into_tokens_kernel, out_shape=shaped(*tokens.shape), in_sp...  146 us
    pallas_call x1, Pallas kernels, feed_forward(): pl.pallas_call(feed_forward_kernel, out_shape=[shaped(count, width)] * 2...  124 us
    pallas_call x2, Pallas kernels, self_call(): pl.pallas_call(functools.partial(kernel, depth), out_shape=out_shape, gri...  63.7 us
    all_to_all x1, waiting for transfers between devices, by_heads(): lax.all_to_all(own_context, ROWS, split_axis=0, concat_axis=0, tiled=True)  52.5 us
    pallas_call x2, Pallas kernels, cross_call(): pl.pallas_call(kernel, out_shape=[shaped(trees, seg_len, width)] + [shape...  51.8 us
    all_to_all x4, waiting for transfers between devices, summed_to_owner(): lax.all_to_all(parts, axes, split_axis=0, concat_axis=0, tiled=True)  41.2 us
    pallas_call x4, Pallas kernels, rows_call(): pl.pallas_call(kernel, out_shape=out_shape, grid=(1,), in_specs=[whole_sp...  40.8 us
  transfers between devices with their start and end apart: 15, of which 5 were waited for; matrix products, arithmetic and copies ran while one was open for 4% of the time, Pallas kernels for 62%

profile of v2, /device:TPU:0, one launch (start us, length us, event | category | flops | bytes accessed | tf_op | source)
XLA Modules:
  0.0 964.4 jit_solution(11815486926200824959)
XLA Ops:
  24.0 230.8 %shard_map.259 = (f32[8,256,1024]{2,1,0:T(8,128)}, f32[8,2,128,48]{3,2,1,0:T(8,128)S(1)}, f32[8,3,2,128,128]{4,3,2,1,0:T(8,128)}, f32[3,1024,128]{2,1,0:T(8,128)S(1)}) custom-call(f32[2,128,1024]{2,1,0:T(8,128)S(1)} %copy-done.2, f32[3,1024]{1,0:T(4,128)S(1)} %copy-done.5, f32[1024,384]{1,0:T(8,128)S(1)} %copy-done.7, bf16[2,48,1024]{2,1,0:T(8,128)(2,1)S(1)} %bitcast.116, ...), custom_call_target="tpu_custom_call" | custom-call | flops 109999996928 | bytes 330000000 | tf_op jit(solution)/shard_map/pallas_call | solution.py:751
  257.0 20.3 %shard_map.260 = f32[8,2,128,128]{3,2,1,0:T(8,128)} custom-call(s32[2,8]{1,0:T(2,128)} %order_ref.3, s32[2,8]{1,0:T(2,128)} %parents_ref.3, f32[8,3,2,128,128]{4,3,2,1,0:T(8,128)} %get-tuple-element.53.qkv_ref), custom_call_target="tpu_custom_call" | custom-call | flops 20000000000 | bytes 60000000 | tf_op jit(solution)/shard_map/pallas_call | solution.py:931
  285.0 52.5 %all-to-all-done.context_ref = f32[8,2,128,128]{3,2,1,0:T(8,128)S(1)} async-done(((f32[8,2,128,128]{3,2,1,0:T(8,128)}), f32[8,2,128,128]{3,2,1,0:T(8,128)S(1)}, u32[]{:S(2)}, u32[]{:S(2)}) %all-to-all-start) | async-done | bytes 1048608 | tf_op jit(solution)/shard_map/all_to_all | solution.py:1905
  338.5 11.2 %shard_map.261 = (f32[2,128,1024]{2,1,0:T(8,128)}, f32[2,128,1024]{2,1,0:T(8,128)}) custom-call(f32[8,2,128,128]{3,2,1,0:T(8,128)} %copy-done.13, f32[2,128,1024]{2,1,0:T(8,128)} %tokens_ref.5, f32[3,1024]{1,0:T(4,128)} %gains_ref.11, f32[8,4,160,1024]{3,2,1,0:T(8,128)} %bitcast.118, f32[8,4,160,1024]{3,2,1,0:T(8,128)} %bitcast.119, ...), custom_call_target="tpu_custom_call" | custom-call | flops 10000000000 | bytes 30000000 | tf_op jit(solution)/shard_map/pallas_call | solution.py:1127
  349.7 22.5 %shard_map.262.key_ref.value_ref = f32[2,512,2048]{2,1,0:T(8,128)} custom-call(f32[2,512,1024]{2,1,0:T(8,128)} %encoder_ref.3, f32[8,4,160,1024]{3,2,1,0:T(8,128)} %bitcast.120, bf16[2,8,16,1024]{3,2,1,0:T(8,128)(2,1)} %get-tuple-element.119.down_ref, bf16[2,8,16,1024]{3,2,1,0:T(8,128)(2,1)} %get-tuple-element.120.up_ref), custom_call_target="tpu_custom_call" | custom-call | flops 22000001024 | bytes 66000000 | tf_op jit(solution)/shard_map/pallas_call | solution.py:1172
  372.1 19.0 %shard_map.263.context_ref = f32[2,128,1024]{2,1,0:T(8,128)S(1)} custom-call(f32[2,128,1024]{2,1,0:T(8,128)S(1)} %copy-done.8, f32[2,512,2048]{2,1,0:T(8,128)} %shard_map.262.key_ref.value_ref, f32[2,512,2048]{2,1,0:T(8,128)} %shard_map.262.key_ref.value_ref), custom_call_target="tpu_custom_call" | custom-call | flops 19000000512 | bytes 57000000 | tf_op jit(solution)/shard_map/pallas_call | solution.py:972
  392.1 7.2 shard_map.264
  410.3 11.5 %collective-permute-done = f32[2,128,1024]{2,1,0:T(8,128)} collective-permute-done((f32[2,128,1024]{2,1,0:T(8,128)}, f32[2,128,1024]{2,1,0:T(8,128)}, u32[]{:S(2)}, u32[]{:S(2)}) %collective-permute-start) | collective-permute-done | bytes 1048608 | tf_op jit(solution)/shard_map/ppermute | solution.py:1821
  424.6 124.2 %shard_map.265 = (f32[512,1024]{1,0:T(8,128)}, f32[512,1024]{1,0:T(8,128)}, f32[2,8,16,512]{3,2,1,0:T(8,128)}, f32[2,8,16,512]{3,2,1,0:T(8,128)}, f32[2,16,1024]{2,1,0:T(8,128)}, /*index=5*/f32[2,16,1024]{2,1,0:T(8,128)}) custom-call(f32[512,1024]{1,0:T(8,128)} %bitcast.129, f32[512,1024]{1,0:T(8,128)} %bitcast.128, f32[4,1024,1024]{2,1,0:T(8,128)} %bitcast.149, ...), custom_call_target="tpu_custom_call" | custom-call | flops 109999996928 | bytes 330000000 | tf_op jit(solution)/shard_map/pallas_call | solution.py:1572
  562.6 21.6 %all-to-all-done.5 = f32[4,2,2,16,1024]{4,3,2,1,0:T(8,128)S(1)} async-done(((f32[4,2,2,16,1024]{4,3,2,1,0:T(8,128)}), f32[4,2,2,16,1024]{4,3,2,1,0:T(8,128)S(1)}, u32[]{:S(2)}, u32[]{:S(2)}) %all-to-all-start.5) | async-done | bytes 1048608 | tf_op jit(solution)/shard_map/all_to_all | solution.py:1825
  588.1 8.8 shard_map.266
  598.1 32.7 %shard_map.267 = (f32[2,128,1024]{2,1,0:T(8,128)S(1)}, f32[2,512,1024]{2,1,0:T(8,128)}, f32[2,512,1024]{2,1,0:T(8,128)}) custom-call(f32[2,128,1024]{2,1,0:T(8,128)S(1)} %copy-done.8, f32[2,512,2048]{2,1,0:T(8,128)} %shard_map.262.key_ref.value_ref, f32[2,512,2048]{2,1,0:T(8,128)} %shard_map.262.key_ref.value_ref, f32[2,128,1024]{2,1,0:T(8,128)S(1)} %copy-done.10), custom_call_target="tpu_custom_call" | custom-call | flops 32000000000 | bytes 96000000 | tf_op jit(solution)/shard_map/pallas_call | solution.py:972
  632.6 13.6 %shard_map.268 = (f32[2,128,1024]{2,1,0:T(8,128)}, f32[8,2,128,128]{3,2,1,0:T(8,128)}, f32[2,2,16,1024]{3,2,1,0:T(8,128)}, f32[2,2,16,1024]{3,2,1,0:T(8,128)}) custom-call(f32[2,128,1024]{2,1,0:T(8,128)} %copy-done.3, f32[2,128,1024]{2,1,0:T(8,128)} %get-tuple-element.66.d_after_ref, f32[2,128,1024]{2,1,0:T(8,128)} %get-tuple-element.55.middle_ref, ...), custom_call_target="tpu_custom_call" | custom-call | flops 10000000000 | bytes 30000000 | tf_op jit(solution)/shard_map/pallas_call | solution.py:1127
  646.2 5.1 all-to-all-start.1
  651.3 31.2 %shard_map.271 = (f32[2,512,1024]{2,1,0:T(8,128)}, f32[2,2,16,1024]{3,2,1,0:T(8,128)}, f32[2,2,16,1024]{3,2,1,0:T(8,128)}) custom-call(f32[2,512,1024]{2,1,0:T(8,128)} %encoder_ref.3, f32[2,512,1024]{2,1,0:T(8,128)} %get-tuple-element.74.d_key_ref, f32[2,512,1024]{2,1,0:T(8,128)} %get-tuple-element.75.d_value_ref, f32[8,4,160,1024]{3,2,1,0:T(8,128)} %bitcast.125, ...), custom_call_target="tpu_custom_call" | custom-call | flops 31000000512 | bytes 93000000 | tf_op jit(solution)/shard_map/pallas_call | solution.py:1252
  689.6 4.8 all-to-all-start.4
  694.4 43.3 %shard_map.269 = (f32[8,3,2,128,128]{4,3,2,1,0:T(8,128)}, f32[2,3,16,1024]{3,2,1,0:T(8,128)}, f32[2,3,16,128]{3,2,1,0:T(8,128)}) custom-call(s32[2,8]{1,0:T(2,128)} %order_ref.3, s32[2,8]{1,0:T(2,128)} %parents_ref.3, f32[8,3,2,128,128]{4,3,2,1,0:T(8,128)} %get-tuple-element.53.qkv_ref, f32[8,2,128,128]{3,2,1,0:T(8,128)} %all-to-all-done.1.d_context_ref, ...), custom_call_target="tpu_custom_call" | custom-call | flops 43000000512 | bytes 129000000 | tf_op jit(solution)/shard_map/pallas_call | solution.py:931
  737.7 5.3 collective-permute-done.4
  747.5 5.8 all-to-all-start.3
  753.4 19.6 %all-to-all-done.3 = f32[8,2,7,16,128]{4,3,2,1,0:T(8,128)S(1)} async-done(((f32[8,2,7,16,128]{4,3,2,1,0:T(8,128)}), f32[8,2,7,16,128]{4,3,2,1,0:T(8,128)S(1)}, u32[]{:S(2)}, u32[]{:S(2)}) %all-to-all-start.3) | async-done | bytes 917536 | tf_op jit(solution)/shard_map/all_to_all | solution.py:1825
  775.4 7.6 all-reduce
  789.3 146.3 %shard_map.270 = f32[2,128,1024]{2,1,0:T(8,128)} custom-call(f32[8,3,2,128,128]{4,3,2,1,0:T(8,128)} %get-tuple-element.70.d_qkv_ref, f32[3,1024,128]{2,1,0:T(8,128)} %copy-done.12, f32[2,128,1024]{2,1,0:T(8,128)} %tokens_ref.5, f32[2,128,1024]{2,1,0:T(8,128)} %get-tuple-element.72.d_middle_ref, f32[3,1024]{1,0:T(4,128)} %gains_ref.11, ...), custom_call_target="tpu_custom_call" | custom-call | flops 109999996928 | bytes 330000000 | tf_op jit(solution)/shard_map/pallas_call | solution.py:1738
  936.6 9.5 shard_map.273
  946.1 10.3 %shard_map.272 = (f32[8,8,16,1024]{3,2,1,0:T(8,128)}, f32[8,8,16,1024]{3,2,1,0:T(8,128)}, f32[8,16,1024]{2,1,0:T(8,128)}, f32[8,16,1024]{2,1,0:T(8,128)}) custom-call(s32[8]{0:T(128)S(1)} %select_reduce_fusion.source_ref, f32[4,8,2,18,16,128]{5,4,3,2,1,0:T(8,128)} %bitcast.150), custom_call_target="tpu_custom_call" | custom-call | flops 8999999488 | bytes 27000000 | tf_op jit(solution)/shard_map/pallas_call | solution.py:1787
  (163 shorter events, 80.2 us)
Async XLA Ops:
  7.2 330.3 %all-gather.10.cloned.1.call-start = ((), (), s32[]{:S(2)}) async-start(), calls=%async_computation.7 | async-start | bytes 21626880 | tf_op jit(solution)/shard_map/all_gather | solution.py:1883
  11.1 413.6 %all-gather.8.cloned.1.call-start = ((), (), s32[]{:S(2)}) async-start(), calls=%async_computation.6 | async-start | bytes 17825792 | tf_op jit(solution)/shard_map/all_gather | solution.py:1807
  13.5 393.9 %collective-permute-start.1 = (f32[2,128,1024]{2,1,0:T(8,128)}, f32[2,128,1024]{2,1,0:T(8,128)}, u32[]{:S(2)}, u32[]{:S(2)}) collective-permute-start(f32[2,128,1024]{2,1,0:T(8,128)} %cotangent_ref.1), channel_id=1, source_target_pairs={{0,1},{1,0},{2,3},{3,2},{4,5},{5,4},{6,7},{7,6},{8,9},{9,8},{10,11... | collective-permute-start | bytes 3145736 | tf_op jit(solution)/shard_map/ppermute | solution.py:1821
  22.2 232.7 %copy-start.6 = (bf16[2,3,16,128]{3,2,1,0:T(8,128)(2,1)}, bf16[2,3,16,128]{3,2,1,0:T(8,128)(2,1)S(1)}, u32[]{:S(2)}) copy-start(bf16[2,3,16,128]{3,2,1,0:T(8,128)(2,1)S(1)} %dynamic-slice_maximum_fusion.up_ref) | copy-start | bytes 73732
  24.0 230.9 %copy-start.4 = (bf16[2,3,16,1024]{3,2,1,0:T(8,128)(2,1)}, bf16[2,3,16,1024]{3,2,1,0:T(8,128)(2,1)S(1)}, u32[]{:S(2)}) copy-start(bf16[2,3,16,1024]{3,2,1,0:T(8,128)(2,1)S(1)} %fusion.3) | copy-start | bytes 589828
  277.4 60.1 %all-to-all-start = ((f32[8,2,128,128]{3,2,1,0:T(8,128)}), f32[8,2,128,128]{3,2,1,0:T(8,128)S(1)}, u32[]{:S(2)}, u32[]{:S(2)}) async-start(f32[8,2,128,128]{3,2,1,0:T(8,128)} %shard_map.260), calls=%async_computation | async-start | bytes 2097152 | tf_op jit(solution)/shard_map/all_to_all | solution.py:1905
  399.4 22.4 %collective-permute-start = (f32[2,128,1024]{2,1,0:T(8,128)}, f32[2,128,1024]{2,1,0:T(8,128)}, u32[]{:S(2)}, u32[]{:S(2)}) collective-permute-start(f32[2,128,1024]{2,1,0:T(8,128)} %get-tuple-element.57), channel_id=1, source_target_pairs={{0,1},{1,0},{2,3},{3,2},{4,5},{5,4},{6,7},{7,6},{8,9},{9,8},{10,11... | collective-permute-start | bytes 3145736 | tf_op jit(solution)/shard_map/ppermute | solution.py:1821
  554.2 30.0 %all-to-all-start.5 = ((f32[4,2,2,16,1024]{4,3,2,1,0:T(8,128)}), f32[4,2,2,16,1024]{4,3,2,1,0:T(8,128)S(1)}, u32[]{:S(2)}, u32[]{:S(2)}) async-start(f32[4,2,2,16,1024]{4,3,2,1,0:T(8,128)} %reshape.101), calls=%async_computation.5 | async-start | bytes 2097152 | tf_op jit(solution)/shard_map/all_to_all | solution.py:1825
  557.7 378.8 %all-gather.14.cloned.1.call-start = ((), (), s32[]{:S(2)}) async-start(), calls=%async_computation.9 | async-start | bytes 8650752 | tf_op jit(solution)/shard_map/all_gather | solution.py:1829
  558.2 26.8 %copy-start.30 = (f32[2,16,1024]{2,1,0:T(8,128)S(1)}, f32[2,16,1024]{2,1,0:T(8,128)}, u32[]{:S(2)}) copy-start(f32[2,16,1024]{2,1,0:T(8,128)} %get-tuple-element.87) | copy-start | bytes 393220
  558.2 26.8 %copy-start.29 = (f32[2,16,1024]{2,1,0:T(8,128)S(1)}, f32[2,16,1024]{2,1,0:T(8,128)}, u32[]{:S(2)}) copy-start(f32[2,16,1024]{2,1,0:T(8,128)} %get-tuple-element.88) | copy-start | bytes 393220
  561.0 25.5 %collective-permute-start.2 = (f32[2,128,1024]{2,1,0:T(8,128)S(1)}, f32[2,128,1024]{2,1,0:T(8,128)}, u32[]{:S(2)}, u32[]{:S(2)}) collective-permute-start(f32[2,128,1024]{2,1,0:T(8,128)S(1)} %get-tuple-element.100), channel_id=1, source_target_pairs={{0,1},{1,0},{2,3},{3,2},{4,5},{5,4},{6,7},{7,6},{8,9},{9,8},{10,11... | collective-permute-start | bytes 3145736 | tf_op jit(solution)/shard_map/ppermute | solution.py:1821
  586.4 46.1 %collective-permute-start.3 = (f32[2,128,1024]{2,1,0:T(8,128)S(1)}, f32[2,128,1024]{2,1,0:T(8,128)S(1)}, u32[]{:S(2)}, u32[]{:S(2)}) collective-permute-start(f32[2,128,1024]{2,1,0:T(8,128)S(1)} %slice_bitcast_fusion.2), channel_id=1, source_target_pairs={{0,1},{1,0},{2,3},{3,2},{4,5},{5,4},{6,7},{7,6},{8,9},{9,8},{10,11... | collective-permute-start | bytes 3145736 | tf_op jit(solution)/shard_map/ppermute | solution.py:1821
  598.1 33.7 %copy-start.32 = (f32[2,1,16,1024]{3,2,1,0:T(8,128)S(1)}, f32[2,1,16,1024]{3,2,1,0:T(8,128)}, u32[]{:S(2)}) copy-start(f32[2,1,16,1024]{3,2,1,0:T(8,128)} %get-tuple-element.84) | copy-start | bytes 393220
  598.1 34.4 %copy-start.31 = (f32[2,1,16,1024]{3,2,1,0:T(8,128)S(1)}, f32[2,1,16,1024]{3,2,1,0:T(8,128)}, u32[]{:S(2)}) copy-start(f32[2,1,16,1024]{3,2,1,0:T(8,128)} %get-tuple-element.86) | copy-start | bytes 393220
  646.2 42.5 %all-to-all-start.1 = ((f32[8,2,128,128]{3,2,1,0:T(8,128)}), f32[8,2,128,128]{3,2,1,0:T(8,128)}, u32[]{:S(2)}, u32[]{:S(2)}) async-start(f32[8,2,128,128]{3,2,1,0:T(8,128)} %get-tuple-element.67), calls=%async_computation.1 | async-start | bytes 2097152 | tf_op jit(solution)/shard_map/all_to_all | solution.py:1970
  686.5 56.5 %collective-permute-start.4 = (f32[4,2,64,1024]{3,2,1,0:T(8,128)}, f32[4,2,64,1024]{3,2,1,0:T(8,128)}, u32[]{:S(2)}, u32[]{:S(2)}) collective-permute-start(f32[4,2,64,1024]{3,2,1,0:T(8,128)} %bitcast.113), channel_id=1, source_target_pairs={{0,1},{1,0},{2,3},{3,2},{4,5},{5,4},{6,7},{7,6},{8,9},{9,8},{10,11... | collective-permute-start | bytes 6291464 | tf_op jit(solution)/shard_map/ppermute | solution.py:1821
  689.6 57.9 %all-to-all-start.4 = ((f32[8,2,8,16,128]{4,3,2,1,0:T(8,128)}), f32[8,2,8,16,128]{4,3,2,1,0:T(8,128)S(1)}, u32[]{:S(2)}, u32[]{:S(2)}) async-start(f32[8,2,8,16,128]{4,3,2,1,0:T(8,128)} %bitcast.132), calls=%async_computation.4 | async-start | bytes 2097152 | tf_op jit(solution)/shard_map/all_to_all | solution.py:1825
  747.5 27.7 %copy-start.35 = (s32[2]{0:T(128)S(1)}, s32[2]{0:T(128)}, u32[]{:S(2)}) copy-start(s32[2]{0:T(128)} %param.23) | copy-start | bytes 28
  747.5 35.7 %copy-start.19 = (f32[2,128,1024]{2,1,0:T(8,128)S(1)}, f32[2,128,1024]{2,1,0:T(8,128)}, u32[]{:S(2)}) copy-start(f32[2,128,1024]{2,1,0:T(8,128)} %get-tuple-element.56.after_ref) | copy-start | bytes 3145732
  747.5 25.6 %all-to-all-start.3 = ((f32[8,2,7,16,128]{4,3,2,1,0:T(8,128)}), f32[8,2,7,16,128]{4,3,2,1,0:T(8,128)S(1)}, u32[]{:S(2)}, u32[]{:S(2)}) async-start(f32[8,2,7,16,128]{4,3,2,1,0:T(8,128)} %bitcast_bitcast_fusion), calls=%async_computation.3 | async-start | bytes 1835008 | tf_op jit(solution)/shard_map/all_to_all | solution.py:1825
  753.3 192.8 %all-gather.12.cloned.1.call-start = ((), (), s32[]{:S(2)}) async-start(), calls=%async_computation.8 | async-start | bytes 9732096 | tf_op jit(solution)/shard_map/all_gather | solution.py:1829
  753.4 29.7 %copy-start.21 = (f32[2,128,1024]{2,1,0:T(8,128)S(1)}, f32[2,128,1024]{2,1,0:T(8,128)}, u32[]{:S(2)}) copy-start(f32[2,128,1024]{2,1,0:T(8,128)} %copy-done.20) | copy-start | bytes 3145732
  785.7 149.9 %all-to-all-start.2 = ((f32[4,2,64,1024]{3,2,1,0:T(8,128)}), f32[4,2,64,1024]{3,2,1,0:T(8,128)S(1)}, u32[]{:S(2)}, u32[]{:S(2)}) async-start(f32[4,2,64,1024]{3,2,1,0:T(8,128)} %fusion), calls=%async_computation.2 | async-start | bytes 4194304 | tf_op jit(solution)/shard_map/all_to_all | solution.py:1825
  (28 other events, 199.4 us)
Sparse Core Ops, SparseCore 0:
  11.5 206.4 all-gather.9
  220.1 155.3 all-gather.7
  585.1 85.0 all-gather.13
  774.0 133.5 all-gather.11

commit v3 on v2

--- a/solution.py
+++ b/solution.py
@@ -514,60 +514,74 @@
     return met
 
 
+def remote(source, target, sem, arrival, device):
+    return pltpu.make_async_remote_copy(
+        src_ref=source,
+        dst_ref=target,
+        send_sem=sem,
+        recv_sem=arrival,
+        device_id=device,
+        device_id_type=pl.DeviceIdType.MESH,
+    )
+
+
+def start(copy):
+    copy.start()
+
+
+def wait_send(copy):
+    copy.wait_send()
+
+
 def heads_kernel(
+    order_ref,
+    parents_ref,
     tokens_ref,
     gains_ref,
     weight_ref,
+    shard_ref,
     down_ref,
     up_ref,
     normed_ref,
     inner_ref,
     qkv_ref,
     own_weight_ref,
+    packed_ref,
+    context_ref,
+    own_context_ref,
     rows_ref,
     blocks_ref,
     w_high,
     w_low,
-    out_sem,
-    up_sem,
-    down_sem,
-    across_sem,
-    here_sem,
+    keep_sem,
     block_sem,
     block_here_sem,
-    keep_sem,
+    here_sem,
+    across_sem,
+    over_first_sem,
+    over_second_sem,
+    line_sem,
+    line_first_sem,
+    line_second_sem,
+    shard_here_sem,
+    plane_sem,
+    plane_here_sem,
+    core_sem,
+    core_here_sem,
+    context_sem,
+    context_here_sem,
 ):
+    x, c = lax.axis_index("x"), lax.axis_index("c")
     z, y = lax.axis_index("z"), lax.axis_index("y")
     last = lax.axis_size("z") - 1
     trees, seg_len, width = tokens_ref.shape
     lanes = weight_ref.shape[1] // 3
     rank = up_ref.shape[2]
     slots = rows_ref.shape[0]
+    mine, facing = 2 * x + c, 2 * (1 - x) + c
 
     def place(level, side):
         return level * 2 + side
-
-    def move(slot, sems, index, target):
-        return pltpu.make_async_remote_copy(
-            src_ref=rows_ref.at[slot],
-            dst_ref=rows_ref.at[slot],
-            send_sem=sems.at[index],
-            recv_sem=here_sem.at[slot],
-            device_id=target,
-            device_id_type=pl.DeviceIdType.MESH,
-        )
-
-    def upward(hop):
-        return move(place(z - hop, y), up_sem, hop, {"z": z + 1})
-
-    def downward(hop):
-        return move(place(z + hop, y), down_sem, hop, {"z": z - 1})
-
-    def across(level, index):
-        return move(place(level, y), across_sem, index, {"y": 1 - y})
-
-    def arrived(slot):
-        move(slot, across_sem, 0, {"y": 1 - y}).wait_recv()
 
     own = place(z, y)
 
@@ -577,13 +591,12 @@
         source = weight_ref.at[:, i * lanes : (i + 1) * lanes]
 
         def sent():
-            return pltpu.make_async_remote_copy(
-                src_ref=source,
-                dst_ref=blocks_ref.at[kind],
-                send_sem=block_sem.at[i],
-                recv_sem=block_here_sem.at[kind],
-                device_id={"z": target // 2, "y": target % 2},
-                device_id_type=pl.DeviceIdType.MESH,
+            return remote(
+                source,
+                blocks_ref.at[kind],
+                block_sem.at[i],
+                block_here_sem.at[kind],
+                {"z": target // 2, "y": target % 2},
             )
 
         def kept():
@@ -591,30 +604,72 @@
 
         return target, sent, kept
 
-    away = jnp.int32(0)
-    for i in range(3):
-        giver = (slots * i + own) // 3
-        away = away + ((3 * own + i) % slots != own).astype(jnp.int32)
-
-        @pl.when(giver != own)
-        def _(giver=giver):
-            signal({"z": giver // 2, "y": giver % 2})
-
-    met = greet(z, last, [{"y": 1 - y}], away)
+    half = shard_ref.shape[1] // 2
+
+    def rows_move(slot, sem, device):
+        return remote(rows_ref.at[slot], rows_ref.at[slot], sem, here_sem.at[slot], device)
+
+    def shard_move(part, slot, sem, device):
+        rows = slice(part * half, (part + 1) * half)
+        piece = packed_ref.at[slot, mine, rows]
+        source = shard_ref.at[mine, rows] if slot is own else piece
+        return remote(source, piece, sem, shard_here_sem.at[part, slot], device)
+
+    first = functools.partial(shard_move, 0)
+    second = functools.partial(shard_move, 1)
+
+    def along(move, sems, slot, level, action):
+        @pl.when(jnp.logical_and(level <= z, z < last))
+        def _():
+            action(move(slot, sems.at[0, slot], {"z": z + 1}))
+
+        @pl.when(jnp.logical_and(level >= z, z > 0))
+        def _():
+            action(move(slot, sems.at[1, slot], {"z": z - 1}))
+
+    def over(move, sems, slot, action):
+        action(move(slot, sems.at[slot], {"y": 1 - y}))
+
+    def beside(level):
+        return own if level is z else place(level, y)
+
+    def plane_move(part, slot):
+        piece = packed_ref.at[slot, mine, part * half : (part + 1) * half]
+        return remote(
+            piece, piece, plane_sem.at[part, slot], plane_here_sem.at[part, slot], {"x": 1 - x}
+        )
+
+    def core_move(part, slot, kind):
+        piece = packed_ref.at[slot, facing if kind else mine, part * half : (part + 1) * half]
+        index = 2 * part + kind
+        return remote(
+            piece, piece, core_sem.at[index, slot], core_here_sem.at[index, slot], {"c": 1 - c}
+        )
+
+    def levels_at(hop, action):
+        if hop == 0:
+            action(z)
+            return
+        for level in (z - hop, z + hop):
+
+            @pl.when(jnp.logical_and(level >= 0, level <= last))
+            def _(level=level):
+                action(level)
+
+    def peer(step):
+        target = (own + step) % slots
+        return target, {"z": target // 2, "y": target % 2}
+
+    for step in range(1, slots):
+        signal(peer(step)[1])
+    signal({"x": 1 - x})
+    signal({"c": 1 - c})
     for tree in range(trees):
         normed = layer_norm(tokens_ref[tree], gains_ref[0:1])[0]
         rows_ref[own, tree * seg_len : (tree + 1) * seg_len] = normed
-    met()
-
-    @pl.when(z < last)
-    def _():
-        upward(0).start()
-
-    @pl.when(z > 0)
-    def _():
-        downward(0).start()
-
-    across(z, 0).start()
+    pl.semaphore_wait(pltpu.get_barrier_semaphore(), slots + 1)
+    along(rows_move, line_sem, own, z, start)
+    over(rows_move, across_sem, own, start)
     for i in range(3):
         target, sent, kept = block_move(i)
 
@@ -626,8 +681,30 @@
         def _(kept=kept):
             kept().start()
 
+    def start_shards():
+        over(second, over_second_sem, own, start)
+        along(first, line_first_sem, own, z, start)
+        over(first, over_first_sem, own, start)
+        along(second, line_second_sem, own, z, start)
+
     def keep(slot):
-        return pltpu.make_async_copy(rows_ref.at[slot], normed_ref.at[slot], out_sem.at[slot])
+        return pltpu.make_async_copy(rows_ref.at[slot], normed_ref.at[slot], keep_sem.at[slot])
+
+    def keep_shard():
+        return pltpu.make_async_copy(shard_ref, packed_ref.at[own], keep_sem.at[slots])
+
+    def keep_blocks():
+        return pltpu.make_async_copy(blocks_ref, own_weight_ref, keep_sem.at[slots + 1])
+
+    keep_shard().start()
+
+    def take_blocks():
+        for kind in range(3):
+            block = blocks_ref.at[kind]
+            pltpu.make_async_copy(block, block, block_here_sem.at[kind]).wait()
+            where = slice(kind * lanes, (kind + 1) * lanes)
+            w_high[:, where], w_low[:, where] = split(block[...])
+        keep_blocks().start()
 
     def work(slot):
         keep(slot).start()
@@ -647,65 +724,138 @@
                     product[rows, kind * lanes : (kind + 1) * lanes] + term
                 )
 
-    def keep_blocks():
-        return pltpu.make_async_copy(blocks_ref, own_weight_ref, keep_sem)
-
-    def take_blocks():
-        for kind in range(3):
-            block = blocks_ref.at[kind]
-            pltpu.make_async_copy(block, block, block_here_sem.at[kind]).wait()
-            where = slice(kind * lanes, (kind + 1) * lanes)
-            w_high[:, where], w_low[:, where] = split(block[...])
-        keep_blocks().start()
-
-    for hop in range(1, last + 1):
-
-        @pl.when(z - hop >= 0)
-        def _(hop=hop):
-            arrived(place(z - hop, y))
-
-            @pl.when(z < last)
-            def _():
-                upward(hop).start()
-
-            across(z - hop, hop).start()
-
-        @pl.when(z + hop <= last)
-        def _(hop=hop):
-            arrived(place(z + hop, y))
-
-            @pl.when(z > 0)
-            def _():
-                downward(hop).start()
-
-            across(z + hop, last + hop).start()
-
-        if hop == 1:
-            take_blocks()
-            work(own)
-        for step in (-1, 1):
-            level = z + step * hop
-            before = level - step
-
-            @pl.when(jnp.logical_and(level >= 0, level <= last))
-            def _(level=level):
-                work(place(level, y))
-
-            if hop == 1 and step == 1:
-                continue
-
-            @pl.when(jnp.logical_and(before >= 0, before <= last))
-            def _(before=before):
-                arrived(place(before, 1 - y))
-                work(place(before, 1 - y))
-
-    for level in (z - last, z + last):
-
-        @pl.when(jnp.logical_and(level >= 0, level <= last))
-        def _(level=level):
-            arrived(place(level, 1 - y))
-            work(place(level, 1 - y))
-
+    def arrived(move, slot):
+        move(slot, across_sem.at[0], {"y": 1 - y}).wait_recv()
+
+    def share(part, slot):
+        plane_move(part, slot).start()
+        core_move(part, slot, 0).start()
+
+    def rows_by_line(level):
+        slot = place(level, y)
+        arrived(rows_move, slot)
+        along(rows_move, line_sem, slot, level, start)
+        over(rows_move, across_sem, slot, start)
+
+    def first_by_line(level):
+        slot = place(level, y)
+        arrived(first, slot)
+        along(first, line_first_sem, slot, level, start)
+        over(first, over_first_sem, slot, start)
+        share(0, slot)
+
+    def second_by_line(level):
+        for side in (y, 1 - y):
+            slot = place(level, side)
+            arrived(second, slot)
+            along(second, line_second_sem, slot, level, start)
+            share(1, slot)
+
+    def rows_over(level):
+        slot = place(level, 1 - y)
+        arrived(rows_move, slot)
+        work(slot)
+
+    def first_over(level):
+        slot = place(level, 1 - y)
+        arrived(first, slot)
+        share(0, slot)
+
+    def faced(part, slot):
+        plane_move(part, slot).wait_recv()
+        core_move(part, slot, 1).start()
+
+    def faced_at(hop):
+        def act(level):
+            if level is not z:
+                faced(0, place(level, y))
+                faced(1, place(level, y))
+            faced(1, place(level, 1 - y))
+
+        levels_at(hop, act)
+
+    def attend_tree(tree):
+        def slot_of(segment):
+            found = jnp.int32(0)
+            for slot in range(1, slots):
+                found = jnp.where(order_ref[tree, slot] == segment, slot, found)
+            return found
+
+        def attend_slot(slot, carry):
+            chain = ancestor_slots(order_ref, parents_ref, slot_of, tree, slot)
+            own_context_ref[slot, tree] = attend(
+                qkv_ref[slot, 0, tree] * HD ** (-0.5),
+                jnp.concatenate([qkv_ref[where, 1, tree] for where, _ in chain], axis=0),
+                jnp.concatenate([qkv_ref[where, 2, tree] for where, _ in chain], axis=0),
+                chain_mask(chain, seg_len),
+            )
+            return carry
+
+        lax.fori_loop(0, slots, attend_slot, 0)
+
+    def context_move(step):
+        target, device = peer(step)
+        return remote(
+            own_context_ref.at[target],
+            context_ref.at[own],
+            context_sem.at[step],
+            context_here_sem.at[step],
+            device,
+        )
+
+    def context_keep():
+        return pltpu.make_async_copy(
+            own_context_ref.at[own], context_ref.at[own], context_sem.at[0]
+        )
+
+    other = place(z, 1 - y)
+    levels_at(1, rows_by_line)
+    take_blocks()
+    work(own)
+    levels_at(1, lambda level: work(place(level, y)))
+    levels_at(2, rows_by_line)
+    start_shards()
+    rows_over(z)
+    levels_at(2, lambda level: work(place(level, y)))
+    for hop in range(3, last + 1):
+        levels_at(hop, rows_by_line)
+    levels_at(1, rows_over)
+    arrived(second, other)
+    along(second, line_second_sem, other, z, start)
+    share(1, other)
+    levels_at(1, first_by_line)
+    levels_at(1, second_by_line)
+    for hop in range(3, last + 1):
+        levels_at(hop, lambda level: work(place(level, y)))
+    first_over(z)
+    for hop in range(2, last + 1):
+        levels_at(hop, rows_over)
+    for tree in range(trees):
+        attend_tree(tree)
+        if tree == 0:
+            levels_at(2, first_by_line)
+            levels_at(2, second_by_line)
+            levels_at(1, first_over)
+            faced_at(0)
+    context_keep().start()
+    for step in range(1, slots):
+        context_move(step).start()
+    for hop in range(3, last + 1):
+        levels_at(hop, first_by_line)
+        levels_at(hop, second_by_line)
+    faced_at(1)
+    for hop in range(2, last + 1):
+        levels_at(hop, first_over)
+    for hop in range(2, last + 1):
+        faced_at(hop)
+    for hop in range(last + 1):
+        levels_at(hop, lambda level: faced(0, place(level, 1 - y)))
+
+    context_keep().wait()
+    for step in range(1, slots):
+        context_move(step).wait_send()
+        context_move(step).wait_recv()
+    keep_shard().wait()
     keep_blocks().wait()
     for i in range(3):
         target, sent, _ = block_move(i)
@@ -714,40 +864,42 @@
         def _(sent=sent):
             sent().wait_send()
 
-    across(z, 0).wait_send()
-    for hop in range(0, last + 1):
-
-        @pl.when(jnp.logical_and(z - hop >= 0, z < last))
-        def _(hop=hop):
-            upward(hop).wait_send()
-
-        @pl.when(jnp.logical_and(z + hop <= last, z > 0))
-        def _(hop=hop):
-            downward(hop).wait_send()
-
-        if hop:
-
-            @pl.when(z - hop >= 0)
-            def _(hop=hop):
-                across(z - hop, hop).wait_send()
-
-            @pl.when(z + hop <= last)
-            def _(hop=hop):
-                across(z + hop, last + hop).wait_send()
-
-    for slot in range(normed_ref.shape[0]):
+    def finish(slot):
+        for part in range(2):
+            plane_move(part, slot).wait_send()
+            for kind in range(2):
+                core_move(part, slot, kind).wait_recv()
+                core_move(part, slot, kind).wait_send()
+
+    def sent_on(level):
+        slot = beside(level)
+        along(rows_move, line_sem, slot, level, wait_send)
+        over(rows_move, across_sem, slot, wait_send)
+        along(first, line_first_sem, slot, level, wait_send)
+        over(first, over_first_sem, slot, wait_send)
+        along(second, line_second_sem, slot, level, wait_send)
+        along(second, line_second_sem, place(level, 1 - y), level, wait_send)
+        if level is z:
+            over(second, over_second_sem, own, wait_send)
+        else:
+            finish(slot)
+        finish(place(level, 1 - y))
+
+    for hop in range(last + 1):
+        levels_at(hop, sent_on)
+    for slot in range(slots):
         keep(slot).wait()
 
 
-def heads_call(tokens, gains, weight, down, up):
+def heads_call(order, parents, tokens, gains, weight, shard, down, up):
     trees, seg_len, width = tokens.shape
     slots = lax.axis_size(ROWS)
-    levels = lax.axis_size("z")
     lanes = weight.shape[1] // 3
     inner = down.shape[1]
     dma = pltpu.SemaphoreType.DMA
     here = pl.BlockSpec(memory_space=pltpu.VMEM)
     there = pl.BlockSpec(memory_space=pl.ANY)
+    scalars = pl.BlockSpec(memory_space=pltpu.SMEM)
     return pl.pallas_call(
         heads_kernel,
         out_shape=[
@@ -755,31 +907,33 @@
             shaped(slots, trees, seg_len, inner),
             shaped(slots, 3, trees, seg_len, lanes),
             shaped(3, width, lanes),
+            shaped(slots, *shard.shape),
+            shaped(slots, trees, seg_len, lanes),
         ],
-        in_specs=[here, here, there, here, here],
-        out_specs=[there, here, here, there],
+        in_specs=[scalars, scalars, here, here, there, there, here, here],
+        out_specs=[there, here, here, there, there, there],
         scratch_shapes=[
+            pltpu.VMEM((slots, trees, seg_len, lanes), F32),
             pltpu.VMEM((slots, trees * seg_len, width), F32),
             pltpu.VMEM((3, width, lanes), F32),
             pltpu.VMEM((width, 3 * lanes), BF16),
             pltpu.VMEM((width, 3 * lanes), BF16),
-            dma((slots,)),
-            dma((levels,)),
-            dma((levels,)),
-            dma((2 * levels - 1,)),
-            dma((slots,)),
+            dma((slots + 2,)),
             dma((3,)),
             dma((3,)),
-            dma,
-        ],
+        ]
+        + [dma((slots,))] * 4
+        + [dma((2, slots))] * 6
+        + [dma((4, slots))] * 2
+        + [dma((slots,))] * 2,
         compiler_params=pltpu.CompilerParams(
             vmem_limit_bytes=48 * MIB, collective_id=0, has_side_effects=True
         ),
-        cost_estimate=lasting(110),
-    )(tokens, gains, weight, down, up)
-
-
-def ancestor_slots(order_ref, parents_ref, slot_of, tree, slot, depth):
+        cost_estimate=lasting(180),
+    )(order, parents, tokens, gains, weight, shard, down, up)
+
+
+def ancestor_slots(order_ref, parents_ref, slot_of, tree, slot, depth=4):
     segment = order_ref[tree, slot]
     chain = [(slot, None)]
     there = None
@@ -787,7 +941,7 @@
         parent = parents_ref[tree, segment]
         there = parent >= 0 if there is None else jnp.logical_and(there, parent >= 0)
         segment = jnp.maximum(parent, 0)
-        chain.append((slot_of[segment], there))
+        chain.append((slot_of(segment), there))
     return chain
 
 
@@ -802,69 +956,68 @@
     masks = [(column <= row).astype(jnp.int32)]
     for _, there in chain[1:]:
         masks.append(jnp.full((seg_len, seg_len), there.astype(jnp.int32)))
-    return jnp.concatenate(masks, axis=1) > 0
-
-
-def attend(queries, keys, values, mask):
-    scores = dot3(split(queries), split(keys), NT)
+    mask = jnp.concatenate(masks, axis=1)
+    return jnp.concatenate([mask, mask], axis=0) > 0
+
+
+def stacked_heads(parts):
+    lane = lax.broadcasted_iota(jnp.int32, parts[0].shape, 1)
+    return tuple(
+        jnp.concatenate(
+            [jnp.where(lane < HD, part, 0), jnp.where(lane >= HD, part, 0)], axis=0
+        ).astype(BF16)
+        for part in parts
+    )
+
+
+def beside_heads(stacked):
+    count = stacked.shape[0] // 2
+    lane = lax.broadcasted_iota(jnp.int32, (count, stacked.shape[1]), 1)
+    return jnp.where(lane < HD, stacked[:count], stacked[count:])
+
+
+def by_lanes(left, right):
+    wide = jnp.concatenate(left, axis=1)
+    return dot(wide, jnp.concatenate([right[0], right[0]], axis=1), NT) + dot(
+        left[0], right[1], NT
+    )
+
+
+def by_rows(left, right, dims):
+    width = right[0].shape[1]
+    wide = dot(left[0], jnp.concatenate(right, axis=1), dims)
+    return wide[:, :width] + wide[:, width:] + dot(left[1], right[0], dims)
+
+
+def pair_scores(query_parts, key_parts, mask):
+    scores = by_lanes(query_parts, key_parts)
     if mask is not None:
         scores = jnp.where(mask, scores, MASK_FILL)
-    weights = jnp.exp(scores - jnp.max(scores, -1, keepdims=True))
+    return jnp.exp(scores - jnp.max(scores, -1, keepdims=True))
+
+
+def attend(queries, keys, values, mask=None):
+    weights = pair_scores(stacked_heads(split(queries)), split(keys), mask)
     mass = jnp.sum(weights, -1, keepdims=True)
-    return dot3(split(weights), split(values)) / mass
-
-
-def attend_back(queries, keys, values, d_context, mask):
-    query_parts, key_parts = split(queries), split(keys)
-    value_parts, out_parts = split(values), split(d_context)
-    scores = dot3(query_parts, key_parts, NT)
-    if mask is not None:
-        scores = jnp.where(mask, scores, MASK_FILL)
-    weights = jnp.exp(scores - jnp.max(scores, -1, keepdims=True))
-    weights = weights / jnp.sum(weights, -1, keepdims=True)
-    d_weights = dot3(out_parts, value_parts, NT)
+    return beside_heads(by_rows(split(weights), split(values), NN) / mass)
+
+
+def attend_back(queries, keys, values, d_context, mask=None):
+    query_parts, out_parts = stacked_heads(split(queries)), stacked_heads(split(d_context))
+    key_parts, value_parts = split(keys), split(values)
+    weights = pair_scores(query_parts, key_parts, mask)
+    weights = weights * (1.0 / jnp.sum(weights, -1, keepdims=True))
+    d_weights = by_lanes(out_parts, value_parts)
     shared = jnp.sum(weights * d_weights, -1, keepdims=True)
     score_parts = split(weights * (d_weights - shared))
     return (
-        dot3(score_parts, key_parts) * HD ** (-0.5),
-        dot3(score_parts, query_parts, TN),
-        dot3(split(weights), out_parts, TN),
-    )
-
-
-def by_head(formula, *arrays, mask=None):
-    results = []
-    for head in range(arrays[0].shape[1] // HD):
-        lanes = slice(head * HD, (head + 1) * HD)
-        results.append(formula(*[array[:, lanes] for array in arrays], mask))
-    if isinstance(results[0], tuple):
-        return [jnp.concatenate(parts, axis=1) for parts in zip(*results)]
-    return jnp.concatenate(results, axis=1)
-
-
-def self_forward_kernel(depth, order_ref, parents_ref, qkv_ref, context_ref, slot_of):
-    tree = pl.program_id(0)
-    slots, seg_len = qkv_ref.shape[0], qkv_ref.shape[3]
-    fill_slot_of(order_ref, slot_of, tree, slots)
-
-    def one_slot(slot, carry):
-        chain = ancestor_slots(order_ref, parents_ref, slot_of, tree, slot, depth)
-        keys = jnp.concatenate([qkv_ref[where, 1, 0] for where, _ in chain], axis=0)
-        values = jnp.concatenate([qkv_ref[where, 2, 0] for where, _ in chain], axis=0)
-        context_ref[slot, 0] = by_head(
-            attend,
-            qkv_ref[slot, 0, 0] * HD ** (-0.5),
-            keys,
-            values,
-            mask=chain_mask(chain, seg_len),
-        )
-        return carry
-
-    lax.fori_loop(0, slots, one_slot, 0)
+        beside_heads(by_rows(score_parts, key_parts, NN)) * HD ** (-0.5),
+        by_rows(score_parts, query_parts, TN),
+        by_rows(split(weights), out_parts, TN),
+    )
 
 
 def self_backward_kernel(
-    depth,
     order_ref,
     parents_ref,
     qkv_ref,
@@ -872,6 +1025,8 @@
     normed_ref,
     inner_ref,
     up_ref,
+    _,
+    __,
     d_qkv_ref,
     g_down_ref,
     g_up_ref,
@@ -884,11 +1039,10 @@
     d_qkv_ref[...] = jnp.zeros_like(d_qkv_ref)
 
     def one_slot(slot, carry):
-        chain = ancestor_slots(order_ref, parents_ref, slot_of, tree, slot, depth)
+        chain = ancestor_slots(order_ref, parents_ref, lambda seg: slot_of[seg], tree, slot)
         keys = jnp.concatenate([qkv_ref[where, 1, 0] for where, _ in chain], axis=0)
         values = jnp.concatenate([qkv_ref[where, 2, 0] for where, _ in chain], axis=0)
-        d_queries, d_keys, d_values = by_head(
-            attend_back,
+        d_queries, d_keys, d_values = attend_back(
             qkv_ref[slot, 0, 0] * HD ** (-0.5),
             keys,
             values,
@@ -904,14 +1058,18 @@
 
     lax.fori_loop(0, slots, one_slot, 0)
 
-    normed = split(normed_ref[...].reshape(slots * seg_len, -1))
     inner = split(ADAPT_SCALE * inner_ref[...].reshape(slots * seg_len, 3 * rank))
+    d_inner = []
     for kind in range(3):
         grads = split(d_qkv_ref[:, kind, 0].reshape(slots * seg_len, pair))
         ranks = slice(kind * rank, (kind + 1) * rank)
-        d_inner = split(ADAPT_SCALE * dot2(grads, up_ref[0, kind], NT))
-        g_down_ref[0, kind] = dot3(d_inner, normed, TN)
+        d_inner.append(dot2(grads, up_ref[0, kind], NT))
         g_up_ref[0, kind] = dot3(both(inner, (slice(None), ranks)), grads, TN)
+    high, low = split(ADAPT_SCALE * jnp.concatenate(d_inner, axis=1))
+    rows_high, rows_low = split(normed_ref[...].reshape(slots * seg_len, -1))
+    wide = dot(jnp.concatenate([high, low], axis=1), rows_high, TN)
+    g_down = wide[: 3 * rank] + wide[3 * rank :] + dot(high, rows_low, TN)
+    g_down_ref[0] = g_down.reshape(3, rank, -1)
 
 
 def slots_spec(shape):
@@ -926,10 +1084,10 @@
     return pl.BlockSpec((1,) + shape[1:], lambda tree, *_: (tree,) + (0,) * (len(shape) - 1))
 
 
-def self_call(kernel, depth, order, parents, operands, in_specs, out_shape, out_specs, micros):
+def self_call(kernel, order, parents, operands, in_specs, out_shape, out_specs, micros):
     trees, slots = order.shape
     return pl.pallas_call(
-        functools.partial(kernel, depth),
+        kernel,
         out_shape=out_shape,
         grid_spec=pltpu.PrefetchScalarGridSpec(
             num_scalar_prefetch=2,
@@ -943,28 +1101,33 @@
     )(order, parents, *operands)
 
 
-def cross_forward_kernel(query_ref, key_ref, value_ref, context_ref):
-    context_ref[0] = by_head(
-        attend, query_ref[0] * HD ** (-0.5), key_ref[0], value_ref[0]
-    )
+def head_pairs(ref):
+    return [slice(2 * pair * HD, 2 * (pair + 1) * HD) for pair in range(ref.shape[2] // (2 * HD))]
+
+
+def cross_forward_kernel(query_ref, key_ref, value_ref, _, context_ref):
+    for lanes in head_pairs(query_ref):
+        context_ref[0, :, lanes] = attend(
+            query_ref[0, :, lanes] * HD ** (-0.5), key_ref[0, :, lanes], value_ref[0, :, lanes]
+        )
 
 
 def cross_backward_kernel(
     query_ref, key_ref, value_ref, d_context_ref, d_query_ref, d_key_ref, d_value_ref
 ):
-    d_query_ref[0], d_key_ref[0], d_value_ref[0] = by_head(
-        attend_back,
-        query_ref[0] * HD ** (-0.5),
-        key_ref[0],
-        value_ref[0],
-        d_context_ref[0],
-    )
-
-
-def cross_call(kernel, queries, memory, rest, long_outs):
+    for lanes in head_pairs(query_ref):
+        d_query_ref[0, :, lanes], d_key_ref[0, :, lanes], d_value_ref[0, :, lanes] = attend_back(
+            query_ref[0, :, lanes] * HD ** (-0.5),
+            key_ref[0, :, lanes],
+            value_ref[0, :, lanes],
+            d_context_ref[0, :, lanes],
+        )
+
+
+def cross_call(kernel, queries, memory, rest, long_outs, ahead=()):
     trees, seg_len, width = queries.shape
     enc_rows = memory.shape[1]
-    lanes = 2 * HD
+    lanes = 4 * HD
     steps = width // lanes
     short = pl.BlockSpec((1, seg_len, lanes), lambda tree, step: (tree, 0, step))
     keys = pl.BlockSpec((1, enc_rows, lanes), lambda tree, step: (tree, 0, step))
@@ -973,11 +1136,13 @@
         kernel,
         out_shape=[shaped(trees, seg_len, width)] + [shaped(trees, enc_rows, width)] * long_outs,
         grid=(trees, steps),
-        in_specs=[short, keys, values] + [short] * len(rest),
+        in_specs=[short, keys, values]
+        + [short] * len(rest)
+        + [pl.BlockSpec(memory_space=pl.ANY)] * len(ahead),
         out_specs=[short] + [keys] * long_outs,
         compiler_params=vmem(48),
         cost_estimate=lasting(32 if long_outs else 19),
-    )(queries, memory, memory, *rest)
+    )(queries, memory, memory, *rest, *ahead)
 
 
 def square(ref):
@@ -1052,8 +1217,7 @@
 
 
 def into_cross_kernel(
-    own_ref,
-    other_ref,
+    d_rows_ref,
     after_ref,
     cotangent_ref,
     context_ref,
@@ -1061,23 +1225,72 @@
     out_ref,
     down_ref,
     up_ref,
+    g_in_up_ref,
+    g_out_down_ref,
     d_after_ref,
     d_context_ref,
     g_down_ref,
     g_up_ref,
+    hidden_ref,
+    other_ref,
+    parts_ref,
+    swap_sem,
+    part_sem,
+    part_here_sem,
 ):
     trees = after_ref.shape[0]
+    z, levels = lax.axis_index("z"), lax.axis_size("z")
+    partner = {"y": 1 - lax.axis_index("y")}
+    signal(partner)
+    for step in range(1, levels):
+        signal({"z": (z + step) % levels})
+    pl.semaphore_wait(pltpu.get_barrier_semaphore(), levels)
+    swapped = remote(
+        d_rows_ref.at[:, 1], other_ref, swap_sem.at[0], swap_sem.at[1], partner
+    )
+    swapped.start()
+
+    unit_grads = (g_in_up_ref, g_out_down_ref)
+
+    def part_move(step, which):
+        level = (z + step) % levels
+        return remote(
+            unit_grads[which].at[:, pl.ds(2 * level, 2)],
+            parts_ref.at[step - 1, which],
+            part_sem.at[step - 1, which],
+            part_here_sem.at[step - 1, which],
+            {"z": level},
+        )
+
+    moves = [(step, which) for step in range(1, levels) for which in range(2)]
+    for step, which in moves:
+        part_move(step, which).start()
+    context = split(rows_of(context_ref))
+    weight = split(square(out_ref))
     _, normal, inverse = layer_norm(rows_of(after_ref), gains_ref[2:3])
-    d_normed = rows_of(own_ref) + rows_of(other_ref)
+    for step, which in moves:
+        part_move(step, which).wait_recv()
+    for which in range(2):
+        total = unit_grads[which][:, pl.ds(2 * z, 2)]
+        for step in range(1, levels):
+            total = total + parts_ref[step - 1, which]
+        block = total.shape[3]
+        for plane in range(2):
+            lanes = slice(plane * block, (plane + 1) * block)
+            hidden_ref[:, which, :, lanes] = total[:, plane]
+    own_rows = jnp.concatenate([d_rows_ref[tree, 0] for tree in range(trees)], axis=0)
+    swapped.wait()
+    d_normed = own_rows + rows_of(other_ref)
     d_after = rows_of(cotangent_ref) + norm_back(normal, inverse, gains_ref[2:3], d_normed)
     d_after_ref[...] = d_after.reshape(d_after_ref.shape)
     grads = split(d_after)
-    context = split(rows_of(context_ref))
-    d_context = dot3(grads, split(square(out_ref)), NT)
+    d_context = dot3(grads, weight, NT)
     d_context = d_context + with_adapters_back(
         context, grads, down_ref, up_ref, 7, trees, g_down_ref, g_up_ref, 0
     )
     d_context_ref[...] = d_context.reshape(d_context_ref.shape)
+    for step, which in moves:
+        part_move(step, which).wait_send()
 
 
 def into_self_kernel(
@@ -1123,7 +1336,7 @@
     )
 
 
-def rows_call(kernel, operands, specs, out_shape):
+def rows_call(kernel, operands, specs, out_shape, scratch=(), params=None):
     return pl.pallas_call(
         kernel,
         out_shape=out_shape,
@@ -1133,7 +1346,8 @@
             for operand, spec in zip(operands, specs)
         ],
         out_specs=[whole_spec(out.shape) for out in out_shape],
-        compiler_params=vmem(56),
+        scratch_shapes=scratch,
+        compiler_params=params or vmem(56),
         cost_estimate=lasting(10),
     )(*operands)
 
@@ -1297,6 +1511,8 @@
     cot_ref,
     w_in_ref,
     w_out_ref,
+    below_ref,
+    above_ref,
     in_up_ref,
     out_down_ref,
     in_down_ref,
@@ -1327,6 +1543,7 @@
     plane_here_sem,
     core_sem,
     core_here_sem,
+    near_sem,
 ):
     trees, rank = in_up_ref.shape[0], in_up_ref.shape[2]
     spans = tree_rows(trees, rows_ref.shape[0] // trees)
@@ -1339,39 +1556,36 @@
     def piece(level, plane, core):
         return shards_ref.at[level, plane, pl.ds(pl.multiple_of(core * part, part), part)]
 
-    def move(source, target, sem, arrival, device):
-        return pltpu.make_async_remote_copy(
-            src_ref=source,
-            dst_ref=target,
-            send_sem=sem,
-            recv_sem=arrival,
-            device_id=device,
-            device_id_type=pl.DeviceIdType.MESH,
-        )
-
-    mine = w_out_ref.at[pl.ds(pl.multiple_of(x * block + c * part, part), part)]
-
-    def own_move(index, target):
-        return move(
-            mine, piece(z, x, c), line_sem.at[index], line_here_sem.at[z], {"z": target}
-        )
-
     def line_move(turn, target):
         level = levels[turn]
         here = piece(level, x, c)
-        return move(here, here, line_sem.at[2 + turn], line_here_sem.at[level], {"z": target})
+        return remote(here, here, line_sem.at[turn], line_here_sem.at[level], {"z": target})
 
     def plane_move(turn):
         here = piece(levels[turn], x, c)
-        return move(here, here, plane_sem.at[turn], plane_here_sem.at[turn], {"x": 1 - x})
+        return remote(here, here, plane_sem.at[turn], plane_here_sem.at[turn], {"x": 1 - x})
 
     def core_move(turn, kind):
         here = piece(levels[turn], x if kind == 0 else 1 - x, c)
         index = 2 * turn + kind
-        return move(here, here, core_sem.at[index], core_here_sem.at[index], {"c": 1 - c})
+        return remote(here, here, core_sem.at[index], core_here_sem.at[index], {"c": 1 - c})
+
+    def near_copy(source, level, index):
+        return pltpu.make_async_copy(source, piece(level, x, c), near_sem.at[index])
+
+    def near(action):
+        @pl.when(z > 0)
+        def _():
+            action(near_copy(below_ref, z - 1, 0))
+
+        @pl.when(z < last)
+        def _():
+            action(near_copy(above_ref, z + 1, 1))
 
     def wait_line(turn):
-        line_move(turn, z).wait_recv()
+        @pl.when(jnp.abs(levels[turn] - z) > 1)
+        def _():
+            line_move(turn, z).wait_recv()
 
     def passing(turn, action):
         level = levels[turn]
@@ -1421,15 +1635,10 @@
     for plane in range(2):
         own_copy(plane).start()
     w_in_copy(0).start()
+    near(start)
     met()
-
-    @pl.when(z < last)
-    def _():
-        own_move(0, z + 1).start()
-
-    @pl.when(z > 0)
-    def _():
-        own_move(1, z - 1).start()
+    near(lambda copy: copy.wait())
+    relay(0)
 
     row_high[...], row_low[...] = split(rows_ref[...])
     cot_high[...], cot_low[...] = split(cot_ref[...])
@@ -1462,13 +1671,12 @@
 
         @pl.when(step == 2)
         def _():
-            relay(0)
             core_move(0, 0).wait_recv()
+            relay(1)
+            relay_plane(0)
 
         @pl.when(step == 3)
         def _():
-            relay(1)
-            relay_plane(0)
             core_move(1, 0).wait_recv()
 
         @pl.when(step == 4)
@@ -1546,14 +1754,6 @@
         g_in_down_ref[tree] = dot3(d_inner, (row_high[own], row_low[own]), TN)
         g_out_up_ref[tree] = dot3(inner, (cot_high[own], cot_low[own]), TN)
 
-    @pl.when(z < last)
-    def _():
-        own_move(0, z + 1).wait_send()
-
-    @pl.when(z > 0)
-    def _():
-        own_move(1, z - 1).wait_send()
-
     for turn in range(last):
         passing(turn, lambda copy: copy.wait_send())
         plane_move(turn).wait_send()
@@ -1561,7 +1761,7 @@
         core_move(turn, 1).wait_send()
 
 
-def feed_forward(rows, cots, w_in, w_out, in_up, out_down, in_down, out_up):
+def feed_forward(rows, cots, w_in, w_out, near, in_up, out_down, in_down, out_up):
     count, width = rows.shape
     levels, _, units = w_in.shape
     block = units // 2
@@ -1574,7 +1774,7 @@
         out_shape=[shaped(count, width)] * 2
         + [shaped(*in_up.shape), shaped(*out_down.shape)]
         + [shaped(*in_down.shape), shaped(*out_up.shape)],
-        in_specs=[here, here, there, there] + [here] * 4,
+        in_specs=[here, here] + [there] * 4 + [here] * 4,
         out_specs=[here] * 6,
         scratch_shapes=[
             pltpu.VMEM((levels, 2, block, width), F32),
@@ -1587,18 +1787,19 @@
         + [
             dma((2,)),
             dma((2,)),
-            dma((levels + 1,)),
+            dma((levels - 1,)),
             dma((levels,)),
             dma((levels - 1,)),
             dma((levels - 1,)),
             dma((2 * levels - 2,)),
             dma((2 * levels - 2,)),
+            dma((2,)),
         ],
         compiler_params=pltpu.CompilerParams(
             vmem_limit_bytes=60 * MIB, collective_id=2, has_side_effects=True
         ),
         cost_estimate=lasting(110),
-    )(rows, cots, w_in, w_out, in_up, out_down, in_down, out_up)
+    )(rows, cots, w_in, w_out, *near, in_up, out_down, in_down, out_up)
 
 
 def by_distance(z, last, turn):
@@ -1803,9 +2004,9 @@
     return lax.dynamic_slice_in_dim(shard, lax.axis_index(COPIES) * part, part, 0)
 
 
-def gather_pair_half(shard):
-    whole = lax.all_gather(my_quarter(shard), ("z",) + COPIES, axis=0, tiled=True)
-    return whole.reshape((-1,) + shard.shape)
+def gather_pair_half(quarter, shape):
+    whole = lax.all_gather(quarter, ("z",) + COPIES, axis=0, tiled=True)
+    return whole.reshape((-1,) + shape)
 
 
 def pick(table, adapter_pick):
@@ -1817,12 +2018,28 @@
     )
 
 
+def after(array, other):
+    return array + 0.0 * other[(0,) * other.ndim]
+
+
 def swap(array):
     return lax.ppermute(array, "y", SWAP)
 
 
 def summed_to_owner(parts, axes):
     return jnp.sum(lax.all_to_all(parts, axes, split_axis=0, concat_axis=0, tiled=True), axis=0)
+
+
+def summed_along_line(parts):
+    levels = lax.axis_size("z")
+    z = lax.axis_index("z")
+    total = lax.dynamic_index_in_dim(parts, z, 0, keepdims=False)
+    for other in range(1, levels):
+        sent = lax.dynamic_index_in_dim(parts, z ^ other, 0, keepdims=False)
+        total = total + lax.ppermute(
+            sent, "z", [(level, level ^ other) for level in range(levels)]
+        )
+    return total
 
 
 def to_everyone(array):
@@ -1860,7 +2077,6 @@
     pairs = lax.axis_size("y")
     me, my_y = lax.axis_index(ROWS), lax.axis_index("y")
     lanes = width // slots
-    depth = 4
 
     down = pick(attn_down.swapaxes(2, 3), adapter_pick)
     up = pick(attn_up, adapter_pick)
@@ -1879,31 +2095,31 @@
     down_qkv = down[:, 0:3].reshape(trees, 3 * rank, width)
     up_own = lax.dynamic_slice_in_dim(up[:, 0:3], me * lanes, lanes, 3)
 
-    parts = [my_quarter(w) for w in (w_cross_kv.T, w_self_out, w_cross_out, w_cross_q.T)]
-    packed = lax.all_gather(jnp.concatenate(parts, axis=0), EVERY, axis=0, tiled=False)
-    packed = packed.reshape((slots, copies) + packed.shape[1:])
+    shard = jnp.concatenate(
+        [
+            w.reshape(copies, -1, width)
+            for w in (w_cross_kv.T, w_self_out, w_cross_out, w_cross_q.T)
+        ],
+        axis=1,
+    )
+    normed_all, inner_all, qkv, qkv_own, packed, context = heads_call(
+        segment_order, parents, tokens, norm_gains, w_qkv, shard, down_qkv, up_own
+    )
     row = width // (slots * copies)
     self_out_spec = packed_spec(packed, 2 * row, row)
     cross_out_spec = packed_spec(packed, 3 * row, row)
     cross_q_spec = packed_spec(packed, 4 * row, row)
-    fc_in_half = gather_pair_half(w_fc_in)
-
-    normed_all, inner_all, qkv, qkv_own = heads_call(
-        tokens, norm_gains, w_qkv, down_qkv, up_own
-    )
-    own_context = self_call(
-        self_forward_kernel,
-        depth,
-        segment_order,
-        parents,
-        (qkv,),
-        [slots_spec(qkv.shape)],
-        shaped(slots, trees, seg_len, lanes),
-        slots_spec((slots, trees, seg_len, lanes)),
-        20,
-    )
-    context = lax.all_to_all(own_context, ROWS, split_axis=0, concat_axis=0, tiled=True)
-
+
+    fc_in_late, qkv = lax.optimization_barrier((my_quarter(w_fc_in), qkv))
+    fc_in_half = gather_pair_half(fc_in_late, w_fc_in.shape)
+    fc_out_late, context = lax.optimization_barrier((my_quarter(w_fc_out), context))
+    levels = range(lax.axis_size("z") - 1)
+    fc_out_near = (
+        lax.ppermute(fc_out_late, "z", [(level, level + 1) for level in levels]),
+        lax.ppermute(fc_out_late, "z", [(level + 1, level) for level in levels]),
+    )
+
+    cotangent_other = swap(after(cotangent, context))
     memory = memory_call(encoder, packed, down, up)
     middle, cross_queries = rows_call(
         after_self_kernel,
@@ -1911,7 +2127,9 @@
         (None, None, None, self_out_spec, cross_q_spec, None, None),
         [shaped(*tokens.shape)] * 2,
     )
-    (cross_context,) = cross_call(cross_forward_kernel, cross_queries, memory, (), 0)
+    (cross_context,) = cross_call(
+        cross_forward_kernel, cross_queries, memory, (), 0, (cotangent_other,)
+    )
     after_cross, normed_three = rows_call(
         after_cross_kernel,
         (cross_context, middle, norm_gains, packed, down, up),
@@ -1919,14 +2137,19 @@
         [shaped(*tokens.shape)] * 2,
     )
 
-    def with_partner(rows):
-        return jnp.stack([rows, swap(rows)], axis=1).reshape(-1, width)
+    all_picks = lax.all_gather(adapter_pick, COPIES, axis=0, tiled=True)
+    entry = lax.broadcasted_iota(jnp.int32, (adapters, 1), 0)
+    tree_index = lax.broadcasted_iota(jnp.int32, (1, all_picks.shape[0]), 1)
+    source = jnp.sum(jnp.where(entry == all_picks[None, :], tree_index, 0), axis=1)
+    def paired(own_rows, other_rows):
+        return jnp.stack([own_rows, other_rows], axis=1).reshape(-1, width)
 
     out_part, d_rows_part, g_in_up, g_out_down, g_in_down, g_out_up = feed_forward(
-        with_partner(normed_three),
-        with_partner(cotangent),
+        paired(normed_three, swap(normed_three)),
+        paired(cotangent, cotangent_other),
         fc_in_half,
         w_fc_out,
+        fc_out_near,
         in_up,
         out_down,
         in_down,
@@ -1934,16 +2157,13 @@
     )
     d_rows_part = d_rows_part.reshape(trees, 2, seg_len, width)
     out_part = out_part.reshape(trees, 2, seg_len, width)
-    d_rows_other = swap(d_rows_part[:, 1])
-    out_other, d_rows_other = lax.optimization_barrier((out_part[:, 1], d_rows_other))
-    out_other = swap(out_other)
-
+
+    ahead = pl.BlockSpec(memory_space=pl.ANY)
     pair_maps = [shaped(trees, 1, rank, width)] * 2
-    d_after, d_cross_ctx, g_down_seven, g_up_seven = rows_call(
+    d_after, d_cross_ctx, g_down_seven, g_up_seven, hidden_sums = rows_call(
         into_cross_kernel,
         (
-            d_rows_part[:, 0],
-            d_rows_other,
+            d_rows_part,
             after_cross,
             cotangent,
             cross_context,
@@ -1951,14 +2171,33 @@
             packed,
             down,
             up,
+            g_in_up,
+            g_out_down,
         ),
-        (None,) * 6 + (cross_out_spec, None, None),
-        [shaped(*tokens.shape)] * 2 + pair_maps,
-    )
+        (None,) * 5 + (cross_out_spec,) + (None,) * 4,
+        [shaped(*tokens.shape)] * 2
+        + pair_maps
+        + [shaped(trees, 2, rank, hidden_units // slots)],
+        [
+            pltpu.VMEM(tokens.shape, F32),
+            pltpu.VMEM((len(levels), 2, trees, 2) + g_in_up.shape[2:], F32),
+            pltpu.SemaphoreType.DMA((2,)),
+            pltpu.SemaphoreType.DMA((len(levels), 2)),
+            pltpu.SemaphoreType.DMA((len(levels), 2)),
+        ],
+        pltpu.CompilerParams(
+            vmem_limit_bytes=56 * MIB, collective_id=3, has_side_effects=True
+        ),
+    )
+    def columns(parts):
+        stack = jnp.concatenate(parts, axis=1)
+        return stack.reshape(stack.shape[:3] + (slots, lanes)).transpose(3, 0, 1, 2, 4)
+
     d_cross_q, d_cross_k, d_cross_v = cross_call(
         cross_backward_kernel, cross_queries, memory, (d_cross_ctx,), 2
     )
-    out_other, d_cross_q = lax.optimization_barrier((out_other, d_cross_q))
+    out_other = swap(after(out_part[:, 1], d_cross_q))
+    hidden_all = to_everyone(hidden_sums)
     layer_out = after_cross + out_part[:, 0] + out_other
     d_middle, d_context, g_down_mid, g_up_mid = rows_call(
         into_self_kernel,
@@ -1977,18 +2216,6 @@
     other_side = lax.dynamic_index_in_dim(sides, 1 - my_y, 0, keepdims=False)
     own_side = lax.dynamic_index_in_dim(sides, my_y, 0, keepdims=False)
     enc_side = own_side + swap(other_side)
-
-    def columns(parts):
-        stack = jnp.concatenate(parts, axis=1)
-        return stack.reshape(stack.shape[:3] + (slots, lanes)).transpose(3, 0, 1, 2, 4)
-
-    hidden_parts = jnp.stack([g_in_up, g_out_down], axis=1).reshape(
-        trees, 2, slots // pairs, 2, rank, -1
-    )
-    hidden_parts = hidden_parts.transpose(2, 0, 1, 4, 3, 5).reshape(
-        slots // pairs, trees, 2, rank, hidden_units // slots
-    )
-    hidden_all = to_everyone(summed_to_owner(hidden_parts, "z"))
     early = summed_to_owner(
         columns(
             [
@@ -2003,19 +2230,32 @@
         ROWS,
     )
 
+    grad_in_up, grad_out_down = place_call(
+        place_hidden_kernel, source, (hidden_all,), [shaped(adapters, rank, hidden_units)] * 2
+    )
+
     normed_shape = (slots, trees, seg_len, width)
     d_qkv, g_down_part, g_up_qkv = self_call(
         self_backward_kernel,
-        depth,
         segment_order,
         parents,
-        (qkv, d_own_context, normed_all.reshape(normed_shape), inner_all, up_own),
+        (
+            qkv,
+            d_own_context,
+            normed_all.reshape(normed_shape),
+            inner_all,
+            up_own,
+            grad_in_up,
+            out_other,
+        ),
         [
             slots_spec(qkv.shape),
             slots_spec(d_own_context.shape),
             slots_spec(normed_shape),
             slots_spec(inner_all.shape),
             tree_spec(up_own.shape),
+            ahead,
+            ahead,
         ],
         [
             shaped(*qkv.shape),
@@ -2027,27 +2267,19 @@
             tree_spec((trees, 3, rank, width)),
             tree_spec((trees, 3, rank, lanes)),
         ],
-        43,
-    )
-    enc_side, g_down_part = lax.optimization_barrier((enc_side, g_down_part))
+        28,
+    )
     late = summed_to_owner(columns([g_down_part, g_down_memory, g_up_memory]), ROWS)
-    grad_encoder = summed_to_owner(enc_side, "z")
+    enc_side, late = lax.optimization_barrier((enc_side, late))
+    grad_encoder = summed_along_line(enc_side)
     attention_all = to_everyone(jnp.concatenate([late, g_up_qkv, early], axis=1))
     grad_tokens = into_tokens_call(
         d_qkv, qkv_own, tokens, d_middle, norm_gains, down_qkv, up_own
     )
-
-    all_picks = lax.all_gather(adapter_pick, COPIES, axis=0, tiled=True)
-    entry = lax.broadcasted_iota(jnp.int32, (adapters, 1), 0)
-    tree_index = lax.broadcasted_iota(jnp.int32, (1, all_picks.shape[0]), 1)
-    source = jnp.sum(jnp.where(entry == all_picks[None, :], tree_index, 0), axis=1)
     wide = shaped(adapters, projections, rank, width)
     narrow = shaped(adapters, rank, width)
     grad_down, grad_up, grad_in_down, grad_out_up = place_call(
         place_kernel, source, (attention_all,), [wide, wide, narrow, narrow]
-    )
-    grad_in_up, grad_out_down = place_call(
-        place_hidden_kernel, source, (hidden_all,), [shaped(adapters, rank, hidden_units)] * 2
     )
     return (
         layer_out,

time: 975 us -> 903 us (0.926)
  Pallas kernels: 731 us -> 677 us
    all_to_all x1 -> x0, waiting for transfers between devices: 52.5 us -> none  [by_heads(): lax.all_to_all(own_context, ROWS, split_axis=0, concat_axis=0, tiled=True)]
    all_gather x2 -> x1, waiting for transfers between devices: 0.01 us -> 51.2 us  [gather_pair_half(): whole = lax.all_gather(quarter, ('z',) + COPIES, axis=0, tiled=True)]
    pallas_call x2 -> x1, Pallas kernels: 63.7 us -> 27.9 us  [self_call(): pl.pallas_call(kernel, out_shape=out_shape, grid_spec=pltpu.PrefetchScala...]
    pallas_call x4, Pallas kernels: 40.8 us -> 67.8 us  [rows_call(): pl.pallas_call(kernel, out_shape=out_shape, grid=(1,), in_specs=[whole_sp...]
    pallas_call x2, Pallas kernels: 51.8 us -> 29.7 us  [cross_call(): pl.pallas_call(kernel, out_shape=[shaped(trees, seg_len, width)] + [shape...]
    pallas_call x1, Pallas kernels: 124 us -> 113 us  [feed_forward(): pl.pallas_call(feed_forward_kernel, out_shape=[shaped(count, width)] * 2...]
    all_to_all x4 -> x2, waiting for transfers between devices: 41.2 us -> 30.7 us  [summed_to_owner(): lax.all_to_all(parts, axes, split_axis=0, concat_axis=0, tiled=True)]
    all_gather x2, waiting for transfers between devices: 0.01 us -> 10.4 us  [to_everyone(): everyone = lax.all_gather(array, COPIES + ROWS, axis=0, tiled=False)]
  transfers between devices with their start and end apart: 15 -> 15, of which waited for: 5 -> 5; matrix products, arithmetic and copies ran while one was open for 4% -> 5% of each run, Pallas kernels for 62% -> 33%
where the time goes in v3:
time: 903 us; the launch traced here: 892 us
  Pallas kernels  677 us (75%)
  waiting for transfers between devices  103 us (11%)
  local copies, waits for them, and re-layouts  43.9 us (5%)
  starting transfers between devices  26.5 us (3%)
  between operations  20.7 us (2%)
  other arithmetic  16 us (2%)
    pallas_call x1, Pallas kernels, heads_call(): pl.pallas_call(heads_kernel, out_shape=[shaped(slots, trees * seg_len, wi...  221 us
    pallas_call x1, Pallas kernels, into_tokens_call(): pl.pallas_call(into_tokens_kernel, out_shape=shaped(*tokens.shape), in_sp...  144 us
    pallas_call x1, Pallas kernels, feed_forward(): pl.pallas_call(feed_forward_kernel, out_shape=[shaped(count, width)] * 2...  113 us
    pallas_call x4, Pallas kernels, rows_call(): pl.pallas_call(kernel, out_shape=out_shape, grid=(1,), in_specs=[whole_sp...  67.8 us
    all_gather x1, waiting for transfers between devices, gather_pair_half(): whole = lax.all_gather(quarter, ('z',) + COPIES, axis=0, tiled=True)  51.2 us
    pallas_call x1, Pallas kernels, memory_back_call(): pl.pallas_call(memory_back_kernel, out_shape=[shaped(trees, count, width)...  31 us
    all_to_all x2, waiting for transfers between devices, summed_to_owner(): lax.all_to_all(parts, axes, split_axis=0, concat_axis=0, tiled=True)  30.7 us
    pallas_call x2, Pallas kernels, cross_call(): pl.pallas_call(kernel, out_shape=[shaped(trees, seg_len, width)] + [shape...  29.7 us
  transfers between devices with their start and end apart: 15, of which 5 were waited for; matrix products, arithmetic and copies ran while one was open for 5% of the time, Pallas kernels for 33%

profile of v3, /device:TPU:0, one launch (start us, length us, event | category | flops | bytes accessed | tf_op | source)
XLA Modules:
  0.0 892.4 jit_solution(9255785237164127237)
XLA Ops:
  22.1 221.3 %shard_map.259 = (f32[8,256,1024]{2,1,0:T(8,128)}, f32[8,2,128,48]{3,2,1,0:T(8,128)S(1)}, f32[8,3,2,128,128]{4,3,2,1,0:T(8,128)}, f32[3,1024,128]{2,1,0:T(8,128)...) custom-call(s32[2,8]{1,0:T(2,128)S(1)} %copy-done.8, s32[2,8]{1,0:T(2,128)S(1)} %copy-done.9, ...), custom_call_target="tpu_custom_call" | custom-call | flops 179999997952 | bytes 540000000 | tf_op jit(solution)/shard_map/pallas_call | solution.py:903
  255.9 22.3 %shard_map.261.key_ref.value_ref = f32[2,512,2048]{2,1,0:T(8,128)} custom-call(f32[2,512,1024]{2,1,0:T(8,128)} %encoder_ref.3, f32[8,4,160,1024]{3,2,1,0:T(8,128)} %get-tuple-element.58.out_ref.query_ref.weight_ref, bf16[2,8,16,1024]{3,2,1,0:T(8,128)(2,1)} %get-tuple-element.124.down_ref, bf16[2,8,16,1024]{3,2,1,0:T(8,128)(2,1)} %get-tuple-element.125.up_ref), custom_call_target="tpu_custom_call" | custom-call | flops 22000001024 | bytes 66000000 | tf_op jit(solution)/shard_map/pallas_call | solution.py:1386
  278.3 11.2 %shard_map.260 = (f32[2,128,1024]{2,1,0:T(8,128)}, f32[2,128,1024]{2,1,0:T(8,128)}) custom-call(f32[8,2,128,128]{3,2,1,0:T(8,128)} %copy-done, f32[2,128,1024]{2,1,0:T(8,128)} %tokens_ref.5, f32[3,1024]{1,0:T(4,128)} %gains_ref.11, f32[8,4,160,1024]{3,2,1,0:T(8,128)} %get-tuple-element.58.out_ref.query_ref.weight_ref, ...), custom_call_target="tpu_custom_call" | custom-call | flops 10000000000 | bytes 30000000 | tf_op jit(solution)/shard_map/pallas_call | solution.py:1340
  290.7 10.7 %shard_map.262.context_ref = f32[2,128,1024]{2,1,0:T(8,128)S(1)} custom-call(f32[2,128,1024]{2,1,0:T(8,128)S(1)} %copy-done.6, f32[2,512,2048]{2,1,0:T(8,128)} %shard_map.261.key_ref.value_ref, f32[2,512,2048]{2,1,0:T(8,128)} %shard_map.261.key_ref.value_ref, f32[2,128,1024]{2,1,0:T(8,128)S(1)} %collective-permute-done._), custom_call_target="tpu_custom_call" | custom-call | flops 19000000512 | bytes 57000000 | tf_op jit(solution)/shard_map/pallas_call | solution.py:1135
  302.4 7.2 shard_map.263
  313.4 3.9 dynamic-slice_reduce_fusion
  323.9 10.9 %collective-permute-done.1 = f32[2,128,1024]{2,1,0:T(8,128)} collective-permute-done((f32[2,128,1024]{2,1,0:T(8,128)}, f32[2,128,1024]{2,1,0:T(8,128)}, u32[]{:S(2)}, u32[]{:S(2)}) %collective-permute-start.1) | collective-permute-done | bytes 1048608 | tf_op jit(solution)/shard_map/ppermute | solution.py:2026
  337.7 51.2 %all-gather.6.cloned.1.call-done = f32[4096,1024]{1,0:T(8,128)} async-done(((f32[256,1024]{1,0:T(8,128)}), f32[4096,1024]{1,0:T(8,128)}) %all-gather.6.cloned.1.call-update) | async-done | bytes 16777232 | tf_op jit(solution)/shard_map/all_gather | solution.py:2008
  388.9 113.1 %shard_map.264 = (f32[512,1024]{1,0:T(8,128)}, f32[512,1024]{1,0:T(8,128)}, f32[2,8,16,512]{3,2,1,0:T(8,128)}, f32[2,8,16,512]{3,2,1,0:T(8,128)}, f32[2,16,1024]{2,1,0:T(8,128)}, /*index=5*/f32[2,16,1024]{2,1,0:T(8,128)}) custom-call(f32[512,1024]{1,0:T(8,128)} %bitcast.135, f32[512,1024]{1,0:T(8,128)} %bitcast.134, f32[4,1024,1024]{2,1,0:T(8,128)} %bitcast.151, ...), custom_call_target="tpu_custom_call" | custom-call | flops 109999996928 | bytes 330000000 | tf_op jit(solution)/shard_map/pallas_call | solution.py:1772
  502.1 37.0 %shard_map.265 = (f32[2,128,1024]{2,1,0:T(8,128)}, f32[2,128,1024]{2,1,0:T(8,128)}, f32[2,1,16,1024]{3,2,1,0:T(8,128)}, f32[2,1,16,1024]{3,2,1,0:T(8,128)}, f32[2,2,16,1024]{3,2,1,0:T(8,128)}) custom-call(f32[2,2,128,1024]{3,2,1,0:T(8,128)} %bitcast.157, f32[2,128,1024]{2,1,0:T(8,128)} %get-tuple-element.61.after_ref, f32[2,128,1024]{2,1,0:T(8,128)} %cotangent_ref.1, ...), custom_call_target="tpu_custom_call" | custom-call | flops 10000000000 | bytes 30000000 | tf_op jit(solution)/shard_map/pallas_call | solution.py:1340
  540.7 4.9 all-reduce
  549.5 19.1 %shard_map.266 = (f32[2,128,1024]{2,1,0:T(8,128)S(1)}, f32[2,512,1024]{2,1,0:T(8,128)}, f32[2,512,1024]{2,1,0:T(8,128)}) custom-call(f32[2,128,1024]{2,1,0:T(8,128)S(1)} %copy-done.7, f32[2,512,2048]{2,1,0:T(8,128)} %shard_map.261.key_ref.value_ref, f32[2,512,2048]{2,1,0:T(8,128)} %shard_map.261.key_ref.value_ref, f32[2,128,1024]{2,1,0:T(8,128)S(1)} %copy-done.11), custom_call_target="tpu_custom_call" | custom-call | flops 32000000000 | bytes 96000000 | tf_op jit(solution)/shard_map/pallas_call | solution.py:1135
  569.6 12.5 %shard_map.267 = (f32[2,128,1024]{2,1,0:T(8,128)}, f32[8,2,128,128]{3,2,1,0:T(8,128)}, f32[2,2,16,1024]{3,2,1,0:T(8,128)}, f32[2,2,16,1024]{3,2,1,0:T(8,128)}) custom-call(f32[2,128,1024]{2,1,0:T(8,128)} %copy-done.2, f32[2,128,1024]{2,1,0:T(8,128)} %get-tuple-element.73.d_after_ref, f32[2,128,1024]{2,1,0:T(8,128)} %get-tuple-element.60.middle_ref, ...), custom_call_target="tpu_custom_call" | custom-call | flops 10000000000 | bytes 30000000 | tf_op jit(solution)/shard_map/pallas_call | solution.py:1340
  582.0 4.6 all-to-all-start
  589.3 31.0 %shard_map.271 = (f32[2,512,1024]{2,1,0:T(8,128)}, f32[2,2,16,1024]{3,2,1,0:T(8,128)}, f32[2,2,16,1024]{3,2,1,0:T(8,128)}) custom-call(f32[2,512,1024]{2,1,0:T(8,128)} %encoder_ref.3, f32[2,512,1024]{2,1,0:T(8,128)} %get-tuple-element.83.d_key_ref, f32[2,512,1024]{2,1,0:T(8,128)} %get-tuple-element.84.d_value_ref, ...), custom_call_target="tpu_custom_call" | custom-call | flops 31000000512 | bytes 93000000 | tf_op jit(solution)/shard_map/pallas_call | solution.py:1466
  627.8 10.4 %all-gather.8.cloned.1.call-done = f32[64,2,16,1024]{3,2,1,0:T(8,128)} async-done(((f32[2,2,16,1024]{3,2,1,0:T(8,128)}), f32[64,2,16,1024]{3,2,1,0:T(8,128)}) %all-gather.8.cloned.1.call-update) | async-done | bytes 8388624 | tf_op jit(solution)/shard_map/all_gather | solution.py:2046
  638.2 9.5 %shard_map.268 = (f32[8,16,8192]{2,1,0:T(8,128)}, f32[8,16,8192]{2,1,0:T(8,128)}) custom-call(s32[8]{0:T(128)S(1)} %select_reduce_fusion.source_ref, f32[4,8,2,2,16,1024]{5,4,3,2,1,0:T(8,128)} %bitcast.153), custom_call_target="tpu_custom_call" | custom-call | flops 8999999488 | bytes 27000000 | tf_op jit(solution)/shard_map/pallas_call | solution.py:1988
  647.8 3.6 all-to-all-start.2
  652.3 27.9 %shard_map.269 = (f32[8,3,2,128,128]{4,3,2,1,0:T(8,128)}, f32[2,3,16,1024]{3,2,1,0:T(8,128)}, f32[2,3,16,128]{3,2,1,0:T(8,128)}) custom-call(s32[2,8]{1,0:T(2,128)} %order_ref.3, s32[2,8]{1,0:T(2,128)} %parents_ref.3, f32[8,3,2,128,128]{4,3,2,1,0:T(8,128)} %get-tuple-element.72.qkv_ref, f32[8,2,128,128]{3,2,1,0:T(8,128)} %all-to-all-done.d_context_ref, ...), custom_call_target="tpu_custom_call" | custom-call | flops 28000000000 | bytes 84000000 | tf_op jit(solution)/shard_map/pallas_call | solution.py:1089
  682.3 10.6 %all-to-all-done.2 = f32[8,2,8,16,128]{4,3,2,1,0:T(8,128)S(1)} async-done(((f32[8,2,8,16,128]{4,3,2,1,0:T(8,128)}), f32[8,2,8,16,128]{4,3,2,1,0:T(8,128)S(1)}, u32[]{:S(2)}, u32[]{:S(2)}) %all-to-all-start.2) | async-done | bytes 1048608 | tf_op jit(solution)/shard_map/all_to_all | solution.py:2030
  692.9 4.6 all-to-all-start.1
  700.5 20.0 %all-to-all-done.1 = f32[8,2,7,16,128]{4,3,2,1,0:T(8,128)S(1)} async-done(((f32[8,2,7,16,128]{4,3,2,1,0:T(8,128)}), f32[8,2,7,16,128]{4,3,2,1,0:T(8,128)S(1)}, u32[]{:S(2)}, u32[]{:S(2)}) %all-to-all-start.1) | async-done | bytes 917536 | tf_op jit(solution)/shard_map/all_to_all | solution.py:2030
  729.1 144.1 %shard_map.270 = f32[2,128,1024]{2,1,0:T(8,128)} custom-call(f32[8,3,2,128,128]{4,3,2,1,0:T(8,128)} %get-tuple-element.79.d_qkv_ref, f32[3,1024,128]{2,1,0:T(8,128)} %copy-done.13, f32[2,128,1024]{2,1,0:T(8,128)} %tokens_ref.5, f32[2,128,1024]{2,1,0:T(8,128)} %get-tuple-element.81.d_middle_ref, f32[3,1024]{1,0:T(4,128)} %gains_ref.11, ...), custom_call_target="tpu_custom_call" | custom-call | flops 109999996928 | bytes 330000000 | tf_op jit(solution)/shard_map/pallas_call | solution.py:1939
  874.2 10.3 %shard_map.272 = (f32[8,8,16,1024]{3,2,1,0:T(8,128)}, f32[8,8,16,1024]{3,2,1,0:T(8,128)}, f32[8,16,1024]{2,1,0:T(8,128)}, f32[8,16,1024]{2,1,0:T(8,128)}) custom-call(s32[8]{0:T(128)S(1)} %select_reduce_fusion.source_ref, f32[4,8,2,18,16,128]{5,4,3,2,1,0:T(8,128)} %bitcast.152), custom_call_target="tpu_custom_call" | custom-call | flops 8999999488 | bytes 27000000 | tf_op jit(solution)/shard_map/pallas_call | solution.py:1988
  (161 shorter events, 69.9 us)
Async XLA Ops:
  7.2 381.8 %all-gather.6.cloned.1.call-start = ((), (), s32[]{:S(2)}) async-start(), calls=%async_computation.3 | async-start | bytes 17825792 | tf_op jit(solution)/shard_map/all_gather | solution.py:2008
  22.1 229.5 %copy-start.14 = (f32[2,128,1024]{2,1,0:T(8,128)S(1)}, f32[2,128,1024]{2,1,0:T(8,128)}, u32[]{:S(2)}) copy-start(f32[2,128,1024]{2,1,0:T(8,128)} %cotangent_ref.1) | copy-start | bytes 3145732
  245.6 392.7 %all-gather.8.cloned.1.call-start = ((), (), s32[]{:S(2)}) async-start(), calls=%async_computation.4 | async-start | bytes 8650752 | tf_op jit(solution)/shard_map/all_gather | solution.py:2046
  245.6 92.1 %collective-permute-start.2 = (f32[256,1024]{1,0:T(8,128)}, f32[256,1024]{1,0:T(8,128)}, u32[]{:S(2)}, u32[]{:S(2)}) collective-permute-start(f32[256,1024]{1,0:T(8,128)} %get-tuple-element.65), channel_id=1, source_target_pairs={{0,2},{2,4},{4,6},{1,3},{3,5},{5,7},{8,10},{10,12},{12,14},{9,11},... | collective-permute-start | bytes 3145736 | tf_op jit(solution)/shard_map/ppermute | solution.py:2118
  249.2 88.6 %collective-permute-start.3 = (f32[256,1024]{1,0:T(8,128)}, f32[256,1024]{1,0:T(8,128)}, u32[]{:S(2)}, u32[]{:S(2)}) collective-permute-start(f32[256,1024]{1,0:T(8,128)} %get-tuple-element.65), channel_id=1, source_target_pairs={{2,0},{4,2},{6,4},{3,1},{5,3},{7,5},{10,8},{12,10},{14,12},{11,9},... | collective-permute-start | bytes 3145736 | tf_op jit(solution)/shard_map/ppermute | solution.py:2119
  251.7 37.8 %collective-permute-start = (f32[2,128,1024]{2,1,0:T(8,128)S(1)}, f32[2,128,1024]{2,1,0:T(8,128)S(1)}, u32[]{:S(2)}, u32[]{:S(2)}) collective-permute-start(f32[2,128,1024]{2,1,0:T(8,128)S(1)} %broadcast_add_fusion), channel_id=1, source_target_pairs={{0,1},{1,0},{2,3},{3,2},{4,5},{5,4},{6,7},{7,6},{8,9},{9,8},{10,11... | collective-permute-start | bytes 3145736 | tf_op jit(solution)/shard_map/ppermute | solution.py:2026
  309.5 25.3 %collective-permute-start.1 = (f32[2,128,1024]{2,1,0:T(8,128)}, f32[2,128,1024]{2,1,0:T(8,128)}, u32[]{:S(2)}, u32[]{:S(2)}) collective-permute-start(f32[2,128,1024]{2,1,0:T(8,128)} %get-tuple-element.62), channel_id=1, source_target_pairs={{0,1},{1,0},{2,3},{3,2},{4,5},{5,4},{6,7},{7,6},{8,9},{9,8},{10,11... | collective-permute-start | bytes 3145736 | tf_op jit(solution)/shard_map/ppermute | solution.py:2026
  502.1 37.1 %copy-start.39 = (u32[32]{0:T(128)S(1)}, u32[32]{0:T(128)}, u32[]{:S(2)}) copy-start(u32[32]{0:T(128)} %constant.98) | copy-start | bytes 388
  502.1 38.3 %copy-start.38 = (s32[2]{0:T(128)S(1)}, s32[2]{0:T(128)}, u32[]{:S(2)}) copy-start(s32[2]{0:T(128)} %param.23) | copy-start | bytes 28
  502.1 46.1 %copy-start.36 = (f32[2,16,1024]{2,1,0:T(8,128)S(1)}, f32[2,16,1024]{2,1,0:T(8,128)}, u32[]{:S(2)}) copy-start(f32[2,16,1024]{2,1,0:T(8,128)} %get-tuple-element.96) | copy-start | bytes 393220
  502.1 46.1 %copy-start.35 = (f32[2,16,1024]{2,1,0:T(8,128)S(1)}, f32[2,16,1024]{2,1,0:T(8,128)}, u32[]{:S(2)}) copy-start(f32[2,16,1024]{2,1,0:T(8,128)} %get-tuple-element.97) | copy-start | bytes 393220
  502.1 46.2 %copy-start.7 = (f32[2,128,1024]{2,1,0:T(8,128)S(1)}, f32[2,128,1024]{2,1,0:T(8,128)}, u32[]{:S(2)}) copy-start(f32[2,128,1024]{2,1,0:T(8,128)} %get-tuple-element.59.query_ref) | copy-start | bytes 3145732
  582.0 65.7 %all-to-all-start = ((f32[8,2,128,128]{3,2,1,0:T(8,128)}), f32[8,2,128,128]{3,2,1,0:T(8,128)}, u32[]{:S(2)}, u32[]{:S(2)}) async-start(f32[8,2,128,128]{3,2,1,0:T(8,128)} %get-tuple-element.74), calls=%async_computation | async-start | bytes 2097152 | tf_op jit(solution)/shard_map/all_to_all | solution.py:2209
  587.3 64.0 %collective-permute-start.4 = (f32[2,128,1024]{2,1,0:T(8,128)S(1)}, f32[2,128,1024]{2,1,0:T(8,128)S(1)}, u32[]{:S(2)}, u32[]{:S(2)}) collective-permute-start(f32[2,128,1024]{2,1,0:T(8,128)S(1)} %fusion.1), channel_id=1, source_target_pairs={{0,1},{1,0},{2,3},{3,2},{4,5},{5,4},{6,7},{7,6},{8,9},{9,8},{10,11... | collective-permute-start | bytes 3145736 | tf_op jit(solution)/shard_map/ppermute | solution.py:2026
  623.6 74.3 %collective-permute-start.5 = (f32[4,2,64,1024]{3,2,0,1:T(8,128)}, f32[4,2,64,1024]{3,2,0,1:T(8,128)}, u32[]{:S(2)}, u32[]{:S(2)}) collective-permute-start(f32[4,2,64,1024]{3,2,0,1:T(8,128)} %dynamic-slice_bitcast_fusion), channel_id=1, source_target_pairs={{0,1},{1,0},{2,3},{3,2},{4,5},{5,4},{6,7},{7,6},{8,9},{9,8},{10,11... | collective-permute-start | bytes 6291464 | tf_op jit(solution)/shard_map/ppermute | solution.py:2026
  647.8 45.1 %all-to-all-start.2 = ((f32[8,2,8,16,128]{4,3,2,1,0:T(8,128)}), f32[8,2,8,16,128]{4,3,2,1,0:T(8,128)S(1)}, u32[]{:S(2)}, u32[]{:S(2)}) async-start(f32[8,2,8,16,128]{4,3,2,1,0:T(8,128)} %bitcast.43), calls=%async_computation.2 | async-start | bytes 2097152 | tf_op jit(solution)/shard_map/all_to_all | solution.py:2030
  652.3 27.9 %copy-start.31 = (f32[2,2,16,1024]{3,2,1,0:T(8,128)S(1)}, f32[2,2,16,1024]{3,2,1,0:T(8,128)}, u32[]{:S(2)}) copy-start(f32[2,2,16,1024]{3,2,1,0:T(8,128)} %get-tuple-element.87) | copy-start | bytes 786436
  652.3 27.9 %copy-start.32 = (f32[2,2,16,1024]{3,2,1,0:T(8,128)S(1)}, f32[2,2,16,1024]{3,2,1,0:T(8,128)}, u32[]{:S(2)}) copy-start(f32[2,2,16,1024]{3,2,1,0:T(8,128)} %get-tuple-element.88) | copy-start | bytes 786436
  692.9 27.6 %all-to-all-start.1 = ((f32[8,2,7,16,128]{4,3,2,1,0:T(8,128)}), f32[8,2,7,16,128]{4,3,2,1,0:T(8,128)S(1)}, u32[]{:S(2)}, u32[]{:S(2)}) async-start(f32[8,2,7,16,128]{4,3,2,1,0:T(8,128)} %bitcast_bitcast_fusion), calls=%async_computation.1 | async-start | bytes 1835008 | tf_op jit(solution)/shard_map/all_to_all | solution.py:2030
  697.5 176.7 %all-gather.10.cloned.1.call-start = ((), (), s32[]{:S(2)}) async-start(), calls=%async_computation.5 | async-start | bytes 9732096 | tf_op jit(solution)/shard_map/all_gather | solution.py:2046
  697.9 22.7 %copy-start.37 = (f32[2,3,16,128]{3,2,1,0:T(8,128)S(1)}, f32[2,3,16,128]{3,2,1,0:T(8,128)}, u32[]{:S(2)}) copy-start(f32[2,3,16,128]{3,2,1,0:T(8,128)} %get-tuple-element.91) | copy-start | bytes 147460
  724.7 148.5 %collective-permute-start.6 = (f32[2,64,1024]{2,1,0:T(8,128)S(1)}, f32[2,64,1024]{2,1,0:T(8,128)S(1)}, u32[]{:S(2)}, u32[]{:S(2)}) collective-permute-start(f32[2,64,1024]{2,1,0:T(8,128)S(1)} %get-tuple-element.103), channel_id=1, source_target_pairs={{0,2},{2,0},{4,6},{6,4},{1,3},{3,1},{5,7},{7,5},{8,10},{10,8},{12,... | collective-permute-start | bytes 1572872 | tf_op jit(solution)/shard_map/ppermute | solution.py:2039
  724.7 148.5 %collective-permute-start.7 = (f32[2,64,1024]{2,1,0:T(8,128)S(1)}, f32[2,64,1024]{2,1,0:T(8,128)S(1)}, u32[]{:S(2)}, u32[]{:S(2)}) collective-permute-start(f32[2,64,1024]{2,1,0:T(8,128)S(1)} %get-tuple-element.105), channel_id=1, source_target_pairs={{0,4},{2,6},{4,0},{6,2},{1,5},{3,7},{5,1},{7,3},{8,12},{10,14},{12... | collective-permute-start | bytes 1572872 | tf_op jit(solution)/shard_map/ppermute | solution.py:2039
  726.4 146.9 %collective-permute-start.8 = (f32[2,64,1024]{2,1,0:T(8,128)S(1)}, f32[2,64,1024]{2,1,0:T(8,128)S(1)}, u32[]{:S(2)}, u32[]{:S(2)}) collective-permute-start(f32[2,64,1024]{2,1,0:T(8,128)S(1)} %get-tuple-element.104), channel_id=1, source_target_pairs={{0,6},{2,4},{4,2},{6,0},{1,7},{3,5},{5,3},{7,1},{8,14},{10,12},{12... | collective-permute-start | bytes 1572872 | tf_op jit(solution)/shard_map/ppermute | solution.py:2039
  (31 other events, 122.5 us)
Sparse Core Ops, SparseCore 0:
  245.7 143.2 all-gather.5
  539.3 98.9 all-gather.7
  721.5 137.5 all-gather.9

commit v4 on v3

--- a/solution.py
+++ b/solution.py
@@ -556,6 +556,8 @@
     keep_sem,
     block_sem,
     block_here_sem,
+    block_core_sem,
+    block_core_here_sem,
     here_sem,
     across_sem,
     over_first_sem,
@@ -585,34 +587,44 @@
 
     own = place(z, y)
 
+    half = pl.ds(pl.multiple_of(c * (width // 2), width // 2), width // 2)
+
     def block_move(i):
         block = 3 * own + i
         target, kind = block % slots, block // slots
-        source = weight_ref.at[:, i * lanes : (i + 1) * lanes]
+        source = weight_ref.at[half, i * lanes : (i + 1) * lanes]
 
         def sent():
             return remote(
                 source,
-                blocks_ref.at[kind],
+                blocks_ref.at[kind, half],
                 block_sem.at[i],
                 block_here_sem.at[kind],
                 {"z": target // 2, "y": target % 2},
             )
 
         def kept():
-            return pltpu.make_async_copy(source, blocks_ref.at[kind], block_here_sem.at[kind])
+            return pltpu.make_async_copy(
+                source, blocks_ref.at[kind, half], block_here_sem.at[kind]
+            )
 
         return target, sent, kept
 
-    half = shard_ref.shape[1] // 2
+    def block_across(kind):
+        block = blocks_ref.at[kind, half]
+        return remote(
+            block, block, block_core_sem.at[kind], block_core_here_sem.at[kind], {"c": 1 - c}
+        )
+
+    cut = shard_ref.shape[1] * 7 // 80 * 8
+    spans = (slice(0, cut), slice(cut, shard_ref.shape[1]))
 
     def rows_move(slot, sem, device):
         return remote(rows_ref.at[slot], rows_ref.at[slot], sem, here_sem.at[slot], device)
 
     def shard_move(part, slot, sem, device):
-        rows = slice(part * half, (part + 1) * half)
-        piece = packed_ref.at[slot, mine, rows]
-        source = shard_ref.at[mine, rows] if slot is own else piece
+        piece = packed_ref.at[slot, mine, spans[part]]
+        source = shard_ref.at[mine, spans[part]] if slot is own else piece
         return remote(source, piece, sem, shard_here_sem.at[part, slot], device)
 
     first = functools.partial(shard_move, 0)
@@ -634,13 +646,13 @@
         return own if level is z else place(level, y)
 
     def plane_move(part, slot):
-        piece = packed_ref.at[slot, mine, part * half : (part + 1) * half]
+        piece = packed_ref.at[slot, mine, spans[part]]
         return remote(
             piece, piece, plane_sem.at[part, slot], plane_here_sem.at[part, slot], {"x": 1 - x}
         )
 
     def core_move(part, slot, kind):
-        piece = packed_ref.at[slot, facing if kind else mine, part * half : (part + 1) * half]
+        piece = packed_ref.at[slot, facing if kind else mine, spans[part]]
         index = 2 * part + kind
         return remote(
             piece, piece, core_sem.at[index, slot], core_here_sem.at[index, slot], {"c": 1 - c}
@@ -700,10 +712,13 @@
 
     def take_blocks():
         for kind in range(3):
-            block = blocks_ref.at[kind]
+            block = blocks_ref.at[kind, half]
             pltpu.make_async_copy(block, block, block_here_sem.at[kind]).wait()
+            block_across(kind).start()
+        for kind in range(3):
+            block_across(kind).wait_recv()
             where = slice(kind * lanes, (kind + 1) * lanes)
-            w_high[:, where], w_low[:, where] = split(block[...])
+            w_high[:, where], w_low[:, where] = split(blocks_ref[kind])
         keep_blocks().start()
 
     def work(slot):
@@ -858,6 +873,7 @@
     keep_shard().wait()
     keep_blocks().wait()
     for i in range(3):
+        block_across(i).wait_send()
         target, sent, _ = block_move(i)
 
         @pl.when(target != own)
@@ -919,9 +935,8 @@
             pltpu.VMEM((width, 3 * lanes), BF16),
             pltpu.VMEM((width, 3 * lanes), BF16),
             dma((slots + 2,)),
-            dma((3,)),
-            dma((3,)),
         ]
+        + [dma((3,))] * 4
         + [dma((slots,))] * 4
         + [dma((2, slots))] * 6
         + [dma((4, slots))] * 2
@@ -1026,7 +1041,6 @@
     inner_ref,
     up_ref,
     _,
-    __,
     d_qkv_ref,
     g_down_ref,
     g_up_ref,
@@ -1517,6 +1531,7 @@
     out_down_ref,
     in_down_ref,
     out_up_ref,
+    _,
     out_ref,
     d_rows_ref,
     g_in_up_ref,
@@ -1761,7 +1776,7 @@
         core_move(turn, 1).wait_send()
 
 
-def feed_forward(rows, cots, w_in, w_out, near, in_up, out_down, in_down, out_up):
+def feed_forward(rows, cots, w_in, w_out, near, in_up, out_down, in_down, out_up, ahead):
     count, width = rows.shape
     levels, _, units = w_in.shape
     block = units // 2
@@ -1774,7 +1789,7 @@
         out_shape=[shaped(count, width)] * 2
         + [shaped(*in_up.shape), shaped(*out_down.shape)]
         + [shaped(*in_down.shape), shaped(*out_up.shape)],
-        in_specs=[here, here] + [there] * 4 + [here] * 4,
+        in_specs=[here, here] + [there] * 4 + [here] * 4 + [there],
         out_specs=[here] * 6,
         scratch_shapes=[
             pltpu.VMEM((levels, 2, block, width), F32),
@@ -1799,7 +1814,7 @@
             vmem_limit_bytes=60 * MIB, collective_id=2, has_side_effects=True
         ),
         cost_estimate=lasting(110),
-    )(rows, cots, w_in, w_out, *near, in_up, out_down, in_down, out_up)
+    )(rows, cots, w_in, w_out, *near, in_up, out_down, in_down, out_up, ahead)
 
 
 def by_distance(z, last, turn):
@@ -1951,15 +1966,10 @@
     )(d_qkv, weight, tokens, d_middle, gains, down, up)
 
 
-LATE_DOWN, LATE_UP = (0, 1, 2, 5, 6), (5, 6)
-OWN_UP = (0, 1, 2)
-EARLY = (3, 4, 7)
-
-
 def place_kernel(source_ref, parts_ref, down_ref, up_ref, in_down_ref, out_up_ref):
-    places = [(down_ref, entry) for entry in LATE_DOWN] + [(up_ref, entry) for entry in LATE_UP]
-    places += [(up_ref, entry) for entry in OWN_UP]
-    places += [(down_ref, entry) for entry in EARLY] + [(up_ref, entry) for entry in EARLY]
+    places = [(down_ref, entry) for entry in range(3)] + [(up_ref, entry) for entry in range(3)]
+    places += [(down_ref, entry) for entry in range(3, 8)]
+    places += [(up_ref, entry) for entry in range(3, 8)]
     span = parts_ref.shape[5]
     for owner in range(parts_ref.shape[1]):
         lanes = slice(owner * span, (owner + 1) * span)
@@ -1969,7 +1979,7 @@
         out_up_ref[0, :, lanes] = parts_ref[0, owner, 0, len(places) + 1]
 
 
-def place_hidden_kernel(source_ref, parts_ref, in_up_ref, out_down_ref):
+def place_hidden_kernel(source_ref, parts_ref, _, in_up_ref, out_down_ref):
     for owner in range(parts_ref.shape[1]):
         units = parts_ref.shape[5]
         lanes = slice(owner * units, (owner + 1) * units)
@@ -1977,7 +1987,7 @@
         out_down_ref[0, :, lanes] = parts_ref[0, owner, 0, 1]
 
 
-def place_call(kernel, source, arrays, out_shape):
+def place_call(kernel, source, arrays, out_shape, ahead=()):
     def chosen(array):
         groups = array.shape[2]
         return pl.BlockSpec(
@@ -1991,12 +2001,13 @@
         grid_spec=pltpu.PrefetchScalarGridSpec(
             num_scalar_prefetch=1,
             grid=(out_shape[0].shape[0],),
-            in_specs=[chosen(array) for array in arrays],
+            in_specs=[chosen(array) for array in arrays]
+            + [pl.BlockSpec(memory_space=pl.ANY)] * len(ahead),
             out_specs=[tree_spec(out.shape) for out in out_shape],
         ),
         compiler_params=vmem(48),
         cost_estimate=lasting(9),
-    )(source, *arrays)
+    )(source, *arrays, *ahead)
 
 
 def my_quarter(shard):
@@ -2154,6 +2165,7 @@
         out_down,
         in_down,
         out_up,
+        source,
     )
     d_rows_part = d_rows_part.reshape(trees, 2, seg_len, width)
     out_part = out_part.reshape(trees, 2, seg_len, width)
@@ -2220,18 +2232,16 @@
         columns(
             [
                 g_down_mid,
+                g_down_memory,
                 g_down_seven,
                 g_up_mid,
+                g_up_memory,
                 g_up_seven,
                 g_in_down[:, None],
                 g_out_up[:, None],
             ]
         ),
         ROWS,
-    )
-
-    grad_in_up, grad_out_down = place_call(
-        place_hidden_kernel, source, (hidden_all,), [shaped(adapters, rank, hidden_units)] * 2
     )
 
     normed_shape = (slots, trees, seg_len, width)
@@ -2245,7 +2255,6 @@
             normed_all.reshape(normed_shape),
             inner_all,
             up_own,
-            grad_in_up,
             out_other,
         ),
         [
@@ -2254,7 +2263,6 @@
             slots_spec(normed_shape),
             slots_spec(inner_all.shape),
             tree_spec(up_own.shape),
-            ahead,
             ahead,
         ],
         [
@@ -2269,10 +2277,16 @@
         ],
         28,
     )
-    late = summed_to_owner(columns([g_down_part, g_down_memory, g_up_memory]), ROWS)
+    late = summed_to_owner(columns([after(g_down_part, early)]), ROWS)
     enc_side, late = lax.optimization_barrier((enc_side, late))
     grad_encoder = summed_along_line(enc_side)
-    attention_all = to_everyone(jnp.concatenate([late, g_up_qkv, early], axis=1))
+    grad_in_up, grad_out_down = place_call(
+        place_hidden_kernel, source, (hidden_all,), [shaped(adapters, rank, hidden_units)] * 2,
+        (g_down_part,),
+    )
+    attention_all = to_everyone(
+        after(jnp.concatenate([late, g_up_qkv, early], axis=1), grad_in_up)
+    )
     grad_tokens = into_tokens_call(
         d_qkv, qkv_own, tokens, d_middle, norm_gains, down_qkv, up_own
     )

time: 903 us -> 886 us (0.981)
  waiting for transfers between devices: 103 us -> 85.4 us
  Pallas kernels: 677 us -> 667 us
    all_to_all x2, waiting for transfers between devices: 30.7 us -> 10.8 us  [summed_to_owner(): lax.all_to_all(parts, axes, split_axis=0, concat_axis=0, tiled=True)]
    ppermute x4, waiting for transfers between devices: 10.9 us -> 27.2 us  [swap(): return lax.ppermute(array, 'y', SWAP)]
    pallas_call x1, Pallas kernels: 221 us -> 207 us  [heads_call(): pl.pallas_call(heads_kernel, out_shape=[shaped(slots, trees * seg_len, wi...]
    all_gather x2, waiting for transfers between devices: 10.4 us -> 0.01 us  [to_everyone(): everyone = lax.all_gather(array, COPIES + ROWS, axis=0, tiled=False)]
where the time goes in v4:
time: 886 us; the launch traced here: 876 us
  Pallas kernels  667 us (75%)
  waiting for transfers between devices  85.4 us (10%)
  local copies, waits for them, and re-layouts  45.7 us (5%)
  starting transfers between devices  34.1 us (4%)
  between operations  21.9 us (2%)
  other arithmetic  16.7 us (2%)
    pallas_call x1, Pallas kernels, heads_call(): pl.pallas_call(heads_kernel, out_shape=[shaped(slots, trees * seg_len, wi...  207 us
    pallas_call x1, Pallas kernels, into_tokens_call(): pl.pallas_call(into_tokens_kernel, out_shape=shaped(*tokens.shape), in_sp...  148 us
    pallas_call x1, Pallas kernels, feed_forward(): pl.pallas_call(feed_forward_kernel, out_shape=[shaped(count, width)] * 2...  113 us
    pallas_call x4, Pallas kernels, rows_call(): pl.pallas_call(kernel, out_shape=out_shape, grid=(1,), in_specs=[whole_sp...  67.8 us
    all_gather x1, waiting for transfers between devices, gather_pair_half(): whole = lax.all_gather(quarter, ('z',) + COPIES, axis=0, tiled=True)  47.3 us
    pallas_call x1, Pallas kernels, memory_back_call(): pl.pallas_call(memory_back_kernel, out_shape=[shaped(trees, count, width)...  31.1 us
    pallas_call x2, Pallas kernels, cross_call(): pl.pallas_call(kernel, out_shape=[shaped(trees, seg_len, width)] + [shape...  29.7 us
    pallas_call x1, Pallas kernels, self_call(): pl.pallas_call(kernel, out_shape=out_shape, grid_spec=pltpu.PrefetchScala...  27.8 us
  transfers between devices with their start and end apart: 15, of which 5 were waited for; matrix products, arithmetic and copies ran while one was open for 5% of the time, Pallas kernels for 33%

profile of v4, /device:TPU:0, one launch (start us, length us, event | category | flops | bytes accessed | tf_op | source)
XLA Modules:
  0.0 875.6 jit_solution(4656211289922354483)
XLA Ops:
  22.1 207.5 %shard_map.259 = (f32[8,256,1024]{2,1,0:T(8,128)}, f32[8,2,128,48]{3,2,1,0:T(8,128)S(1)}, f32[8,3,2,128,128]{4,3,2,1,0:T(8,128)}, f32[3,1024,128]{2,1,0:T(8,128)...) custom-call(s32[2,8]{1,0:T(2,128)S(1)} %copy-done.9, s32[2,8]{1,0:T(2,128)S(1)} %copy-done.10, ...), custom_call_target="tpu_custom_call" | custom-call | flops 179999997952 | bytes 540000000 | tf_op jit(solution)/shard_map/pallas_call | solution.py:919
  231.9 9.1 %collective-permute-start.2 = (f32[256,1024]{1,0:T(8,128)}, f32[256,1024]{1,0:T(8,128)}, u32[]{:S(2)}, u32[]{:S(2)}) collective-permute-start(f32[256,1024]{1,0:T(8,128)} %get-tuple-element.65), channel_id=1, source_target_pairs={{0,2},{2,4},{4,6},{1,3},{3,5},{5,7},{8,10},{10,12},{12,14},{9,11},... | collective-permute-start | bytes 3145736 | tf_op jit(solution)/shard_map/ppermute | solution.py:2129
  249.4 22.3 %shard_map.261.key_ref.value_ref = f32[2,512,2048]{2,1,0:T(8,128)} custom-call(f32[2,512,1024]{2,1,0:T(8,128)} %encoder_ref.3, f32[8,4,160,1024]{3,2,1,0:T(8,128)} %get-tuple-element.58.out_ref.query_ref.weight_ref, bf16[2,8,16,1024]{3,2,1,0:T(8,128)(2,1)} %get-tuple-element.124.down_ref, bf16[2,8,16,1024]{3,2,1,0:T(8,128)(2,1)} %get-tuple-element.125.up_ref), custom_call_target="tpu_custom_call" | custom-call | flops 22000001024 | bytes 66000000 | tf_op jit(solution)/shard_map/pallas_call | solution.py:1400
  273.3 11.1 %shard_map.260 = (f32[2,128,1024]{2,1,0:T(8,128)}, f32[2,128,1024]{2,1,0:T(8,128)}) custom-call(f32[8,2,128,128]{3,2,1,0:T(8,128)} %copy-done, f32[2,128,1024]{2,1,0:T(8,128)} %tokens_ref.5, f32[3,1024]{1,0:T(4,128)} %gains_ref.11, f32[8,4,160,1024]{3,2,1,0:T(8,128)} %get-tuple-element.58.out_ref.query_ref.weight_ref, ...), custom_call_target="tpu_custom_call" | custom-call | flops 10000000000 | bytes 30000000 | tf_op jit(solution)/shard_map/pallas_call | solution.py:1354
  285.6 10.4 %shard_map.262.context_ref = f32[2,128,1024]{2,1,0:T(8,128)S(1)} custom-call(f32[2,128,1024]{2,1,0:T(8,128)S(1)} %copy-done.7, f32[2,512,2048]{2,1,0:T(8,128)} %shard_map.261.key_ref.value_ref, f32[2,512,2048]{2,1,0:T(8,128)} %shard_map.261.key_ref.value_ref, f32[2,128,1024]{2,1,0:T(8,128)S(1)} %collective-permute-done._), custom_call_target="tpu_custom_call" | custom-call | flops 19000000512 | bytes 57000000 | tf_op jit(solution)/shard_map/pallas_call | solution.py:1149
  297.0 7.2 shard_map.263
  305.5 4.7 all-reduce
  311.8 4.3 dynamic-slice_reduce_fusion
  322.4 7.0 collective-permute-done.1
  332.4 47.3 %all-gather.5.cloned.1.call-done = f32[4096,1024]{1,0:T(8,128)} async-done(((f32[256,1024]{1,0:T(8,128)}), f32[4096,1024]{1,0:T(8,128)}) %all-gather.5.cloned.1.call-update) | async-done | bytes 16777232 | tf_op jit(solution)/shard_map/all_gather | solution.py:2019
  379.7 113.2 %shard_map.264 = (f32[512,1024]{1,0:T(8,128)}, f32[512,1024]{1,0:T(8,128)}, f32[2,8,16,512]{3,2,1,0:T(8,128)}, f32[2,8,16,512]{3,2,1,0:T(8,128)}, f32[2,16,1024]{2,1,0:T(8,128)}, /*index=5*/f32[2,16,1024]{2,1,0:T(8,128)}) custom-call(f32[512,1024]{1,0:T(8,128)} %bitcast.150, f32[512,1024]{1,0:T(8,128)} %bitcast.149, f32[4,1024,1024]{2,1,0:T(8,128)} %bitcast.169, ...), custom_call_target="tpu_custom_call" | custom-call | flops 109999996928 | bytes 330000000 | tf_op jit(solution)/shard_map/pallas_call | solution.py:1787
  493.0 36.9 %shard_map.265 = (f32[2,128,1024]{2,1,0:T(8,128)}, f32[2,128,1024]{2,1,0:T(8,128)}, f32[2,1,16,1024]{3,2,1,0:T(8,128)}, f32[2,1,16,1024]{3,2,1,0:T(8,128)}, f32[2,2,16,1024]{3,2,1,0:T(8,128)}) custom-call(f32[2,2,128,1024]{3,2,1,0:T(8,128)} %bitcast.175, f32[2,128,1024]{2,1,0:T(8,128)} %get-tuple-element.61.after_ref, f32[2,128,1024]{2,1,0:T(8,128)} %cotangent_ref.1, ...), custom_call_target="tpu_custom_call" | custom-call | flops 10000000000 | bytes 30000000 | tf_op jit(solution)/shard_map/pallas_call | solution.py:1354
  531.2 19.3 %shard_map.266 = (f32[2,128,1024]{2,1,0:T(8,128)S(1)}, f32[2,512,1024]{2,1,0:T(8,128)}, f32[2,512,1024]{2,1,0:T(8,128)}) custom-call(f32[2,128,1024]{2,1,0:T(8,128)S(1)} %copy-done.8, f32[2,512,2048]{2,1,0:T(8,128)} %shard_map.261.key_ref.value_ref, f32[2,512,2048]{2,1,0:T(8,128)} %shard_map.261.key_ref.value_ref, f32[2,128,1024]{2,1,0:T(8,128)S(1)} %copy-done.13), custom_call_target="tpu_custom_call" | custom-call | flops 32000000000 | bytes 96000000 | tf_op jit(solution)/shard_map/pallas_call | solution.py:1149
  551.4 12.6 %shard_map.267 = (f32[2,128,1024]{2,1,0:T(8,128)}, f32[8,2,128,128]{3,2,1,0:T(8,128)}, f32[2,2,16,1024]{3,2,1,0:T(8,128)}, f32[2,2,16,1024]{3,2,1,0:T(8,128)}) custom-call(f32[2,128,1024]{2,1,0:T(8,128)} %copy-done.2, f32[2,128,1024]{2,1,0:T(8,128)} %get-tuple-element.73.d_after_ref, f32[2,128,1024]{2,1,0:T(8,128)} %get-tuple-element.60.middle_ref, ...), custom_call_target="tpu_custom_call" | custom-call | flops 10000000000 | bytes 30000000 | tf_op jit(solution)/shard_map/pallas_call | solution.py:1354
  564.0 4.8 all-to-all-start
  571.8 31.1 %shard_map.270 = (f32[2,512,1024]{2,1,0:T(8,128)}, f32[2,2,16,1024]{3,2,1,0:T(8,128)}, f32[2,2,16,1024]{3,2,1,0:T(8,128)}) custom-call(f32[2,512,1024]{2,1,0:T(8,128)} %encoder_ref.3, f32[2,512,1024]{2,1,0:T(8,128)} %get-tuple-element.81.d_key_ref, f32[2,512,1024]{2,1,0:T(8,128)} %get-tuple-element.82.d_value_ref, ...), custom_call_target="tpu_custom_call" | custom-call | flops 31000000512 | bytes 93000000 | tf_op jit(solution)/shard_map/pallas_call | solution.py:1480
  610.5 4.6 all-to-all-start.1
  621.0 27.8 %shard_map.268 = (f32[8,3,2,128,128]{4,3,2,1,0:T(8,128)}, f32[2,3,16,1024]{3,2,1,0:T(8,128)}, f32[2,3,16,128]{3,2,1,0:T(8,128)}) custom-call(s32[2,8]{1,0:T(2,128)} %order_ref.3, s32[2,8]{1,0:T(2,128)} %parents_ref.3, f32[8,3,2,128,128]{4,3,2,1,0:T(8,128)} %get-tuple-element.72.qkv_ref, f32[8,2,128,128]{3,2,1,0:T(8,128)} %all-to-all-done.d_context_ref, ...), custom_call_target="tpu_custom_call" | custom-call | flops 28000000000 | bytes 84000000 | tf_op jit(solution)/shard_map/pallas_call | solution.py:1103
  648.8 10.8 %all-to-all-done.1 = f32[8,2,12,16,128]{4,3,2,1,0:T(8,128)S(1)} async-done(((f32[8,2,12,16,128]{4,3,2,1,0:T(8,128)}), f32[8,2,12,16,128]{4,3,2,1,0:T(8,128)S(1)}, u32[]{:S(2)}, u32[]{:S(2)}) %all-to-all-start.1) | async-done | bytes 1572896 | tf_op jit(solution)/shard_map/all_to_all | solution.py:2041
  662.7 3.6 all-to-all-start.2
  666.4 19.4 %collective-permute-done.5 = f32[4,2,64,1024]{3,2,0,1:T(8,128)} collective-permute-done((f32[4,2,64,1024]{3,2,0,1:T(8,128)}, f32[4,2,64,1024]{3,2,0,1:T(8,128)}, u32[]{:S(2)}, u32[]{:S(2)}) %collective-permute-start.5) | collective-permute-done | bytes 2097184 | tf_op jit(solution)/shard_map/ppermute | solution.py:2037
  689.1 9.5 %shard_map.271 = (f32[8,16,8192]{2,1,0:T(8,128)}, f32[8,16,8192]{2,1,0:T(8,128)}) custom-call(s32[8]{0:T(128)S(1)} %copy-done.11, f32[4,8,2,2,16,1024]{5,4,3,2,1,0:T(8,128)} %bitcast.171, f32[2,3,16,1024]{3,2,1,0:T(8,128)S(1)} %copy-done.3), custom_call_target="tpu_custom_call" | custom-call | flops 8999999488 | bytes 27000000 | tf_op jit(solution)/shard_map/pallas_call | solution.py:1998
  708.7 147.9 %shard_map.269 = f32[2,128,1024]{2,1,0:T(8,128)} custom-call(f32[8,3,2,128,128]{4,3,2,1,0:T(8,128)} %get-tuple-element.77.d_qkv_ref, f32[3,1024,128]{2,1,0:T(8,128)} %copy-done.15, f32[2,128,1024]{2,1,0:T(8,128)} %tokens_ref.5, f32[2,128,1024]{2,1,0:T(8,128)} %get-tuple-element.79.d_middle_ref, f32[3,1024]{1,0:T(4,128)} %gains_ref.11, ...), custom_call_target="tpu_custom_call" | custom-call | flops 109999996928 | bytes 330000000 | tf_op jit(solution)/shard_map/pallas_call | solution.py:1954
  857.6 10.3 %shard_map.272 = (f32[8,8,16,1024]{3,2,1,0:T(8,128)}, f32[8,8,16,1024]{3,2,1,0:T(8,128)}, f32[8,16,1024]{2,1,0:T(8,128)}, f32[8,16,1024]{2,1,0:T(8,128)}) custom-call(s32[8]{0:T(128)S(1)} %copy-done.11, f32[4,8,2,18,16,128]{5,4,3,2,1,0:T(8,128)} %bitcast.170), custom_call_target="tpu_custom_call" | custom-call | flops 8999999488 | bytes 27000000 | tf_op jit(solution)/shard_map/pallas_call | solution.py:1998
  (175 shorter events, 70.9 us)
Async XLA Ops:
  7.2 372.5 %all-gather.5.cloned.1.call-start = ((), (), s32[]{:S(2)}) async-start(), calls=%async_computation.3 | async-start | bytes 17825792 | tf_op jit(solution)/shard_map/all_gather | solution.py:2019
  22.1 221.5 %copy-start.16 = (f32[2,128,1024]{2,1,0:T(8,128)S(1)}, f32[2,128,1024]{2,1,0:T(8,128)}, u32[]{:S(2)}) copy-start(f32[2,128,1024]{2,1,0:T(8,128)} %cotangent_ref.1) | copy-start | bytes 3145732
  231.8 14.8 %copy-start = (f32[8,2,128,128]{3,2,1,0:T(8,128)}, f32[8,2,128,128]{3,2,1,0:T(8,128)S(1)}, u32[]{:S(2)}) copy-start(f32[8,2,128,128]{3,2,1,0:T(8,128)S(1)} %get-tuple-element.57.context_ref) | copy-start | bytes 3145732
  231.8 457.3 %all-gather.9.cloned.1.call-start = ((), (), s32[]{:S(2)}) async-start(), calls=%async_computation.5 | async-start | bytes 8650752 | tf_op jit(solution)/shard_map/all_gather | solution.py:2057
  231.9 100.5 %collective-permute-start.2 = (f32[256,1024]{1,0:T(8,128)}, f32[256,1024]{1,0:T(8,128)}, u32[]{:S(2)}, u32[]{:S(2)}) collective-permute-start(f32[256,1024]{1,0:T(8,128)} %get-tuple-element.65), channel_id=1, source_target_pairs={{0,2},{2,4},{4,6},{1,3},{3,5},{5,7},{8,10},{10,12},{12,14},{9,11},... | collective-permute-start | bytes 3145736 | tf_op jit(solution)/shard_map/ppermute | solution.py:2129
  241.0 91.4 %collective-permute-start.3 = (f32[256,1024]{1,0:T(8,128)}, f32[256,1024]{1,0:T(8,128)}, u32[]{:S(2)}, u32[]{:S(2)}) collective-permute-start(f32[256,1024]{1,0:T(8,128)} %get-tuple-element.65), channel_id=1, source_target_pairs={{2,0},{4,2},{6,4},{3,1},{5,3},{7,5},{10,8},{12,10},{14,12},{11,9},... | collective-permute-start | bytes 3145736 | tf_op jit(solution)/shard_map/ppermute | solution.py:2130
  244.7 39.7 %collective-permute-start = (f32[2,128,1024]{2,1,0:T(8,128)}, f32[2,128,1024]{2,1,0:T(8,128)S(1)}, u32[]{:S(2)}, u32[]{:S(2)}) collective-permute-start(f32[2,128,1024]{2,1,0:T(8,128)} %broadcast_add_fusion), channel_id=1, source_target_pairs={{0,1},{1,0},{2,3},{3,2},{4,5},{5,4},{6,7},{7,6},{8,9},{9,8},{10,11... | collective-permute-start | bytes 3145736 | tf_op jit(solution)/shard_map/ppermute | solution.py:2037
  249.4 22.4 %copy-start.44 = (u32[32]{0:T(128)S(1)}, u32[32]{0:T(128)}, u32[]{:S(2)}) copy-start(u32[32]{0:T(128)} %constant.100) | copy-start | bytes 388
  249.4 23.7 %copy-start.43 = (s32[2]{0:T(128)S(1)}, s32[2]{0:T(128)}, u32[]{:S(2)}) copy-start(s32[2]{0:T(128)} %param.23) | copy-start | bytes 28
  304.2 25.2 %collective-permute-start.1 = (f32[2,128,1024]{2,1,0:T(8,128)}, f32[2,128,1024]{2,1,0:T(8,128)}, u32[]{:S(2)}, u32[]{:S(2)}) collective-permute-start(f32[2,128,1024]{2,1,0:T(8,128)} %get-tuple-element.62), channel_id=1, source_target_pairs={{0,1},{1,0},{2,3},{3,2},{4,5},{5,4},{6,7},{7,6},{8,9},{9,8},{10,11... | collective-permute-start | bytes 3145736 | tf_op jit(solution)/shard_map/ppermute | solution.py:2037
  492.9 37.0 %copy-start.8 = (f32[2,128,1024]{2,1,0:T(8,128)S(1)}, f32[2,128,1024]{2,1,0:T(8,128)}, u32[]{:S(2)}) copy-start(f32[2,128,1024]{2,1,0:T(8,128)} %get-tuple-element.59.query_ref) | copy-start | bytes 3145732
  564.0 46.4 %all-to-all-start = ((f32[8,2,128,128]{3,2,1,0:T(8,128)}), f32[8,2,128,128]{3,2,1,0:T(8,128)}, u32[]{:S(2)}, u32[]{:S(2)}) async-start(f32[8,2,128,128]{3,2,1,0:T(8,128)} %get-tuple-element.74), calls=%async_computation | async-start | bytes 2097152 | tf_op jit(solution)/shard_map/all_to_all | solution.py:2221
  569.6 51.4 %collective-permute-start.4 = (f32[2,128,1024]{2,1,0:T(8,128)S(1)}, f32[2,128,1024]{2,1,0:T(8,128)}, u32[]{:S(2)}, u32[]{:S(2)}) collective-permute-start(f32[2,128,1024]{2,1,0:T(8,128)S(1)} %fusion.1), channel_id=1, source_target_pairs={{0,1},{1,0},{2,3},{3,2},{4,5},{5,4},{6,7},{7,6},{8,9},{9,8},{10,11... | collective-permute-start | bytes 3145736 | tf_op jit(solution)/shard_map/ppermute | solution.py:2037
  571.8 31.1 %copy-start.36 = (f32[2,2,16,1024]{3,2,1,0:T(8,128)S(1)}, f32[2,2,16,1024]{3,2,1,0:T(8,128)}, u32[]{:S(2)}) copy-start(f32[2,2,16,1024]{3,2,1,0:T(8,128)} %get-tuple-element.85) | copy-start | bytes 786436
  571.8 34.2 %copy-start.35 = (f32[2,2,16,1024]{3,2,1,0:T(8,128)S(1)}, f32[2,2,16,1024]{3,2,1,0:T(8,128)}, u32[]{:S(2)}) copy-start(f32[2,2,16,1024]{3,2,1,0:T(8,128)} %get-tuple-element.88) | copy-start | bytes 786436
  610.5 49.1 %all-to-all-start.1 = ((f32[8,2,12,16,128]{4,3,2,1,0:T(8,128)}), f32[8,2,12,16,128]{4,3,2,1,0:T(8,128)S(1)}, u32[]{:S(2)}, u32[]{:S(2)}) async-start(f32[8,2,12,16,128]{4,3,2,1,0:T(8,128)} %bitcast.37), calls=%async_computation.1 | async-start | bytes 3145728 | tf_op jit(solution)/shard_map/all_to_all | solution.py:2041
  618.4 67.5 %collective-permute-start.5 = (f32[4,2,64,1024]{3,2,0,1:T(8,128)}, f32[4,2,64,1024]{3,2,0,1:T(8,128)}, u32[]{:S(2)}, u32[]{:S(2)}) collective-permute-start(f32[4,2,64,1024]{3,2,0,1:T(8,128)} %dynamic-slice_bitcast_fusion), channel_id=1, source_target_pairs={{0,1},{1,0},{2,3},{3,2},{4,5},{5,4},{6,7},{7,6},{8,9},{9,8},{10,11... | collective-permute-start | bytes 6291464 | tf_op jit(solution)/shard_map/ppermute | solution.py:2037
  662.7 25.7 %all-to-all-start.2 = ((f32[8,2,3,16,128]{4,3,2,1,0:T(8,128)}), f32[8,2,3,16,128]{4,3,2,1,0:T(8,128)S(1)}, u32[]{:S(2)}, u32[]{:S(2)}) async-start(f32[8,2,3,16,128]{4,3,2,1,0:T(8,128)} %bitcast_bitcast_fusion), calls=%async_computation.2 | async-start | bytes 786432 | tf_op jit(solution)/shard_map/all_to_all | solution.py:2041
  666.3 22.7 %copy-start.3 = (f32[2,3,16,1024]{3,2,1,0:T(8,128)S(1)}, f32[2,3,16,1024]{3,2,1,0:T(8,128)}, u32[]{:S(2)}) copy-start(f32[2,3,16,1024]{3,2,1,0:T(8,128)} %get-tuple-element.84._) | copy-start | bytes 1179652
  666.4 22.7 %copy-start.11 = (s32[8]{0:T(128)S(1)}, s32[8]{0:T(128)}, u32[]{:S(2)}) copy-start(s32[8]{0:T(128)} %select_reduce_fusion._.source_ref) | copy-start | bytes 100
  666.4 191.3 %all-gather.7.cloned.1.call-start = ((), (), s32[]{:S(2)}) async-start(), calls=%async_computation.4 | async-start | bytes 9732096 | tf_op jit(solution)/shard_map/all_gather | solution.py:2057
  704.2 152.4 %collective-permute-start.6 = (f32[2,64,1024]{2,1,0:T(8,128)S(1)}, f32[2,64,1024]{2,1,0:T(8,128)S(1)}, u32[]{:S(2)}, u32[]{:S(2)}) collective-permute-start(f32[2,64,1024]{2,1,0:T(8,128)S(1)} %get-tuple-element.103), channel_id=1, source_target_pairs={{0,2},{2,0},{4,6},{6,4},{1,3},{3,1},{5,7},{7,5},{8,10},{10,8},{12,... | collective-permute-start | bytes 1572872 | tf_op jit(solution)/shard_map/ppermute | solution.py:2050
  705.8 150.9 %collective-permute-start.7 = (f32[2,64,1024]{2,1,0:T(8,128)S(1)}, f32[2,64,1024]{2,1,0:T(8,128)S(1)}, u32[]{:S(2)}, u32[]{:S(2)}) collective-permute-start(f32[2,64,1024]{2,1,0:T(8,128)S(1)} %get-tuple-element.105), channel_id=1, source_target_pairs={{0,4},{2,6},{4,0},{6,2},{1,5},{3,7},{5,1},{7,3},{8,12},{10,14},{12... | collective-permute-start | bytes 1572872 | tf_op jit(solution)/shard_map/ppermute | solution.py:2050
  708.2 148.4 %collective-permute-start.8 = (f32[2,64,1024]{2,1,0:T(8,128)S(1)}, f32[2,64,1024]{2,1,0:T(8,128)S(1)}, u32[]{:S(2)}, u32[]{:S(2)}) collective-permute-start(f32[2,64,1024]{2,1,0:T(8,128)S(1)} %get-tuple-element.104), channel_id=1, source_target_pairs={{0,6},{2,4},{4,2},{6,0},{1,7},{3,5},{5,3},{7,1},{8,14},{10,12},{12... | collective-permute-start | bytes 1572872 | tf_op jit(solution)/shard_map/ppermute | solution.py:2050
  (36 other events, 212.1 us)
Sparse Core Ops, SparseCore 0:
  231.9 147.7 all-gather.4
  530.0 101.2 all-gather.8
  701.4 138.9 all-gather.6

commit v5 on v4

--- a/solution.py
+++ b/solution.py
@@ -542,12 +542,15 @@
     shard_ref,
     down_ref,
     up_ref,
+    quarter_ref,
     normed_ref,
     inner_ref,
     qkv_ref,
     own_weight_ref,
     packed_ref,
     context_ref,
+    below_ref,
+    above_ref,
     own_context_ref,
     rows_ref,
     blocks_ref,
@@ -572,6 +575,8 @@
     core_here_sem,
     context_sem,
     context_here_sem,
+    near_sem,
+    near_here_sem,
 ):
     x, c = lax.axis_index("x"), lax.axis_index("c")
     z, y = lax.axis_index("z"), lax.axis_index("y")
@@ -858,6 +863,25 @@
     for hop in range(3, last + 1):
         levels_at(hop, first_by_line)
         levels_at(hop, second_by_line)
+
+    def to_above():
+        return remote(
+            quarter_ref, below_ref, near_sem.at[0], near_here_sem.at[0], {"z": z + 1}
+        )
+
+    def to_below():
+        return remote(
+            quarter_ref, above_ref, near_sem.at[1], near_here_sem.at[1], {"z": z - 1}
+        )
+
+    @pl.when(z < last)
+    def _():
+        to_above().start()
+
+    @pl.when(z > 0)
+    def _():
+        to_below().start()
+
     faced_at(1)
     for hop in range(2, last + 1):
         levels_at(hop, first_over)
@@ -865,6 +889,16 @@
         faced_at(hop)
     for hop in range(last + 1):
         levels_at(hop, lambda level: faced(0, place(level, 1 - y)))
+
+    @pl.when(z < last)
+    def _():
+        to_above().wait_send()
+        to_below().wait_recv()
+
+    @pl.when(z > 0)
+    def _():
+        to_below().wait_send()
+        to_above().wait_recv()
 
     context_keep().wait()
     for step in range(1, slots):
@@ -907,7 +941,7 @@
         keep(slot).wait()
 
 
-def heads_call(order, parents, tokens, gains, weight, shard, down, up):
+def heads_call(order, parents, tokens, gains, weight, shard, down, up, quarter):
     trees, seg_len, width = tokens.shape
     slots = lax.axis_size(ROWS)
     lanes = weight.shape[1] // 3
@@ -925,9 +959,11 @@
             shaped(3, width, lanes),
             shaped(slots, *shard.shape),
             shaped(slots, trees, seg_len, lanes),
+            shaped(*quarter.shape),
+            shaped(*quarter.shape),
         ],
-        in_specs=[scalars, scalars, here, here, there, there, here, here],
-        out_specs=[there, here, here, there, there, there],
+        in_specs=[scalars, scalars, here, here, there, there, here, here, there],
+        out_specs=[there, here, here] + [there] * 5,
         scratch_shapes=[
             pltpu.VMEM((slots, trees, seg_len, lanes), F32),
             pltpu.VMEM((slots, trees * seg_len, width), F32),
@@ -940,12 +976,13 @@
         + [dma((slots,))] * 4
         + [dma((2, slots))] * 6
         + [dma((4, slots))] * 2
-        + [dma((slots,))] * 2,
+        + [dma((slots,))] * 2
+        + [dma((2,))] * 2,
         compiler_params=pltpu.CompilerParams(
             vmem_limit_bytes=48 * MIB, collective_id=0, has_side_effects=True
         ),
         cost_estimate=lasting(180),
-    )(order, parents, tokens, gains, weight, shard, down, up)
+    )(order, parents, tokens, gains, weight, shard, down, up, quarter)
 
 
 def ancestor_slots(order_ref, parents_ref, slot_of, tree, slot, depth=4):
@@ -2113,8 +2150,16 @@
         ],
         axis=1,
     )
-    normed_all, inner_all, qkv, qkv_own, packed, context = heads_call(
-        segment_order, parents, tokens, norm_gains, w_qkv, shard, down_qkv, up_own
+    normed_all, inner_all, qkv, qkv_own, packed, context, *fc_out_near = heads_call(
+        segment_order,
+        parents,
+        tokens,
+        norm_gains,
+        w_qkv,
+        shard,
+        down_qkv,
+        up_own,
+        my_quarter(w_fc_out),
     )
     row = width // (slots * copies)
     self_out_spec = packed_spec(packed, 2 * row, row)
@@ -2123,13 +2168,7 @@
 
     fc_in_late, qkv = lax.optimization_barrier((my_quarter(w_fc_in), qkv))
     fc_in_half = gather_pair_half(fc_in_late, w_fc_in.shape)
-    fc_out_late, context = lax.optimization_barrier((my_quarter(w_fc_out), context))
     levels = range(lax.axis_size("z") - 1)
-    fc_out_near = (
-        lax.ppermute(fc_out_late, "z", [(level, level + 1) for level in levels]),
-        lax.ppermute(fc_out_late, "z", [(level + 1, level) for level in levels]),
-    )
-
     cotangent_other = swap(after(cotangent, context))
     memory = memory_call(encoder, packed, down, up)
     middle, cross_queries = rows_call(

time: 886 us -> 868 us (0.980)
  starting transfers between devices: 34.1 us -> 23.5 us
  waiting for transfers between devices: 85.4 us -> 76 us
    ppermute x2 -> x0, starting transfers between devices: 10.6 us -> none  [the longest x1 9.12 us: by_heads(): lax.ppermute(fc_out_late, 'z', [(level, level + 1) for level in levels])]
    all_gather x1, waiting for transfers between devices: 47.3 us -> 38.4 us  [gather_pair_half(): whole = lax.all_gather(quarter, ('z',) + COPIES, axis=0, tiled=True)]
  transfers between devices with their start and end apart: 15 -> 13, of which waited for: 5 -> 5; matrix products, arithmetic and copies ran while one was open for 5% -> 5% of each run, Pallas kernels for 33% -> 34%
where the time goes in v5:
time: 868 us; the launch traced here: 858 us
  Pallas kernels  669 us (77%)
  waiting for transfers between devices  76 us (9%)
  local copies, waits for them, and re-layouts  46.5 us (5%)
  starting transfers between devices  23.5 us (3%)
  between operations  22.1 us (3%)
  other arithmetic  16.7 us (2%)
    pallas_call x1, Pallas kernels, heads_call(): pl.pallas_call(heads_kernel, out_shape=[shaped(slots, trees * seg_len, wi...  207 us
    pallas_call x1, Pallas kernels, into_tokens_call(): pl.pallas_call(into_tokens_kernel, out_shape=shaped(*tokens.shape), in_sp...  148 us
    pallas_call x1, Pallas kernels, feed_forward(): pl.pallas_call(feed_forward_kernel, out_shape=[shaped(count, width)] * 2...  113 us
    pallas_call x4, Pallas kernels, rows_call(): pl.pallas_call(kernel, out_shape=out_shape, grid=(1,), in_specs=[whole_sp...  69.4 us
    all_gather x1, waiting for transfers between devices, gather_pair_half(): whole = lax.all_gather(quarter, ('z',) + COPIES, axis=0, tiled=True)  38.4 us
    pallas_call x1, Pallas kernels, memory_back_call(): pl.pallas_call(memory_back_kernel, out_shape=[shaped(trees, count, width)...  31.1 us
    pallas_call x2, Pallas kernels, cross_call(): pl.pallas_call(kernel, out_shape=[shaped(trees, seg_len, width)] + [shape...  29.7 us
    pallas_call x1, Pallas kernels, self_call(): pl.pallas_call(kernel, out_shape=out_shape, grid_spec=pltpu.PrefetchScala...  27.9 us
  transfers between devices with their start and end apart: 13, of which 5 were waited for; matrix products, arithmetic and copies ran while one was open for 5% of the time, Pallas kernels for 34%

profile of v5, /device:TPU:0, one launch (start us, length us, event | category | flops | bytes accessed | tf_op | source)
XLA Modules:
  0.0 858.5 jit_solution(11758989740303522701)
XLA Ops:
  22.1 207.5 %shard_map.259 = (f32[8,256,1024]{2,1,0:T(8,128)}, f32[8,2,128,48]{3,2,1,0:T(8,128)S(1)}, f32[8,3,2,128,128]{4,3,2,1,0:T(8,128)}, f32[3,1024,128]{2,1,0:T(8,128)...) custom-call(s32[2,8]{1,0:T(2,128)S(1)} %copy-done.9, ...), custom_call_target="tpu_custom_call" | custom-call | flops 179999997952 | bytes 540000000 | tf_op jit(solution)/shard_map/pallas_call | solution.py:953
  239.0 22.3 %shard_map.261.key_ref.value_ref = f32[2,512,2048]{2,1,0:T(8,128)} custom-call(f32[2,512,1024]{2,1,0:T(8,128)} %encoder_ref.3, f32[8,4,160,1024]{3,2,1,0:T(8,128)} %get-tuple-element.57.out_ref.query_ref.weight_ref, bf16[2,8,16,1024]{3,2,1,0:T(8,128)(2,1)} %get-tuple-element.124.down_ref, bf16[2,8,16,1024]{3,2,1,0:T(8,128)(2,1)} %get-tuple-element.125.up_ref), custom_call_target="tpu_custom_call" | custom-call | flops 22000001024 | bytes 66000000 | tf_op jit(solution)/shard_map/pallas_call | solution.py:1437
  262.9 11.2 %shard_map.260 = (f32[2,128,1024]{2,1,0:T(8,128)}, f32[2,128,1024]{2,1,0:T(8,128)}) custom-call(f32[8,2,128,128]{3,2,1,0:T(8,128)} %copy-done, f32[2,128,1024]{2,1,0:T(8,128)} %tokens_ref.5, f32[3,1024]{1,0:T(4,128)} %gains_ref.11, f32[8,4,160,1024]{3,2,1,0:T(8,128)} %get-tuple-element.57.out_ref.query_ref.weight_ref, ...), custom_call_target="tpu_custom_call" | custom-call | flops 10000000000 | bytes 30000000 | tf_op jit(solution)/shard_map/pallas_call | solution.py:1391
  275.3 10.4 %shard_map.262.context_ref = f32[2,128,1024]{2,1,0:T(8,128)S(1)} custom-call(f32[2,128,1024]{2,1,0:T(8,128)S(1)} %copy-done.7, f32[2,512,2048]{2,1,0:T(8,128)} %shard_map.261.key_ref.value_ref, f32[2,512,2048]{2,1,0:T(8,128)} %shard_map.261.key_ref.value_ref, f32[2,128,1024]{2,1,0:T(8,128)S(1)} %collective-permute-done._), custom_call_target="tpu_custom_call" | custom-call | flops 19000000512 | bytes 57000000 | tf_op jit(solution)/shard_map/pallas_call | solution.py:1186
  286.8 8.7 %shard_map.263 = (f32[2,128,1024]{2,1,0:T(8,128)}, f32[2,128,1024]{2,1,0:T(8,128)}) custom-call(f32[2,128,1024]{2,1,0:T(8,128)} %copy-done.12, f32[2,128,1024]{2,1,0:T(8,128)} %get-tuple-element.59.middle_ref, f32[3,1024]{1,0:T(4,128)} %gains_ref.11, f32[8,4,160,1024]{3,2,1,0:T(8,128)} %get-tuple-element.57.out_ref.query_ref.weight_ref, ...), custom_call_target="tpu_custom_call" | custom-call | flops 10000000000 | bytes 30000000 | tf_op jit(solution)/shard_map/pallas_call | solution.py:1391
  297.5 4.8 all-reduce
  303.8 4.3 dynamic-slice_reduce_fusion
  314.5 6.7 collective-permute-done.1
  324.1 38.4 %all-gather.5.cloned.1.call-done = f32[4096,1024]{1,0:T(8,128)} async-done(((f32[256,1024]{1,0:T(8,128)}), f32[4096,1024]{1,0:T(8,128)}) %all-gather.5.cloned.1.call-update) | async-done | bytes 16777232 | tf_op jit(solution)/shard_map/all_gather | solution.py:2056
  362.5 113.3 %shard_map.264 = (f32[512,1024]{1,0:T(8,128)}, f32[512,1024]{1,0:T(8,128)}, f32[2,8,16,512]{3,2,1,0:T(8,128)}, f32[2,8,16,512]{3,2,1,0:T(8,128)}, f32[2,16,1024]{2,1,0:T(8,128)}, /*index=5*/f32[2,16,1024]{2,1,0:T(8,128)}) custom-call(f32[512,1024]{1,0:T(8,128)} %bitcast.150, f32[512,1024]{1,0:T(8,128)} %bitcast.149, f32[4,1024,1024]{2,1,0:T(8,128)} %bitcast.169, ...), custom_call_target="tpu_custom_call" | custom-call | flops 109999996928 | bytes 330000000 | tf_op jit(solution)/shard_map/pallas_call | solution.py:1824
  475.8 36.9 %shard_map.265 = (f32[2,128,1024]{2,1,0:T(8,128)}, f32[2,128,1024]{2,1,0:T(8,128)}, f32[2,1,16,1024]{3,2,1,0:T(8,128)}, f32[2,1,16,1024]{3,2,1,0:T(8,128)}, f32[2,2,16,1024]{3,2,1,0:T(8,128)}) custom-call(f32[2,2,128,1024]{3,2,1,0:T(8,128)} %bitcast.175, f32[2,128,1024]{2,1,0:T(8,128)} %get-tuple-element.60.after_ref, f32[2,128,1024]{2,1,0:T(8,128)} %cotangent_ref.1, ...), custom_call_target="tpu_custom_call" | custom-call | flops 10000000000 | bytes 30000000 | tf_op jit(solution)/shard_map/pallas_call | solution.py:1391
  514.0 19.2 %shard_map.266 = (f32[2,128,1024]{2,1,0:T(8,128)S(1)}, f32[2,512,1024]{2,1,0:T(8,128)}, f32[2,512,1024]{2,1,0:T(8,128)}) custom-call(f32[2,128,1024]{2,1,0:T(8,128)S(1)} %copy-done.8, f32[2,512,2048]{2,1,0:T(8,128)} %shard_map.261.key_ref.value_ref, f32[2,512,2048]{2,1,0:T(8,128)} %shard_map.261.key_ref.value_ref, f32[2,128,1024]{2,1,0:T(8,128)S(1)} %copy-done.13), custom_call_target="tpu_custom_call" | custom-call | flops 32000000000 | bytes 96000000 | tf_op jit(solution)/shard_map/pallas_call | solution.py:1186
  534.2 12.6 %shard_map.267 = (f32[2,128,1024]{2,1,0:T(8,128)}, f32[8,2,128,128]{3,2,1,0:T(8,128)}, f32[2,2,16,1024]{3,2,1,0:T(8,128)}, f32[2,2,16,1024]{3,2,1,0:T(8,128)}) custom-call(f32[2,128,1024]{2,1,0:T(8,128)} %copy-done.2, f32[2,128,1024]{2,1,0:T(8,128)} %get-tuple-element.73.d_after_ref, f32[2,128,1024]{2,1,0:T(8,128)} %get-tuple-element.59.middle_ref, ...), custom_call_target="tpu_custom_call" | custom-call | flops 10000000000 | bytes 30000000 | tf_op jit(solution)/shard_map/pallas_call | solution.py:1391
  546.8 4.6 all-to-all-start
  554.5 31.1 %shard_map.270 = (f32[2,512,1024]{2,1,0:T(8,128)}, f32[2,2,16,1024]{3,2,1,0:T(8,128)}, f32[2,2,16,1024]{3,2,1,0:T(8,128)}) custom-call(f32[2,512,1024]{2,1,0:T(8,128)} %encoder_ref.3, f32[2,512,1024]{2,1,0:T(8,128)} %get-tuple-element.81.d_key_ref, f32[2,512,1024]{2,1,0:T(8,128)} %get-tuple-element.82.d_value_ref, ...), custom_call_target="tpu_custom_call" | custom-call | flops 31000000512 | bytes 93000000 | tf_op jit(solution)/shard_map/pallas_call | solution.py:1517
  593.1 4.6 all-to-all-start.1
  597.7 3.3 dynamic-slice_bitcast_fusion
  603.7 27.9 %shard_map.268 = (f32[8,3,2,128,128]{4,3,2,1,0:T(8,128)}, f32[2,3,16,1024]{3,2,1,0:T(8,128)}, f32[2,3,16,128]{3,2,1,0:T(8,128)}) custom-call(s32[2,8]{1,0:T(2,128)} %order_ref.3, s32[2,8]{1,0:T(2,128)} %parents_ref.3, f32[8,3,2,128,128]{4,3,2,1,0:T(8,128)} %get-tuple-element.72.qkv_ref, f32[8,2,128,128]{3,2,1,0:T(8,128)} %all-to-all-done.d_context_ref, ...), custom_call_target="tpu_custom_call" | custom-call | flops 28000000000 | bytes 84000000 | tf_op jit(solution)/shard_map/pallas_call | solution.py:1140
  631.5 10.8 %all-to-all-done.1 = f32[8,2,12,16,128]{4,3,2,1,0:T(8,128)S(1)} async-done(((f32[8,2,12,16,128]{4,3,2,1,0:T(8,128)}), f32[8,2,12,16,128]{4,3,2,1,0:T(8,128)S(1)}, u32[]{:S(2)}, u32[]{:S(2)}) %all-to-all-start.1) | async-done | bytes 1572896 | tf_op jit(solution)/shard_map/all_to_all | solution.py:2078
  645.4 3.7 all-to-all-start.2
  649.2 19.3 %collective-permute-done.3 = f32[4,2,64,1024]{3,2,0,1:T(8,128)} collective-permute-done((f32[4,2,64,1024]{3,2,0,1:T(8,128)}, f32[4,2,64,1024]{3,2,0,1:T(8,128)}, u32[]{:S(2)}, u32[]{:S(2)}) %collective-permute-start.3) | collective-permute-done | bytes 2097184 | tf_op jit(solution)/shard_map/ppermute | solution.py:2074
  671.8 9.5 %shard_map.271 = (f32[8,16,8192]{2,1,0:T(8,128)}, f32[8,16,8192]{2,1,0:T(8,128)}) custom-call(s32[8]{0:T(128)S(1)} %copy-done.11, f32[4,8,2,2,16,1024]{5,4,3,2,1,0:T(8,128)} %bitcast.171, f32[2,3,16,1024]{3,2,1,0:T(8,128)S(1)} %copy-done.3), custom_call_target="tpu_custom_call" | custom-call | flops 8999999488 | bytes 27000000 | tf_op jit(solution)/shard_map/pallas_call | solution.py:2035
  691.4 147.9 %shard_map.269 = f32[2,128,1024]{2,1,0:T(8,128)} custom-call(f32[8,3,2,128,128]{4,3,2,1,0:T(8,128)} %get-tuple-element.77.d_qkv_ref, f32[3,1024,128]{2,1,0:T(8,128)} %get-tuple-element.78.weight_ref, f32[2,128,1024]{2,1,0:T(8,128)} %tokens_ref.5, f32[2,128,1024]{2,1,0:T(8,128)} %get-tuple-element.79.d_middle_ref, f32[3,1024]{1,0:T(4,128)} %gains_ref.11, ...), custom_call_target="tpu_custom_call" | custom-call | flops 109999996928 | bytes 330000000 | tf_op jit(solution)/shard_map/pallas_call | solution.py:1991
  840.3 10.3 %shard_map.272 = (f32[8,8,16,1024]{3,2,1,0:T(8,128)}, f32[8,8,16,1024]{3,2,1,0:T(8,128)}, f32[8,16,1024]{2,1,0:T(8,128)}, f32[8,16,1024]{2,1,0:T(8,128)}) custom-call(s32[8]{0:T(128)S(1)} %copy-done.11, f32[4,8,2,18,16,128]{5,4,3,2,1,0:T(8,128)} %bitcast.170), custom_call_target="tpu_custom_call" | custom-call | flops 8999999488 | bytes 27000000 | tf_op jit(solution)/shard_map/pallas_call | solution.py:2035
  (173 shorter events, 67.0 us)
Async XLA Ops:
  7.2 355.3 %all-gather.5.cloned.1.call-start = ((), (), s32[]{:S(2)}) async-start(), calls=%async_computation.3 | async-start | bytes 17825792 | tf_op jit(solution)/shard_map/all_gather | solution.py:2056
  22.1 212.0 %copy-start.17 = (f32[2,128,1024]{2,1,0:T(8,128)S(1)}, f32[2,128,1024]{2,1,0:T(8,128)}, u32[]{:S(2)}) copy-start(f32[2,128,1024]{2,1,0:T(8,128)} %cotangent_ref.1) | copy-start | bytes 3145732
  232.6 439.1 %all-gather.9.cloned.1.call-start = ((), (), s32[]{:S(2)}) async-start(), calls=%async_computation.5 | async-start | bytes 8650752 | tf_op jit(solution)/shard_map/all_gather | solution.py:2094
  235.1 39.0 %collective-permute-start = (f32[2,128,1024]{2,1,0:T(8,128)}, f32[2,128,1024]{2,1,0:T(8,128)S(1)}, u32[]{:S(2)}, u32[]{:S(2)}) collective-permute-start(f32[2,128,1024]{2,1,0:T(8,128)} %broadcast_add_fusion), channel_id=1, source_target_pairs={{0,1},{1,0},{2,3},{3,2},{4,5},{5,4},{6,7},{7,6},{8,9},{9,8},{10,11... | collective-permute-start | bytes 3145736 | tf_op jit(solution)/shard_map/ppermute | solution.py:2074
  239.0 22.4 %copy-start.45 = (u32[32]{0:T(128)S(1)}, u32[32]{0:T(128)}, u32[]{:S(2)}) copy-start(u32[32]{0:T(128)} %constant.100) | copy-start | bytes 388
  239.0 23.7 %copy-start.44 = (s32[2]{0:T(128)S(1)}, s32[2]{0:T(128)}, u32[]{:S(2)}) copy-start(s32[2]{0:T(128)} %param.23) | copy-start | bytes 28
  295.4 25.8 %collective-permute-start.1 = (f32[2,128,1024]{2,1,0:T(8,128)}, f32[2,128,1024]{2,1,0:T(8,128)}, u32[]{:S(2)}, u32[]{:S(2)}) collective-permute-start(f32[2,128,1024]{2,1,0:T(8,128)} %get-tuple-element.61), channel_id=1, source_target_pairs={{0,1},{1,0},{2,3},{3,2},{4,5},{5,4},{6,7},{7,6},{8,9},{9,8},{10,11... | collective-permute-start | bytes 3145736 | tf_op jit(solution)/shard_map/ppermute | solution.py:2074
  475.8 37.0 %copy-start.8 = (f32[2,128,1024]{2,1,0:T(8,128)S(1)}, f32[2,128,1024]{2,1,0:T(8,128)}, u32[]{:S(2)}) copy-start(f32[2,128,1024]{2,1,0:T(8,128)} %get-tuple-element.58.query_ref) | copy-start | bytes 3145732
  546.8 46.3 %all-to-all-start = ((f32[8,2,128,128]{3,2,1,0:T(8,128)}), f32[8,2,128,128]{3,2,1,0:T(8,128)}, u32[]{:S(2)}, u32[]{:S(2)}) async-start(f32[8,2,128,128]{3,2,1,0:T(8,128)} %get-tuple-element.74), calls=%async_computation | async-start | bytes 2097152 | tf_op jit(solution)/shard_map/all_to_all | solution.py:2260
  552.3 51.4 %collective-permute-start.2 = (f32[2,128,1024]{2,1,0:T(8,128)S(1)}, f32[2,128,1024]{2,1,0:T(8,128)}, u32[]{:S(2)}, u32[]{:S(2)}) collective-permute-start(f32[2,128,1024]{2,1,0:T(8,128)S(1)} %fusion.1), channel_id=1, source_target_pairs={{0,1},{1,0},{2,3},{3,2},{4,5},{5,4},{6,7},{7,6},{8,9},{9,8},{10,11... | collective-permute-start | bytes 3145736 | tf_op jit(solution)/shard_map/ppermute | solution.py:2074
  554.5 31.1 %copy-start.37 = (f32[2,2,16,1024]{3,2,1,0:T(8,128)S(1)}, f32[2,2,16,1024]{3,2,1,0:T(8,128)}, u32[]{:S(2)}) copy-start(f32[2,2,16,1024]{3,2,1,0:T(8,128)} %get-tuple-element.85) | copy-start | bytes 786436
  554.5 34.2 %copy-start.36 = (f32[2,2,16,1024]{3,2,1,0:T(8,128)S(1)}, f32[2,2,16,1024]{3,2,1,0:T(8,128)}, u32[]{:S(2)}) copy-start(f32[2,2,16,1024]{3,2,1,0:T(8,128)} %get-tuple-element.88) | copy-start | bytes 786436
  593.1 49.2 %all-to-all-start.1 = ((f32[8,2,12,16,128]{4,3,2,1,0:T(8,128)}), f32[8,2,12,16,128]{4,3,2,1,0:T(8,128)S(1)}, u32[]{:S(2)}, u32[]{:S(2)}) async-start(f32[8,2,12,16,128]{4,3,2,1,0:T(8,128)} %bitcast.37), calls=%async_computation.1 | async-start | bytes 3145728 | tf_op jit(solution)/shard_map/all_to_all | solution.py:2078
  601.0 67.5 %collective-permute-start.3 = (f32[4,2,64,1024]{3,2,0,1:T(8,128)}, f32[4,2,64,1024]{3,2,0,1:T(8,128)}, u32[]{:S(2)}, u32[]{:S(2)}) collective-permute-start(f32[4,2,64,1024]{3,2,0,1:T(8,128)} %dynamic-slice_bitcast_fusion), channel_id=1, source_target_pairs={{0,1},{1,0},{2,3},{3,2},{4,5},{5,4},{6,7},{7,6},{8,9},{9,8},{10,11... | collective-permute-start | bytes 6291464 | tf_op jit(solution)/shard_map/ppermute | solution.py:2074
  645.4 25.7 %all-to-all-start.2 = ((f32[8,2,3,16,128]{4,3,2,1,0:T(8,128)}), f32[8,2,3,16,128]{4,3,2,1,0:T(8,128)S(1)}, u32[]{:S(2)}, u32[]{:S(2)}) async-start(f32[8,2,3,16,128]{4,3,2,1,0:T(8,128)} %bitcast_bitcast_fusion), calls=%async_computation.2 | async-start | bytes 786432 | tf_op jit(solution)/shard_map/all_to_all | solution.py:2078
  649.2 22.6 %copy-start.3 = (f32[2,3,16,1024]{3,2,1,0:T(8,128)S(1)}, f32[2,3,16,1024]{3,2,1,0:T(8,128)}, u32[]{:S(2)}) copy-start(f32[2,3,16,1024]{3,2,1,0:T(8,128)} %get-tuple-element.84._) | copy-start | bytes 1179652
  649.2 22.6 %copy-start.11 = (s32[8]{0:T(128)S(1)}, s32[8]{0:T(128)}, u32[]{:S(2)}) copy-start(s32[8]{0:T(128)} %select_reduce_fusion._.source_ref) | copy-start | bytes 100
  649.2 191.1 %all-gather.7.cloned.1.call-start = ((), (), s32[]{:S(2)}) async-start(), calls=%async_computation.4 | async-start | bytes 9732096 | tf_op jit(solution)/shard_map/all_gather | solution.py:2094
  671.8 11.4 %copy-start.38 = (f32[2,3,16,128]{3,2,1,0:T(8,128)S(1)}, f32[2,3,16,128]{3,2,1,0:T(8,128)}, u32[]{:S(2)}) copy-start(f32[2,3,16,128]{3,2,1,0:T(8,128)} %reduce_sum.29) | copy-start | bytes 147460
  671.8 11.4 %copy-start.43 = (f32[2,3,16,128]{3,2,1,0:T(8,128)S(1)}, f32[2,3,16,128]{3,2,1,0:T(8,128)}, u32[]{:S(2)}) copy-start(f32[2,3,16,128]{3,2,1,0:T(8,128)} %get-tuple-element.95) | copy-start | bytes 147460
  671.8 12.2 %copy-start.29 = (f32[2,128,1024]{2,1,0:T(8,128)S(1)}, f32[2,128,1024]{2,1,0:T(8,128)}, u32[]{:S(2)}) copy-start(f32[2,128,1024]{2,1,0:T(8,128)} %get-tuple-element.60.after_ref) | copy-start | bytes 3145732
  686.9 152.4 %collective-permute-start.4 = (f32[2,64,1024]{2,1,0:T(8,128)S(1)}, f32[2,64,1024]{2,1,0:T(8,128)S(1)}, u32[]{:S(2)}, u32[]{:S(2)}) collective-permute-start(f32[2,64,1024]{2,1,0:T(8,128)S(1)} %get-tuple-element.103), channel_id=1, source_target_pairs={{0,2},{2,0},{4,6},{6,4},{1,3},{3,1},{5,7},{7,5},{8,10},{10,8},{12,... | collective-permute-start | bytes 1572872 | tf_op jit(solution)/shard_map/ppermute | solution.py:2087
  688.4 150.8 %collective-permute-start.5 = (f32[2,64,1024]{2,1,0:T(8,128)S(1)}, f32[2,64,1024]{2,1,0:T(8,128)S(1)}, u32[]{:S(2)}, u32[]{:S(2)}) collective-permute-start(f32[2,64,1024]{2,1,0:T(8,128)S(1)} %get-tuple-element.105), channel_id=1, source_target_pairs={{0,4},{2,6},{4,0},{6,2},{1,5},{3,7},{5,1},{7,3},{8,12},{10,14},{12... | collective-permute-start | bytes 1572872 | tf_op jit(solution)/shard_map/ppermute | solution.py:2087
  690.9 148.4 %collective-permute-start.6 = (f32[2,64,1024]{2,1,0:T(8,128)S(1)}, f32[2,64,1024]{2,1,0:T(8,128)S(1)}, u32[]{:S(2)}, u32[]{:S(2)}) collective-permute-start(f32[2,64,1024]{2,1,0:T(8,128)S(1)} %get-tuple-element.104), channel_id=1, source_target_pairs={{0,6},{2,4},{4,2},{6,0},{1,7},{3,5},{5,3},{7,1},{8,14},{10,12},{12... | collective-permute-start | bytes 1572872 | tf_op jit(solution)/shard_map/ppermute | solution.py:2087
  (35 other events, 133.3 us)
Sparse Core Ops, SparseCore 0:
  232.7 129.7 all-gather.4
  512.9 101.5 all-gather.8
  684.1 138.8 all-gather.6
